TPU v7x, 32 devices: a whole 2x2x4 slice. The times are simulated.
32 devices in a mesh: seq: 16 (over z, y, x), head: 2 (over core).
Axes of the slice: x: 2, y: 2, z: 4, core: 2. Of those that a mesh axis runs over, the one named last changes fastest.
Arguments:
- hidden_in: bfloat16 [8192, 2048], P('seq'), may hold values from -6 to 6
- cotangent: bfloat16 [8192, 2048], P('seq'), may hold values from -6 to 6
- lengths: int32 [3], replicated, may hold values from 1 to 62, as said below
- dealing: int32 [3], replicated, may hold values from 0 to 2, as said below
- norm_attn: float32 [2048], replicated, may hold values from 0.5 to 1.5
- w_query: bfloat16 [2048, 1024], P('seq', 'head'), may hold values from -0.125 to 0.125
- w_key: bfloat16 [2048, 1024], P('seq', 'head'), may hold values from -0.125 to 0.125
- w_value: bfloat16 [2048, 2048], P('seq', 'head'), may hold values from -0.125 to 0.125
- w_rank_in: bfloat16 [2048, 16], replicated, may hold values from -0.125 to 0.125
- w_rank_out: bfloat16 [16, 1024], P(None, 'head'), may hold values from -1.5 to 1.5
- decay_bias: float32 [1024], P('head'), may hold values from -1 to 10
- w_gate_out: bfloat16 [2048, 2048], P('seq', 'head'), may hold values from -0.125 to 0.125
- head_gain: float32 [512], replicated, may hold values from 0.5 to 1.5
- w_out: bfloat16 [2048, 2048], P('head', 'seq'), may hold values from -0.125 to 0.125
- norm_mlp: float32 [2048], replicated, may hold values from 0.5 to 1.5
- w_ff_gate: bfloat16 [2048, 5632], P('seq', 'head'), may hold values from -0.125 to 0.125
- w_ff_up: bfloat16 [2048, 5632], P('seq', 'head'), may hold values from -0.125 to 0.125
- w_ff_down: bfloat16 [5632, 2048], P('head', 'seq'), may hold values from -0.078125 to 0.078125
Outputs:
- block_out: bfloat16 [8192, 2048], P('seq')
- grad_input: float32 [8192, 2048], P('seq')
- grad_norm_attn: float32 [2048], replicated
- grad_query: float32 [2048, 1024], P('seq', 'head')
- grad_key: float32 [2048, 1024], P('seq', 'head')
- grad_value: float32 [2048, 2048], P('seq', 'head')
- grad_rank_in: float32 [2048, 16], replicated
- grad_rank_out: float32 [16, 1024], P(None, 'head')
- grad_decay_bias: float32 [1024], P('head')
- grad_gate_out: float32 [2048, 2048], P('seq', 'head')
- grad_head_gain: float32 [512], replicated
- grad_out_proj: float32 [2048, 2048], P('head', 'seq')
- grad_norm_mlp: float32 [2048], replicated
- grad_ff_gate: float32 [2048, 5632], P('seq', 'head')
- grad_ff_up: float32 [2048, 5632], P('seq', 'head')
- grad_ff_down: float32 [5632, 2048], P('head', 'seq')
Inputs may be any that keep to these rules, and one draw needn't show every extreme that they name: lengths sum to 64; in packed order the first and the last sequence each have fewer than 4 blocks, so the middle one runs from the first device of seq to the last. `dealing`: a permutation of the sequence numbers.
All inputs are finite; a program needn't handle non-finite values.
Results may differ from a plain program's by a relative error of at most 0.0095.
The roundings to bfloat16 on the way count: a program that leaves them out, or rounds other values in their place, can miss the bound.
Values may be sent and summed in bfloat16 or wider, within the bound.
No kernel may reach another device: no remote copies, remote signals or barrier semaphores. Data moves between devices by JAX's collectives and lax.ppermute only.
A program may use at most 256 MiB of HBM per device.

v0:
```python
import jax
import jax.numpy as jnp
from jax import lax
from jax.sharding import PartitionSpec as P

DK = 256
DV = 512
SPAN = 64
BLOCK = 128


EPSILON = 1e-06
HIGH_PRECISION = lax.Precision.HIGHEST


def carried_in(x, axis, combine, identity, reverse):
    peers, position = (lax.axis_size(axis), lax.axis_index(axis))
    everything = jax.tree.map(lambda part: lax.all_gather(part, axis), x)
    start = jax.tree.map(
        lambda part, zero: jnp.broadcast_to(jnp.asarray(zero, part.dtype), part.shape), x, identity
    )

    def lap(k, before):
        at = peers - 1 - k if reverse else k
        reached = at > position if reverse else at < position
        new = combine(before, jax.tree.map(lambda part: part[at], everything))
        return jax.tree.map(lambda a, b: jnp.where(reached, a, b), new, before)

    return lax.fori_loop(0, peers, lap, start)


def rms_scale(value_columns, gain):
    return (
        value_columns
        * lax.rsqrt(jnp.mean(value_columns * value_columns, axis=-1, keepdims=True) + EPSILON)
        * gain
    )


def matmul(left, right):
    return jnp.dot(left, right, preferred_element_type=jnp.float32)


def matmul_tn(left, right):
    return lax.dot_general(
        left, right, (((0,), (0,)), ((), ())), preferred_element_type=jnp.float32
    )


def matmul_nt(left, right):
    return lax.dot_general(
        left, right, (((1,), (1,)), ((), ())), preferred_element_type=jnp.float32
    )


def precise_tn(left, right):
    return lax.dot_general(left, right, (((0,), (0,)), ((), ())), precision=HIGH_PRECISION)


def precise_nt(left, right):
    return lax.dot_general(left, right, (((1,), (1,)), ((), ())), precision=HIGH_PRECISION)


def span_resets(lengths, dealing, count, start_span):
    number = lengths.shape[0]
    picks = (dealing[:, None] == jnp.arange(number, dtype=jnp.int32)[None, :]).astype(jnp.int32)
    placed = jnp.sum(picks * lengths[None, :], axis=1, dtype=jnp.int32)
    ends = jnp.cumsum(placed, dtype=jnp.int32) * BLOCK
    starts = ends - placed * BLOCK
    firsts = (start_span + jnp.arange(count, dtype=jnp.int32)) * SPAN
    return jnp.any(firsts[:, None] == starts[None, :], axis=1).astype(jnp.float32)


def span_step(running_state, block):
    scaled, keys, value_columns, decay, reset = block
    running_state = running_state * (1.0 - reset)
    running = jnp.cumsum(decay, axis=0)
    query_decayed = scaled * jnp.exp(running)
    key_dec = keys * jnp.exp(-running)
    cross_block_term = jnp.einsum(
        "xzt,ztw->xzw", query_decayed, running_state, precision=HIGH_PRECISION
    )
    scores = jnp.einsum("thk,shk->hts", query_decayed, key_dec, precision=HIGH_PRECISION)
    length = scaled.shape[0]
    lower = jnp.arange(length)[:, None] >= jnp.arange(length)[None, :]
    scores = jnp.where(lower[None], scores, 0.0)
    within = jnp.einsum("hts,shv->thv", scores, value_columns, precision=HIGH_PRECISION)
    closing_state = running[-1]
    key_tail_decay = keys * jnp.exp(closing_state[None] - running)
    running_state = jnp.exp(closing_state)[:, :, None] * running_state + jnp.einsum(
        "jur,juo->uro", key_tail_decay, value_columns, precision=HIGH_PRECISION
    )
    return (running_state, cross_block_term + within)


def gla_run(scaled, keys, value_columns, decay, resets, running_state):
    running_state, outputs = lax.scan(
        jax.checkpoint(span_step), running_state, (scaled, keys, value_columns, decay, resets)
    )
    return (outputs, running_state)


def chain(earlier, later):
    return (earlier[0] * later[0], later[0][..., None] * earlier[1] + later[1])


def shards(
    hidden_in,
    cotangent,
    lengths,
    dealing,
    norm_attn,
    w_query,
    w_key,
    w_value,
    w_rank_in,
    w_rank_out,
    decay_bias,
    w_gate_out,
    head_gain,
    w_out,
    norm_mlp,
    w_ff_gate,
    w_ff_up,
    w_ff_down,
):
    rows = hidden_in.shape[0]
    heads_here = decay_bias.shape[0] // DK
    count = rows // SPAN
    scale = DK ** (-0.5)
    resets = span_resets(lengths, dealing, count, lax.axis_index("seq") * count)
    (
        full_query,
        full_key,
        full_value,
        full_gate,
        full_ff_gate,
        full_ff_up,
        full_out,
        full_ff_down,
    ) = (
        lax.all_gather(w_query, "seq", axis=0, tiled=True),
        lax.all_gather(w_key, "seq", axis=0, tiled=True),
        lax.all_gather(w_value, "seq", axis=0, tiled=True),
        lax.all_gather(w_gate_out, "seq", axis=0, tiled=True),
        lax.all_gather(w_ff_gate, "seq", axis=0, tiled=True),
        lax.all_gather(w_ff_up, "seq", axis=0, tiled=True),
        lax.all_gather(w_out, "seq", axis=1, tiled=True),
        lax.all_gather(w_ff_down, "seq", axis=1, tiled=True),
    )
    hidden = hidden_in.astype(jnp.float32)
    normed_attn, attn_norm_pull = jax.vjp(rms_scale, hidden, norm_attn)
    first_in = normed_attn.astype(jnp.bfloat16)
    queries = matmul(first_in, full_query)
    keys = matmul(first_in, full_key)
    value_columns = matmul(first_in, full_value)
    gate_pre = matmul(first_in, full_gate)
    rank_in = matmul(first_in, w_rank_in).astype(jnp.bfloat16)
    logits = matmul(rank_in, w_rank_out) + decay_bias
    log_decay = jax.nn.log_sigmoid(logits) / 16.0
    shape_key = (count, SPAN, heads_here, DK)
    shape_val = (count, SPAN, heads_here, DV)
    scaled = (queries * scale).reshape(shape_key)
    key_blocks = keys.reshape(shape_key)
    val_blocks = value_columns.reshape(shape_val)
    decay_blocks = log_decay.reshape(shape_key)
    zero_state = jnp.zeros((heads_here, DK, DV), jnp.float32)
    within_block_output, local_state = gla_run(
        scaled, key_blocks, val_blocks, decay_blocks, resets, zero_state
    )
    survive = jnp.cumprod(1.0 - resets)
    carried = jnp.exp(jnp.cumsum(log_decay.reshape(rows, heads_here, DK), axis=0)).reshape(
        shape_key
    )
    carried = carried * survive[:, None, None, None]
    through = carried[-1, -1]
    identity = (jnp.ones_like(through), jnp.zeros_like(local_state))
    incoming_state = carried_in((through, local_state), "seq", chain, identity, False)[1]
    decay_reach = scaled * carried
    mixed_output = within_block_output + jnp.einsum(
        "slqa,qai->slqi", decay_reach, incoming_state, precision=HIGH_PRECISION
    )

    def head_gate(mixed_rows, gate_rows, gain):
        normed = rms_scale(mixed_rows, gain).reshape(rows, heads_here * DV)
        return normed * jax.nn.silu(gate_rows)

    gated_full, gate_pull = jax.vjp(
        head_gate, mixed_output.reshape(rows, heads_here, DV), gate_pre, head_gain
    )
    gated = gated_full.astype(jnp.bfloat16)
    attention = lax.psum(matmul(gated, full_out), "head")
    resid = hidden + attention
    normed_mlp, mlp_norm_pull = jax.vjp(rms_scale, resid, norm_mlp)
    second_in = normed_mlp.astype(jnp.bfloat16)
    ff_pre = matmul(second_in, full_ff_gate)
    up_pre = matmul(second_in, full_ff_up)

    def swiglu(gate_rows, up_rows):
        return jax.nn.silu(gate_rows) * up_rows

    inner_full, glu_pull = jax.vjp(swiglu, ff_pre, up_pre)
    inner = inner_full.astype(jnp.bfloat16)
    branch = lax.psum(matmul(inner, full_ff_down), "head")
    block_out = (resid + branch).astype(jnp.bfloat16)
    fresh, anchor = lax.optimization_barrier(
        ((w_query, w_key, w_value, w_gate_out, w_ff_gate, w_ff_up, w_out, w_ff_down), block_out)
    )
    (
        full_query,
        full_key,
        full_value,
        full_gate,
        full_ff_gate,
        full_ff_up,
        full_out,
        full_ff_down,
    ) = (
        lax.all_gather(fresh[0], "seq", axis=0, tiled=True),
        lax.all_gather(fresh[1], "seq", axis=0, tiled=True),
        lax.all_gather(fresh[2], "seq", axis=0, tiled=True),
        lax.all_gather(fresh[3], "seq", axis=0, tiled=True),
        lax.all_gather(fresh[4], "seq", axis=0, tiled=True),
        lax.all_gather(fresh[5], "seq", axis=0, tiled=True),
        lax.all_gather(fresh[6], "seq", axis=1, tiled=True),
        lax.all_gather(fresh[7], "seq", axis=1, tiled=True),
    )
    grad_top = cotangent.astype(jnp.float32)
    grad_inner = matmul_nt(cotangent, full_ff_down)
    grad_w_ff_down = matmul_tn(inner, cotangent)
    grad_ff_full, grad_up_full = glu_pull(grad_inner)
    ff_back = grad_ff_full.astype(jnp.bfloat16)
    up_back = grad_up_full.astype(jnp.bfloat16)
    grad_w_ff_gate = matmul_tn(second_in, ff_back)
    grad_w_ff_up = matmul_tn(second_in, up_back)
    second_part = matmul_nt(ff_back, full_ff_gate) + matmul_nt(up_back, full_ff_up)
    grad_second = lax.psum(second_part, "head")
    grad_resid_norm, grad_norm_mlp_local = mlp_norm_pull(grad_second)
    grad_resid = grad_top + grad_resid_norm
    resid_back = grad_resid.astype(jnp.bfloat16)
    grad_w_out = matmul_tn(gated, resid_back)
    grad_gated = matmul_nt(resid_back, full_out)
    grad_mixed, grad_gate_full, grad_head_gain_local = gate_pull(grad_gated)
    gate_back = grad_gate_full.astype(jnp.bfloat16)
    block_gradients = grad_mixed.reshape(shape_val)
    self_block_term = jnp.einsum(
        "qlyb,qlyi->ybi", decay_reach, block_gradients, precision=HIGH_PRECISION
    )
    leaving = carried_in((through, self_block_term), "seq", chain, identity, True)[1]

    def local_chain(scaled_rows, key_rows, val_rows, decay_rows, state_in):
        return gla_run(scaled_rows, key_rows, val_rows, decay_rows, resets, state_in)

    ignored, chain_pull = jax.vjp(
        local_chain, scaled, key_blocks, val_blocks, decay_blocks, incoming_state
    )
    grad_scaled, grad_keys, grad_vals, grad_decay, grad_entering = chain_pull(
        (block_gradients, leaving)
    )
    query_back = (grad_scaled.reshape(rows, heads_here * DK) * scale).astype(jnp.bfloat16)
    key_back = grad_keys.reshape(rows, heads_here * DK).astype(jnp.bfloat16)
    value_back = grad_vals.reshape(rows, heads_here * DV).astype(jnp.bfloat16)
    grad_logits = grad_decay.reshape(rows, heads_here * DK) * jax.nn.sigmoid(-logits) / 16.0
    grad_bias_local = jnp.sum(grad_logits, axis=0)
    grad_rank_out_local = precise_tn(rank_in.astype(jnp.float32), grad_logits)
    grad_rank = precise_nt(grad_logits, w_rank_out.astype(jnp.float32))
    grad_rank_in_part = precise_tn(first_in.astype(jnp.float32), grad_rank)
    grad_w_query = matmul_tn(first_in, query_back)
    grad_w_key = matmul_tn(first_in, key_back)
    grad_w_value = matmul_tn(first_in, value_back)
    grad_w_gate = matmul_tn(first_in, gate_back)
    first_part = (
        matmul_nt(query_back, full_query)
        + matmul_nt(key_back, full_key)
        + matmul_nt(value_back, full_value)
        + matmul_nt(gate_back, full_gate)
        + precise_nt(grad_rank, w_rank_in.astype(jnp.float32))
    )
    grad_first, grad_rank_in_heads, grad_head_gain_heads = lax.psum(
        (first_part, grad_rank_in_part, grad_head_gain_local), "head"
    )
    grad_hidden_norm, grad_norm_attn_local = attn_norm_pull(grad_first)
    grad_input = grad_resid + grad_hidden_norm
    (
        grad_query,
        grad_key,
        grad_value,
        grad_gate_out,
        grad_ff_gate,
        grad_ff_up,
        grad_out_proj,
        grad_ff_down,
    ) = (
        lax.psum_scatter(grad_w_query, "seq", scatter_dimension=0, tiled=True),
        lax.psum_scatter(grad_w_key, "seq", scatter_dimension=0, tiled=True),
        lax.psum_scatter(grad_w_value, "seq", scatter_dimension=0, tiled=True),
        lax.psum_scatter(grad_w_gate, "seq", scatter_dimension=0, tiled=True),
        lax.psum_scatter(grad_w_ff_gate, "seq", scatter_dimension=0, tiled=True),
        lax.psum_scatter(grad_w_ff_up, "seq", scatter_dimension=0, tiled=True),
        lax.psum_scatter(grad_w_out, "seq", scatter_dimension=1, tiled=True),
        lax.psum_scatter(grad_w_ff_down, "seq", scatter_dimension=1, tiled=True),
    )
    grad_norm_attn, grad_norm_mlp, grad_rank_in, grad_rank_out, grad_decay_bias, grad_head_gain = (
        lax.psum(
            (
                grad_norm_attn_local,
                grad_norm_mlp_local,
                grad_rank_in_heads,
                grad_rank_out_local,
                grad_bias_local,
                grad_head_gain_heads,
            ),
            "seq",
        )
    )
    return (
        block_out,
        grad_input,
        grad_norm_attn,
        grad_query,
        grad_key,
        grad_value,
        grad_rank_in,
        grad_rank_out,
        grad_decay_bias,
        grad_gate_out,
        grad_head_gain,
        grad_out_proj,
        grad_norm_mlp,
        grad_ff_gate,
        grad_ff_up,
        grad_ff_down,
    )


def solution(mesh):
    return jax.shard_map(
        shards,
        mesh=mesh,
        in_specs=(
            P("seq", None),
            P("seq", None),
            P(),
            P(),
            P(),
            P("seq", "head"),
            P("seq", "head"),
            P("seq", "head"),
            P(),
            P(None, "head"),
            P("head"),
            P("seq", "head"),
            P(),
            P("head", "seq"),
            P(),
            P("seq", "head"),
            P("seq", "head"),
            P("head", "seq"),
        ),
        out_specs=(
            P("seq", None),
            P("seq", None),
            P(),
            P("seq", "head"),
            P("seq", "head"),
            P("seq", "head"),
            P(),
            P(None, "head"),
            P("head"),
            P("seq", "head"),
            P(),
            P("head", "seq"),
            P(),
            P("seq", "head"),
            P("seq", "head"),
            P("head", "seq"),
        ),
        check_vma=False,
    )
```

profile of v0, /device:TPU:0, one launch (start us, length us, event | category | flops | bytes accessed | tf_op | source)
XLA Modules:
  0.0 4627.7 jit_solution(6350682990353197680)
XLA Ops:
  22.6 51.7 %all-gather.22.cloned.1.call-done = bf16[2048,512]{1,0:T(8,128)(2,1)} async-done(((bf16[128,512]{1,0:T(8,128)(2,1)}), bf16[2048,512]{1,0:T(8,128)(2,1)}) %all-gather.22.cloned.1.call-update) | async-done | bytes 2097168 | tf_op jit(solution)/shard_map/all_gather | solution.py:143
  81.0 55.4 %all-gather.26.cloned.1.call-done = bf16[2048,512]{1,0:T(8,128)(2,1)} async-done(((bf16[128,512]{1,0:T(8,128)(2,1)}), bf16[2048,512]{1,0:T(8,128)(2,1)}) %all-gather.26.cloned.1.call-update) | async-done | bytes 2097168 | tf_op jit(solution)/shard_map/all_gather | solution.py:142
  136.4 3.9 convolution_multiply_fusion
  145.7 68.2 %all-gather.24.cloned.1.call-done = bf16[2048,1024]{1,0:T(8,128)(2,1)} async-done(((bf16[128,1024]{1,0:T(8,128)(2,1)}), bf16[2048,1024]{1,0:T(8,128)(2,1)}) %all-gather.24.cloned.1.call-update) | async-done | bytes 4194320 | tf_op jit(solution)/shard_map/all_gather | solution.py:144
  214.0 5.9 fusion.102
  219.8 4.2 reshape.314
  226.0 67.4 %while.79 = (s32[]{:T(128)}, f32[2,256,512]{2,1,0:T(8,128)S(1)}, f32[8,64,2,512]{3,1,0,2:T(8,128)}, f32[8,64,2,256]{3,2,1,0:T(2,128)}, f32[8]{0:T(128)S(1)}, /*i...) while((s32[]{:T(128)}, f32[2,256,512]{2,1,0:T(8,128)S(1)}, ...), condition=%wide.region_6.7_spmd.clone, body=%wide.region_4.6_spmd.clone.sunk | while | flops 482029568 | bytes 6149792 | solution.py:97
  302.8 39.5 all-gather
  342.4 142.7 %all-gather.54.cloned.1.call-done = f32[32,256,512]{2,1,0:T(8,128)} async-done(((f32[2,256,512]{2,1,0:T(8,128)}), f32[32,256,512]{2,1,0:T(8,128)}) %all-gather.54.cloned.1.call-update) | async-done | bytes 16777232 | tf_op jit(solution)/shard_map/all_gather | solution.py:18
  485.1 24.8 while.80
  518.2 43.8 all-gather.28.cloned.1.call-done
  562.0 8.9 multiply_convert_fusion.2
  570.9 81.5 %all-gather.30.cloned.1.call-done = bf16[1024,2048]{1,0:T(8,128)(2,1)} async-done(((bf16[1024,128]{1,0:T(8,128)(2,1)}), bf16[1024,2048]{1,0:T(8,128)(2,1)}) %all-gather.30.cloned.1.call-update) | async-done | bytes 4194320 | tf_op jit(solution)/shard_map/all_gather | solution.py:148
  652.4 6.5 fusion.111
  661.1 24.7 all-reduce.9.cloned.1.call-done
  693.0 139.2 %all-gather.32.cloned.1.call-done = bf16[2048,2816]{1,0:T(8,128)(2,1)} async-done(((bf16[128,2816]{1,0:T(8,128)(2,1)}), bf16[2048,2816]{1,0:T(8,128)(2,1)}) %all-gather.32.cloned.1.call-update) | async-done | bytes 11534352 | tf_op jit(solution)/shard_map/all_gather | solution.py:146
  832.2 12.9 fusion.112
  845.2 130.6 %all-gather.34.cloned.1.call-done = bf16[2048,2816]{1,0:T(8,128)(2,1)} async-done(((bf16[128,2816]{1,0:T(8,128)(2,1)}), bf16[2048,2816]{1,0:T(8,128)(2,1)}) %all-gather.34.cloned.1.call-update) | async-done | bytes 11534352 | tf_op jit(solution)/shard_map/all_gather | solution.py:147
  975.8 14.0 multiply_convert_fusion
  989.7 169.7 %all-gather.36.cloned.1.call-done = bf16[2816,2048]{1,0:T(8,128)(2,1)} async-done(((bf16[2816,128]{1,0:T(8,128)(2,1)}), bf16[2816,2048]{1,0:T(8,128)(2,1)}) %all-gather.36.cloned.1.call-update) | async-done | bytes 11534352 | tf_op jit(solution)/shard_map/all_gather | solution.py:149
  1159.4 11.2 fusion.113
  1170.7 26.7 all-reduce.11.cloned.1.call-done
  1197.4 5.4 add_convert_fusion
  1204.3 182.5 %all-gather.38.cloned.1.call-done = bf16[2816,2048]{1,0:T(8,128)(2,1)} async-done(((bf16[2816,128]{1,0:T(8,128)(2,1)}), bf16[2816,2048]{1,0:T(8,128)(2,1)}) %all-gather.38.cloned.1.call-update) | async-done | bytes 11534352 | tf_op jit(solution)/shard_map/all_gather | solution.py:226
  1386.8 17.0 fusion.62
  1403.8 126.1 %all-gather.40.cloned.1.call-done = bf16[2048,2816]{1,0:T(8,128)(2,1)} async-done(((bf16[128,2816]{1,0:T(8,128)(2,1)}), bf16[2048,2816]{1,0:T(8,128)(2,1)}) %all-gather.40.cloned.1.call-update) | async-done | bytes 11534352 | tf_op jit(solution)/shard_map/all_gather | solution.py:223
  1529.9 11.2 fusion.114
  1541.1 131.8 %all-gather.42.cloned.1.call-done = bf16[2048,2816]{1,0:T(8,128)(2,1)} async-done(((bf16[128,2816]{1,0:T(8,128)(2,1)}), bf16[2048,2816]{1,0:T(8,128)(2,1)}) %all-gather.42.cloned.1.call-update) | async-done | bytes 11534352 | tf_op jit(solution)/shard_map/all_gather | solution.py:224
  1672.9 11.8 convolution_add_fusion.6
  1686.2 25.3 all-reduce.13.cloned.1.call-done
  1711.5 5.2 multiply_reduce_fusion.1
  1717.4 4.7 fusion.68
  1722.1 82.7 %all-gather.44.cloned.1.call-done = bf16[1024,2048]{1,0:T(8,128)(2,1)} async-done(((bf16[1024,128]{1,0:T(8,128)(2,1)}), bf16[1024,2048]{1,0:T(8,128)(2,1)}) %all-gather.44.cloned.1.call-update) | async-done | bytes 4194320 | tf_op jit(solution)/shard_map/all_gather | solution.py:225
  1804.8 10.0 multiply_reduce_fusion.4
  1814.8 4.1 reshape.322
  1827.9 51.7 %while.77 = (s32[]{:T(128)}, f32[2,256,512]{2,1,0:T(8,128)S(1)}, f32[8,2,256,512]{3,2,1,0:T(8,128)}, f32[8,64,2,256]{3,2,1,0:T(2,128)}, f32[8]{0:T(128)S(1)}, /*...) while((s32[]{:T(128)}, f32[2,256,512]{2,1,0:T(8,128)S(1)}, ...), condition=%wide.region_23.24_spmd, body=%wide.region_21.23_spmd.sunk | while | flops 204242944 | bytes 5257337 | solution.py:97
  1883.4 6.5 fusion.118
  1889.9 185.6 %all-gather.56.cloned.1.call-done = f32[32,256,512]{2,1,0:T(8,128)} async-done(((f32[2,256,512]{2,1,0:T(8,128)}), f32[32,256,512]{2,1,0:T(8,128)}) %all-gather.56.cloned.1.call-update) | async-done | bytes 16777232 | tf_op jit(solution)/shard_map/all_gather | solution.py:18
  2075.4 35.1 while.81
  2114.1 122.7 %while.78 = (s32[]{:T(128)}, f32[2,256,512]{2,1,0:T(8,128)S(1)}, f32[8,64,2,256]{3,1,2,0:T(8,128)}, bf16[8,64,2,256]{3,1,2,0:T(8,128)(2,1)}, bf16[8,64,2,512]{3,...) while((s32[]{:T(128)}, f32[2,256,512]{2,1,0:T(8,128)S(1)}, ...), condition=%wide.region_29.30_spmd, body=%wide.region_24.29_spmd.sunk | while | flops 988598272 | bytes 18858212 | solution.py:97
  2250.2 5.0 fusion.116
  2255.3 5.1 fusion.115
  2260.4 17.6 all-gather.50.cloned.1.call-done
  2277.9 5.0 fusion.117
  2284.2 4.9 add_add_fusion.2
  2289.1 14.3 fusion.123
  2303.5 8.4 fusion.80
  2312.0 7.3 fusion.89
  2320.0 4.4 fusion.97
  2324.5 4.4 fusion.95
  2329.0 13.3 fusion.121
  2342.4 13.1 fusion.122
  2355.6 7.1 fusion.93
  2369.9 83.4 %all-reduce.1 = (f32[2048]{0:T(1024)}, f32[16,512]{1,0:T(8,128)}, f32[512]{0:T(512)}, f32[512]{0:T(512)}, f32[2048]{0:T(1024)}) all-reduce(f32[2048]{0:T(1024)S(1)} %get-tuple-element.818, f32[16,512]{1,0:T(8,128)S(1)} %fusion.120, f32[512]{0:T(512)S(1)} %get-tuple-element.905, ...), channel_id=1, replica_groups=mesh['seq'=16,'head'=2] {'seq'}, use_global_device_ids=true, to_apply=%region_33.34 | all-reduce | flops 13312 | bytes 106496 | tf_op jit(solution)/shard_map/psum | solution.py:304
  2453.4 6.5 fusion.69
  2459.9 336.3 %reduce-scatter.23.cloned.1.call-done = f32[2816,128]{1,0:T(8,128)} async-done(((f32[2816,2048]{1,0:T(8,128)}), f32[2816,128]{1,0:T(8,128)}) %reduce-scatter.23.cloned.1.call-update) | async-done | bytes 1441808 | tf_op jit(solution)/shard_map/reduce_scatter | solution.py:301
  2796.2 187.4 %reduce-scatter.17.cloned.1.call-done = f32[1024,128]{1,0:T(8,128)} async-done(((f32[1024,2048]{1,0:T(8,128)}), f32[1024,128]{1,0:T(8,128)}) %reduce-scatter.17.cloned.1.call-update) | async-done | bytes 524304 | tf_op jit(solution)/shard_map/reduce_scatter | solution.py:300
  2983.6 183.1 %reduce-scatter.15.cloned.1.call-done = f32[128,1024]{1,0:T(8,128)} async-done(((f32[2048,1024]{1,0:T(8,128)}), f32[128,1024]{1,0:T(8,128)}) %reduce-scatter.15.cloned.1.call-update) | async-done | bytes 524304 | tf_op jit(solution)/shard_map/reduce_scatter | solution.py:297
  3166.8 111.9 %all-reduce.15.cloned.1.call-done = f32[2048,16]{0,1:T(8,128)} async-done(((f32[2048,16]{0,1:T(8,128)}), f32[2048,16]{0,1:T(8,128)}) %all-reduce.15.cloned.1.call-update) | async-done | bytes 131088 | tf_op jit(solution)/shard_map/psum | solution.py:304
  3278.7 96.9 %reduce-scatter.9.cloned.1.call-done = f32[128,512]{1,0:T(8,128)} async-done(((f32[2048,512]{1,0:T(8,128)}), f32[128,512]{1,0:T(8,128)}) %reduce-scatter.9.cloned.1.call-update) | async-done | bytes 262160 | tf_op jit(solution)/shard_map/reduce_scatter | solution.py:294
  3375.6 97.6 %reduce-scatter.11.cloned.1.call-done = f32[128,512]{1,0:T(8,128)} async-done(((f32[2048,512]{1,0:T(8,128)}), f32[128,512]{1,0:T(8,128)}) %reduce-scatter.11.cloned.1.call-update) | async-done | bytes 262160 | tf_op jit(solution)/shard_map/reduce_scatter | solution.py:295
  3473.2 475.5 %reduce-scatter.19.cloned.1.call-done = f32[128,2816]{1,0:T(8,128)} async-done(((f32[2048,2816]{1,0:T(8,128)}), f32[128,2816]{1,0:T(8,128)}) %reduce-scatter.19.cloned.1.call-update) | async-done | bytes 1441808 | tf_op jit(solution)/shard_map/reduce_scatter | solution.py:298
  3948.7 482.6 %reduce-scatter.21.cloned.1.call-done = f32[128,2816]{1,0:T(8,128)} async-done(((f32[2048,2816]{1,0:T(8,128)}), f32[128,2816]{1,0:T(8,128)}) %reduce-scatter.21.cloned.1.call-update) | async-done | bytes 1441808 | tf_op jit(solution)/shard_map/reduce_scatter | solution.py:299
  4431.3 187.5 %reduce-scatter.13.cloned.1.call-done = f32[128,1024]{1,0:T(8,128)} async-done(((f32[2048,1024]{1,0:T(8,128)}), f32[128,1024]{1,0:T(8,128)}) %reduce-scatter.13.cloned.1.call-update) | async-done | bytes 524304 | tf_op jit(solution)/shard_map/reduce_scatter | solution.py:296
  (633 shorter events, 383.4 us)
Async XLA Ops:
  7.2 5.0 copy-start
  7.2 7.3 copy-start.33
  7.2 7.3 copy-start.38
  7.2 67.0 %all-gather.22.cloned.1.call-start = ((), (), s32[]{:S(2)}) async-start(), calls=%async_computation.8 | async-start | bytes 2228224 | tf_op jit(solution)/shard_map/all_gather | solution.py:143
  8.0 128.5 %all-gather.26.cloned.1.call-start = ((), (), s32[]{:S(2)}) async-start(), calls=%async_computation.10 | async-start | bytes 2228224 | tf_op jit(solution)/shard_map/all_gather | solution.py:142
  8.7 205.3 %all-gather.24.cloned.1.call-start = ((), (), s32[]{:S(2)}) async-start(), calls=%async_computation.9 | async-start | bytes 4456448 | tf_op jit(solution)/shard_map/all_gather | solution.py:144
  9.4 475.7 %all-gather.54.cloned.1.call-start = ((), (), s32[]{:S(2)}) async-start(), calls=%async_computation.36 | async-start | bytes 17825792 | tf_op jit(solution)/shard_map/all_gather | solution.py:18
  12.2 549.8 %copy-start.31 = (f32[512]{0:T(512)}, f32[512]{0:T(512)S(1)}, u32[]{:S(2)}) copy-start(f32[512]{0:T(512)S(1)} %fusion.86) | copy-start | bytes 6148
  14.5 63.6 %copy-start.35 = (bf16[512,16]{0,1:T(8,128)(2,1)}, bf16[512,16]{0,1:T(8,128)(2,1)S(1)}, u32[]{:S(2)}) copy-start(bf16[512,16]{0,1:T(8,128)(2,1)S(1)} %convolution_convert_fusion) | copy-start | bytes 49156
  14.5 7.6 copy-start.39
  14.5 7.6 copy-start.40
  14.5 59.7 %copy-start.6 = (bf16[512,2048]{1,0:T(8,128)(2,1)S(1)}, bf16[512,2048]{1,0:T(8,128)(2,1)}, u32[]{:S(2)}) copy-start(bf16[512,2048]{1,0:T(8,128)(2,1)} %param.28) | copy-start | bytes 6291460
  14.6 59.7 %copy-start.24 = (f32[2048]{0:T(1024)S(1)}, f32[2048]{0:T(1024)}, u32[]{:S(2)}) copy-start(f32[2048]{0:T(1024)} %param.32) | copy-start | bytes 24580
  22.6 58.4 %copy-start.43 = (pred[8]{0:T(512)(128)(4,1)}, pred[8]{0:T(512)(128)(4,1)S(1)}, u32[]{:S(2)}) copy-start(pred[8]{0:T(512)(128)(4,1)S(1)} %compare_reduce_fusion) | copy-start | bytes 28
  293.4 8.0 copy-start.41
  294.4 267.6 %all-gather.28.cloned.1.call-start = ((), (), s32[]{:S(2)}) async-start(), calls=%async_computation.11 | async-start | bytes 4456448 | tf_op jit(solution)/shard_map/all_gather | solution.py:145
  295.0 357.4 %all-gather.30.cloned.1.call-start = ((), (), s32[]{:S(2)}) async-start(), calls=%async_computation.12 | async-start | bytes 4456448 | tf_op jit(solution)/shard_map/all_gather | solution.py:148
  295.6 390.2 %all-reduce.9.cloned.1.call-start = ((), (), s32[]{:S(2)}) async-start(), calls=%async_computation.13 | async-start | bytes 8388608 | tf_op jit(solution)/shard_map/psum | solution.py:192
  296.3 5.1 copy-start.27
  296.3 5.3 copy-start.16
  302.8 39.5 copy-start.14
  570.9 88.0 %copy-start.21 = (bf16[512,1024]{1,0:T(8,128)(2,1)}, bf16[512,1024]{1,0:T(8,128)(2,1)S(1)}, u32[]{:S(2)}) copy-start(bf16[512,1024]{1,0:T(8,128)(2,1)S(1)} %get-tuple-element.909) | copy-start | bytes 3145732
  659.0 173.3 %all-gather.32.cloned.1.call-start = ((), (), s32[]{:S(2)}) async-start(), calls=%async_computation.14 | async-start | bytes 12255232 | tf_op jit(solution)/shard_map/all_gather | solution.py:146
  659.7 316.0 %all-gather.34.cloned.1.call-start = ((), (), s32[]{:S(2)}) async-start(), calls=%async_computation.15 | async-start | bytes 12255232 | tf_op jit(solution)/shard_map/all_gather | solution.py:147
  660.4 499.0 %all-gather.36.cloned.1.call-start = ((), (), s32[]{:S(2)}) async-start(), calls=%async_computation.16 | async-start | bytes 12255232 | tf_op jit(solution)/shard_map/all_gather | solution.py:149
  661.0 30.2 copy-start.23
  661.0 536.4 %all-reduce.11.cloned.1.call-start = ((), (), s32[]{:S(2)}) async-start(), calls=%async_computation.17 | async-start | bytes 8388608 | tf_op jit(solution)/shard_map/psum | solution.py:204
  1170.7 216.1 %all-gather.38.cloned.1.call-start = ((), (), s32[]{:S(2)}) async-start(), calls=%async_computation.18 | async-start | bytes 12255232 | tf_op jit(solution)/shard_map/all_gather | solution.py:226
  1202.9 327.0 %all-gather.40.cloned.1.call-start = ((), (), s32[]{:S(2)}) async-start(), calls=%async_computation.19 | async-start | bytes 12255232 | tf_op jit(solution)/shard_map/all_gather | solution.py:223
  1203.6 469.3 %all-gather.42.cloned.1.call-start = ((), (), s32[]{:S(2)}) async-start(), calls=%async_computation.20 | async-start | bytes 12255232 | tf_op jit(solution)/shard_map/all_gather | solution.py:224
  1204.2 507.3 %all-reduce.13.cloned.1.call-start = ((), (), s32[]{:S(2)}) async-start(), calls=%async_computation.21 | async-start | bytes 8388608 | tf_op jit(solution)/shard_map/psum | solution.py:237
  1684.7 120.1 %all-gather.44.cloned.1.call-start = ((), (), s32[]{:S(2)}) async-start(), calls=%async_computation.22 | async-start | bytes 4456448 | tf_op jit(solution)/shard_map/all_gather | solution.py:225
  1685.3 198.0 %all-gather.52.cloned.1.call-start = ((), (), s32[]{:S(2)}) async-start(), calls=%async_computation.26 | async-start | bytes 4456448 | tf_op jit(solution)/shard_map/all_gather | solution.py:222
  1685.9 389.5 %all-gather.56.cloned.1.call-start = ((), (), s32[]{:S(2)}) async-start(), calls=%async_computation.37 | async-start | bytes 17825792 | tf_op jit(solution)/shard_map/all_gather | solution.py:18
  1711.5 5.2 copy-start.5
  1711.5 5.9 copy-start.13
  1814.8 4.1 copy-start.28
  1823.1 4.8 copy-start.2
  1823.1 4.8 copy-start.42
  1826.2 424.1 %all-gather.48.cloned.1.call-start = ((), (), s32[]{:S(2)}) async-start(), calls=%async_computation.24 | async-start | bytes 2228224 | tf_op jit(solution)/shard_map/all_gather | solution.py:220
  1826.9 428.3 %all-gather.46.cloned.1.call-start = ((), (), s32[]{:S(2)}) async-start(), calls=%async_computation.23 | async-start | bytes 2228224 | tf_op jit(solution)/shard_map/all_gather | solution.py:219
  1827.9 450.1 %all-gather.50.cloned.1.call-start = ((), (), s32[]{:S(2)}) async-start(), calls=%async_computation.25 | async-start | bytes 4456448 | tf_op jit(solution)/shard_map/all_gather | solution.py:221
  1879.7 3.7 copy-start.44
  1879.7 439.7 %all-reduce.17.cloned.1.call-start = ((), (), s32[]{:S(2)}) async-start(), calls=%async_computation.38 | async-start | bytes 8650752 | tf_op jit(solution)/shard_map/psum | solution.py:279
  2236.8 5.4 copy-start.18
  2239.4 5.2 copy-start.19
  2244.6 3.3 copy-start.34
  2244.6 3.8 copy-start.7
  2244.6 3.8 copy-start.25
  2244.6 3.8 copy-start.32
  2277.9 5.0 copy-start.8
  2277.9 5.0 copy-start.9
  2277.9 6.2 copy-start.17
  2289.1 507.2 %reduce-scatter.23.cloned.1.call-start = ((), (), s32[]{:S(2)}) async-start(), calls=%async_computation.35 | async-start | bytes 24510464 | tf_op jit(solution)/shard_map/reduce_scatter | solution.py:301
  2303.5 680.2 %reduce-scatter.17.cloned.1.call-start = ((), (), s32[]{:S(2)}) async-start(), calls=%async_computation.32 | async-start | bytes 8912896 | tf_op jit(solution)/shard_map/reduce_scatter | solution.py:300
  2312.0 854.8 %reduce-scatter.15.cloned.1.call-start = ((), (), s32[]{:S(2)}) async-start(), calls=%async_computation.31 | async-start | bytes 8912896 | tf_op jit(solution)/shard_map/reduce_scatter | solution.py:297
  2319.4 959.3 %all-reduce.15.cloned.1.call-start = ((), (), s32[]{:S(2)}) async-start(), calls=%async_computation.30 | async-start | bytes 262144 | tf_op jit(solution)/shard_map/psum | solution.py:304
  2320.0 1055.7 %reduce-scatter.9.cloned.1.call-start = ((), (), s32[]{:S(2)}) async-start(), calls=%async_computation.27 | async-start | bytes 4456448 | tf_op jit(solution)/shard_map/reduce_scatter | solution.py:294
  2324.5 1148.7 %reduce-scatter.11.cloned.1.call-start = ((), (), s32[]{:S(2)}) async-start(), calls=%async_computation.28 | async-start | bytes 4456448 | tf_op jit(solution)/shard_map/reduce_scatter | solution.py:295
  2329.0 1619.8 %reduce-scatter.19.cloned.1.call-start = ((), (), s32[]{:S(2)}) async-start(), calls=%async_computation.33 | async-start | bytes 24510464 | tf_op jit(solution)/shard_map/reduce_scatter | solution.py:298
  2342.3 2088.9 %reduce-scatter.21.cloned.1.call-start = ((), (), s32[]{:S(2)}) async-start(), calls=%async_computation.34 | async-start | bytes 24510464 | tf_op jit(solution)/shard_map/reduce_scatter | solution.py:299
  2355.5 2263.3 %reduce-scatter.13.cloned.1.call-start = ((), (), s32[]{:S(2)}) async-start(), calls=%async_computation.29 | async-start | bytes 8912896 | tf_op jit(solution)/shard_map/reduce_scatter | solution.py:296
  2362.7 7.3 copy-start.26
  2362.7 90.7 %copy-start.30 = (f32[512]{0:T(512)S(1)}, f32[512]{0:T(512)}, u32[]{:S(2)}) copy-start(f32[512]{0:T(512)} %copy-done.29) | copy-start | bytes 6148
  (12 other events, 22.1 us)
Sparse Core Ops, SparseCore 0:
  10.8 63.3 all-gather.21
  77.0 59.3 all-gather.25
  139.2 74.7 all-gather.23
  294.5 190.5 all-gather.53
  487.7 74.2 all-gather.27
  564.6 87.7 all-gather.29
  659.1 26.6 all-reduce.8
  688.9 143.3 all-gather.31
  835.4 140.3 all-gather.33
  978.7 180.7 all-gather.35
  1170.8 26.6 all-reduce.10
  1203.0 183.7 all-gather.37
  1389.5 140.3 all-gather.39
  1532.5 140.3 all-gather.41
  1684.9 26.5 all-reduce.12
  1714.4 90.3 all-gather.43
  1807.8 74.3 all-gather.51
  1885.2 190.2 all-gather.55
  2078.6 59.1 all-gather.47
  2140.7 59.1 all-gather.45
  2203.0 74.8 all-gather.49
  2289.2 27.3 all-reduce.16
  2319.4 476.7 reduce-scatter.22
  2798.9 184.6 reduce-scatter.16
  2986.5 180.2 reduce-scatter.14
  3172.1 106.5 all-reduce.14
  3281.4 94.1 reduce-scatter.8
  3378.5 94.6 reduce-scatter.10
  3476.1 472.5 reduce-scatter.18
  3951.4 479.7 reduce-scatter.20
  4434.2 184.6 reduce-scatter.12
where the time goes:
time: 4640 us; the launch traced here: 4630 us
  waiting for transfers between devices  3850 us (83%)
  matrix products  337 us (7%)
  other arithmetic  143 us (3%)
  local copies, waits for them, and re-layouts  132 us (3%)
  blocking collectives  125 us (3%)
    reduce_scatter x1, waiting for transfers between devices, shards(): lax.psum_scatter(grad_w_ff_up, 'seq', scatter_dimension=0, tiled=True)  483 us
    reduce_scatter x1, waiting for transfers between devices, shards(): lax.psum_scatter(grad_w_ff_gate, 'seq', scatter_dimension=0, tiled=True)  476 us
    reduce_scatter x1, waiting for transfers between devices, shards(): lax.psum_scatter(grad_w_ff_down, 'seq', scatter_dimension=1, tiled=True)  336 us
    all_gather x2, waiting for transfers between devices, carried_in(): everything = jax.tree.map(lambda part: lax.all_gather(part, axis), x)  328 us
    reduce_scatter x1, waiting for transfers between devices, shards(): lax.psum_scatter(grad_w_value, 'seq', scatter_dimension=0, tiled=True)  188 us
    reduce_scatter x1, waiting for transfers between devices, shards(): lax.psum_scatter(grad_w_out, 'seq', scatter_dimension=1, tiled=True)  187 us
    reduce_scatter x1, waiting for transfers between devices, shards(): lax.psum_scatter(grad_w_gate, 'seq', scatter_dimension=0, tiled=True)  183 us
    all_gather x1, waiting for transfers between devices, shards(): lax.all_gather(fresh[7], 'seq', axis=1, tiled=True)  183 us
  transfers between devices with their start and end apart: 31, of which 27 were waited for; matrix products, arithmetic and copies ran while one was open for 10% of the time, Pallas kernels for 0%

commit v1 on v0

v1 whole, which is shorter than its diff:
```python
import functools

import jax
import jax.numpy as jnp
from jax import lax
from jax.experimental import pallas as pl
from jax.experimental.pallas import tpu as pltpu
from jax.sharding import PartitionSpec as P

DK = 256
DV = 512
BLOCK = 128
HALF = BLOCK // 2
EPSILON = 1e-06
LOW = jnp.bfloat16
FULL = jnp.float32
LANES = 128

NN = ((1,), (0,))
TN = ((0,), (0,))
NT = ((1,), (1,))


def dot(left, right, dims=NN):
    return lax.dot_general(left, right, (dims, ((), ())), preferred_element_type=FULL)


def halves(x):
    high = x.astype(LOW)
    return high, (x - high.astype(FULL)).astype(LOW)


def thirds(x):
    high, rest = x.astype(LOW), None
    rest = x - high.astype(FULL)
    middle = rest.astype(LOW)
    return high, middle, (rest - middle.astype(FULL)).astype(LOW)


def fine(left, right, dims=NN):
    (lh, ll), (rh, rl) = left, right
    return dot(lh, rh, dims) + (dot(lh, rl, dims) + dot(ll, rh, dims))


def triangle(lower):
    row = lax.broadcasted_iota(jnp.int32, (BLOCK, BLOCK), 0)
    col = lax.broadcasted_iota(jnp.int32, (BLOCK, BLOCK), 1)
    return row >= col if lower else row <= col


def running_sum(x, lower=True):
    ones = triangle(lower).astype(FULL).astype(LOW)
    high, middle, low = thirds(x)
    return dot(ones, high) + (dot(ones, middle) + dot(ones, low))


def column_sum(x):
    ones = jnp.ones((x.shape[0], LANES), LOW)
    high, middle, low = thirds(x)
    return dot(high, ones, TN) + (dot(middle, ones, TN) + dot(low, ones, TN))


def widen(column, width):
    return jnp.concatenate([column] * (width // LANES), axis=1)


def summary_kernel(info, k_ref, v_ref, decay_ref, out_ref, state, passed, total):
    step, count = pl.program_id(0), pl.num_programs(0)
    at = count - 1 - step

    @pl.when(step == 0)
    def _():
        state[...] = jnp.zeros_like(state)
        passed[...] = jnp.zeros_like(passed)
        total[...] = jnp.zeros_like(total)

    decay = decay_ref[...]
    run = running_sum(decay)
    closing = run[BLOCK - 1 :, :]
    alive = info[1 + count + at].astype(FULL)
    tail = jnp.exp(passed[0:1, :] + closing - run) * (k_ref[...] * alive)
    state[...] += fine(halves(tail), halves(v_ref[...]), TN)
    passed[0:1, :] += closing
    total[...] += column_sum(decay)

    @pl.when(step == count - 1)
    def _():
        out_ref[:, :DV] = state[...]
        out_ref[:, DV:] = jnp.exp(total[...]) * info[1 + 3 * count].astype(FULL)


def mix_kernel(
    info, q_ref, k_ref, v_ref, g_ref, decay_ref, enter_ref, gain_ref, mixed_ref, gated_ref, states_ref, state
):
    step = pl.program_id(0)

    @pl.when(step == 0)
    def _():
        state[...] = enter_ref[...]

    begin = jnp.where(info[1 + step] > 0, jnp.zeros_like(state), state[...])
    states_ref[0] = begin
    decay = decay_ref[...]
    run = running_sum(decay)
    middle, closing = run[HALF - 1 : HALF, :], run[BLOCK - 1 :, :]
    q = q_ref[...] * DK ** (-0.5)
    k = k_ref[...]
    v = halves(v_ref[...])
    near_q, near_k = halves(q * jnp.exp(run - middle)), halves(k * jnp.exp(middle - run))
    scores = jnp.where(triangle(True), fine(near_q, near_k, NT), 0.0)
    out = fine(halves(q * jnp.exp(run)), halves(begin)) + fine(halves(scores), v)
    tail = halves(k * jnp.exp(closing - run))
    state[...] = widen(jnp.exp(column_sum(decay)), DV) * begin + fine(tail, v, TN)
    mixed_ref[...] = out
    normed = out * lax.rsqrt(jnp.mean(out * out, axis=1, keepdims=True) + EPSILON) * gain_ref[...]
    gate = g_ref[...]
    gated_ref[...] = (normed * (gate * jax.nn.sigmoid(gate))).astype(LOW)


def gate_back_kernel(
    info, q_ref, g_ref, decay_ref, mixed_ref, grad_ref, gain_ref, back_ref, dmixed_ref, out_ref, dgain_ref, state, passed
):
    step, count = pl.program_id(0), pl.num_programs(0)

    @pl.when(step == 0)
    def _():
        state[...] = jnp.zeros_like(state)
        passed[...] = jnp.zeros_like(passed)
        dgain_ref[...] = jnp.zeros_like(dgain_ref)

    mixed, gate, grad, gain = mixed_ref[...], g_ref[...], grad_ref[...], gain_ref[...]
    scale = lax.rsqrt(jnp.mean(mixed * mixed, axis=1, keepdims=True) + EPSILON)
    normed = mixed * scale
    soft = jax.nn.sigmoid(gate)
    back_ref[...] = (grad * (normed * gain) * (soft * (1.0 + gate * (1.0 - soft)))).astype(LOW)
    error = grad * (gate * soft)
    dgain_ref[...] += jnp.sum(error * normed, axis=0, keepdims=True)
    scaled = error * gain
    dmixed = scale * (scaled - normed * jnp.mean(scaled * normed, axis=1, keepdims=True))
    dmixed_ref[...] = dmixed
    run = running_sum(decay_ref[...])
    alive = info[1 + 2 * count + step].astype(FULL)
    reach = jnp.exp(passed[0:1, :] + run) * (q_ref[...] * (DK ** (-0.5) * alive))
    state[...] += fine(halves(reach), halves(dmixed), TN)
    passed[0:1, :] += run[BLOCK - 1 :, :]

    @pl.when(step == count - 1)
    def _():
        out_ref[...] = state[...]


def mix_back_kernel(
    info,
    q_ref,
    k_ref,
    v_ref,
    decay_ref,
    logits_ref,
    states_ref,
    dmixed_ref,
    gate_ref,
    leave_ref,
    back_ref,
    dlogits_ref,
    dbias_ref,
    state,
):
    step, count = pl.program_id(0), pl.num_programs(0)
    at = count - 1 - step

    @pl.when(step == 0)
    def _():
        state[...] = leave_ref[...]
        dbias_ref[...] = jnp.zeros_like(dbias_ref)

    after, begin = state[...], states_ref[0]
    decay = decay_ref[...]
    run = running_sum(decay)
    middle, closing = run[HALF - 1 : HALF, :], run[BLOCK - 1 :, :]
    q, k = q_ref[...] * DK ** (-0.5), k_ref[...]
    grow, shrink = jnp.exp(run - middle), jnp.exp(middle - run)
    from_start, to_end = jnp.exp(run), jnp.exp(closing - run)
    near_q, near_k = halves(q * grow), halves(k * shrink)
    v, dout = halves(v_ref[...]), halves(dmixed_ref[...])
    after_parts = halves(after)
    keep = triangle(True)
    scores = halves(jnp.where(keep, fine(near_q, near_k, NT), 0.0))
    dscores = halves(jnp.where(keep, fine(dout, v, NT), 0.0))
    tail = k * to_end
    dtail = fine(v, after_parts, NT)
    dq = fine(dscores, near_k) * grow + fine(dout, halves(begin), NT) * from_start
    dk = fine(dscores, near_q, TN) * shrink + dtail * to_end
    dv = fine(scores, dout, TN) + fine(halves(tail), after_parts)
    ones = jnp.ones((16, DV), LOW)
    high, low = halves(begin * after)
    across = (dot(ones, high, NT) + dot(ones, low, NT))[0:1, :]
    dclosing = jnp.sum(dtail * tail, axis=0, keepdims=True) + jnp.exp(closing) * across
    ddecay = running_sum(dq * q - dk * k, lower=False) + dclosing
    dlogits = ddecay * jax.nn.sigmoid(-logits_ref[...]) * (1.0 / 16.0)
    dlogits_ref[...] = dlogits
    dbias_ref[...] += jnp.sum(dlogits, axis=0, keepdims=True)
    back_ref[:, :DK] = (dq * DK ** (-0.5)).astype(LOW)
    back_ref[:, DK : 2 * DK] = dk.astype(LOW)
    back_ref[:, 2 * DK : 2 * DK + DV] = dv.astype(LOW)
    back_ref[:, 2 * DK + DV :] = gate_ref[...]
    before = widen(jnp.exp(column_sum(decay)), DV) * after + fine(halves(q * from_start), dout, TN)
    state[...] = jnp.where(info[1 + at] > 0, jnp.zeros_like(before), before)


PARAMS = pltpu.CompilerParams(
    dimension_semantics=("arbitrary",), vmem_limit_bytes=40 * 1024 * 1024
)


def token_call(kernel, info, count, quarter, reverse, inputs, outputs, scratch, flops):
    per = quarter // BLOCK

    def place(i):
        return count - 1 - i if reverse else i

    def spec(shape, column):
        if column is None:
            return pl.BlockSpec(shape, lambda i, info: (0, 0))
        if column == "state":
            return pl.BlockSpec(shape, lambda i, info: (place(i), 0, 0))

        def index(i, info):
            j = place(i)
            return ((j // per) ^ info[0]) * per + j % per, column

        return pl.BlockSpec(shape, index)

    return pl.pallas_call(
        kernel,
        grid_spec=pltpu.PrefetchScalarGridSpec(
            num_scalar_prefetch=1,
            grid=(count,),
            in_specs=[spec(shape, column) for _, shape, column in inputs],
            out_specs=[spec(shape, column) for _, shape, column in outputs],
            scratch_shapes=scratch,
        ),
        out_shape=[out for out, _, _ in outputs],
        compiler_params=PARAMS,
        cost_estimate=pl.CostEstimate(flops=flops, bytes_accessed=1 << 24, transcendentals=1 << 20),
    )(info, *[array for array, _, _ in inputs])


def shape_of(*extent, dtype=FULL):
    return jax.ShapeDtypeStruct(extent, dtype)


def columns_in_kernel(order, core, a, b, c, d, oa, ob, oc, od):
    oa[...] = a[...]
    ob[...] = b[...]
    oc[...] = c[...]
    od[...] = d[...]


def columns_in(hidden, cotangent, gain_a, gain_b, order, core, quarter, wide):
    count = order.shape[0]
    if wide % LANES:
        def pick(x):
            return jnp.concatenate(
                [lax.dynamic_slice_in_dim(x, order[i] * wide, wide, 1) for i in range(count)], axis=1
            )

        def rows(x):
            return lax.dynamic_slice_in_dim(x, core * quarter, quarter, 0)

        return pick(rows(hidden)), pick(rows(cotangent)), pick(gain_a), pick(gain_b)
    big = pl.BlockSpec((quarter, wide), lambda i, order, core: (core[0], order[i]))
    small = pl.BlockSpec((1, wide), lambda i, order, core: (0, order[i]))
    big_out = pl.BlockSpec((quarter, wide), lambda i, order, core: (0, i))
    small_out = pl.BlockSpec((1, wide), lambda i, order, core: (0, i))
    total = count * wide
    return pl.pallas_call(
        columns_in_kernel,
        grid_spec=pltpu.PrefetchScalarGridSpec(
            num_scalar_prefetch=2,
            grid=(count,),
            in_specs=[big, big, small, small],
            out_specs=[big_out, big_out, small_out, small_out],
        ),
        out_shape=[
            shape_of(quarter, total, dtype=LOW),
            shape_of(quarter, total, dtype=LOW),
            shape_of(1, total),
            shape_of(1, total),
        ],
        compiler_params=PARAMS,
    )(order, core.reshape(1), hidden, cotangent, gain_a, gain_b)


def columns_out_kernel(order, core, mine, near, out):
    quarter = mine.shape[0]
    first = core[0] == 0
    out[:quarter, :] = jnp.where(first, mine[...], near[...])
    out[quarter:, :] = jnp.where(first, near[...], mine[...])


def columns_out(mine, near, order, inverse, core, wide):
    quarter, total = mine.shape
    count = order.shape[0]
    if wide % LANES:
        first = core == 0
        both = jnp.concatenate([jnp.where(first, mine, near), jnp.where(first, near, mine)], axis=0)
        return jnp.concatenate(
            [lax.dynamic_slice_in_dim(both, inverse[i] * wide, wide, 1) for i in range(count)], axis=1
        )
    spec = pl.BlockSpec((quarter, wide), lambda i, order, core: (0, i))
    return pl.pallas_call(
        columns_out_kernel,
        grid_spec=pltpu.PrefetchScalarGridSpec(
            num_scalar_prefetch=2,
            grid=(count,),
            in_specs=[spec, spec],
            out_specs=pl.BlockSpec((2 * quarter, wide), lambda i, order, core: (0, order[i])),
        ),
        out_shape=shape_of(2 * quarter, total, dtype=mine.dtype),
        compiler_params=PARAMS,
    )(order, core.reshape(1), mine, near)


def block_resets(lengths, dealing, count, start):
    number = lengths.shape[0]
    picks = (dealing[:, None] == jnp.arange(number, dtype=jnp.int32)[None, :]).astype(jnp.int32)
    placed = jnp.sum(picks * lengths[None, :], axis=1, dtype=jnp.int32)
    ends = jnp.cumsum(placed, dtype=jnp.int32)
    starts = ends - placed
    firsts = start + jnp.arange(count, dtype=jnp.int32)
    return jnp.any(firsts[:, None] == starts[None, :], axis=1).astype(jnp.int32)


def tied(*values):
    return lax.optimization_barrier(values)


def silu(x):
    return x * jax.nn.sigmoid(x)


def shards(
    hidden_in,
    cotangent,
    lengths,
    dealing,
    norm_attn,
    w_query,
    w_key,
    w_value,
    w_rank_in,
    w_rank_out,
    decay_bias,
    w_gate_out,
    head_gain,
    w_out,
    norm_mlp,
    w_ff_gate,
    w_ff_up,
    w_ff_down,
):
    peers = lax.axis_size("seq")
    place, core = lax.axis_index("seq"), lax.axis_index("head")
    laps, groups = peers // 4, peers // 2
    group, left = place // 2, place % 2 == 0
    rows, width = hidden_in.shape
    quarter = rows // 2
    tokens = 4 * quarter
    count = tokens // BLOCK
    wide = width // groups
    ff = w_ff_gate.shape[1] // 2

    def pair(x):
        return lax.ppermute(x, "seq", [(i, i ^ 1) for i in range(peers)])

    def side(x):
        return lax.ppermute(x, "seq", [(i, i ^ 2) for i in range(peers)])

    def ring(x):
        return lax.ppermute(x, "seq", [(i, (i + 4) % peers) for i in range(peers)])

    def twin(x):
        return lax.ppermute(x, "head", [(0, 1), (1, 0)])

    lap, flank = group // 2, group % 2
    steps = jnp.arange(groups, dtype=jnp.int32)
    order = ((lap - steps % laps) % laps) * 2 + (flank ^ (steps // laps))
    inverse = (flank ^ (steps % 2)) * laps + (lap - steps // 2) % laps
    resets = block_resets(lengths, dealing, count, group * count)
    ahead = jnp.cumsum(resets)
    info = jnp.concatenate(
        [
            ((place % 2) * 2 + core).astype(jnp.int32).reshape(1),
            resets,
            (ahead == ahead[-1]).astype(jnp.int32),
            (ahead == 0).astype(jnp.int32),
            (ahead[-1:] == 0).astype(jnp.int32),
        ]
    )

    def split(*arrays):
        mid = [a.shape[1] // 2 for a in arrays]
        low = jnp.concatenate([a[:, :m] for a, m in zip(arrays, mid)], axis=1)
        high = jnp.concatenate([a[:, m:] for a, m in zip(arrays, mid)], axis=1)
        return jnp.where(left, low, high), jnp.where(left, high, low)

    def exchanged(mine, other):
        got = pair(other)
        return jnp.concatenate(
            [jnp.where(left, mine, got), jnp.where(left, got, mine)], axis=0
        )

    def collected(own, after):
        if after is not None:
            own, _ = tied(own, after)
        blocks, others = [own], []
        for step in range(laps):
            if step < laps - 1:
                new, other = tied(ring(blocks[-1]), side(blocks[-1]))
                blocks.append(new)
                others.append(other)
            else:
                others.append(side(blocks[-1]))
        return jnp.concatenate(blocks + others, axis=0), blocks[-1]

    mine_q, other_q = split(w_query, w_key, w_value, w_gate_out)
    mine_o, other_o = split(w_out.T)
    mine_f, other_f = split(w_ff_gate, w_ff_up)
    mine_d, other_d = split(w_ff_down.T)
    pair_q = exchanged(mine_q, other_q)

    hidden_low, cot_own, gain_attn, gain_mlp = columns_in(
        hidden_in, cotangent, norm_attn[None], norm_mlp[None], order, core, quarter, wide
    )
    rank_weight = jnp.concatenate(
        [lax.dynamic_slice_in_dim(w_rank_in, order[i] * wide, wide, 0) for i in range(groups)], axis=0
    )

    def spread(x):
        near, far = twin(x), pair(x)
        return jnp.concatenate([x, near, far, twin(far)], axis=0)

    def gathered_sum(parts):
        q = quarter
        far = parts[2 * q : 3 * q] + twin(parts[3 * q :].astype(LOW))
        got = pair(far.astype(LOW))
        return parts[:q] + twin(parts[q : 2 * q].astype(LOW)) + got

    hidden = hidden_low.astype(FULL)
    scale_attn = lax.rsqrt(jnp.mean(hidden * hidden, axis=1, keepdims=True) + EPSILON)
    first = spread((hidden * scale_attn * gain_attn).astype(LOW))

    full_q, done = collected(pair_q, None)
    other_o, other_f, other_d, _ = tied(other_o, other_f, other_d, first)
    pair_o, pair_f, pair_d = (
        exchanged(mine_o, other_o),
        exchanged(mine_f, other_f),
        exchanged(mine_d, other_d),
    )
    full_o, done = collected(pair_o, done)
    full_f, done = collected(pair_f, done)
    full_d, done = collected(pair_d, done)

    mixes = dot(first, full_q)
    rank_in = dot(first, rank_weight).astype(LOW)
    rank_out = jnp.where(left, w_rank_out[:, :DK], w_rank_out[:, DK:])
    bias = jnp.where(left, decay_bias[:DK], decay_bias[DK:])
    logits = dot(rank_in, rank_out) + bias
    decay = jax.nn.log_sigmoid(logits) / 16.0
    gain = head_gain[None]
    state_scratch = pltpu.VMEM((DK, DV), FULL)
    row_scratch = pltpu.VMEM((8, DK), FULL)
    key_block, val_block = (BLOCK, DK), (BLOCK, DV)
    state_shape = (DK, DV)
    call = functools.partial(token_call, info=info, count=count, quarter=quarter)
    (summary,) = call(
        summary_kernel,
        reverse=True,
        inputs=[(mixes, key_block, 1), (mixes, val_block, 1), (decay, key_block, 0)],
        outputs=[(shape_of(DK, DV + LANES), (DK, DV + LANES), None)],
        scratch=[state_scratch, row_scratch, pltpu.VMEM((DK, LANES), FULL)],
        flops=1 << 30,
    )
    halves_of_seq = [[i for i in range(peers) if i % 2 == k] for k in range(2)]
    slab = DK // groups

    def turned(x):
        return lax.all_to_all(x, "seq", 0, 0, axis_index_groups=halves_of_seq, tiled=True)

    pieces = turned(summary).reshape(groups, slab, DV + LANES)
    through = pieces[:, :, DV : DV + 1]

    def carried(local, backwards):
        current, out = jnp.zeros((slab, DV), FULL), [None] * groups
        for j in reversed(range(groups)) if backwards else range(groups):
            out[j] = current
            current = through[j] * current + local[j]
        return turned(jnp.concatenate(out, axis=0))

    entering = carried(pieces[:, :, :DV], False)
    mixed, gated, states = call(
        mix_kernel,
        reverse=False,
        inputs=[
            (mixes, key_block, 0),
            (mixes, key_block, 1),
            (mixes, val_block, 1),
            (mixes, val_block, 2),
            (decay, key_block, 0),
            (entering, state_shape, None),
            (gain, (1, DV), None),
        ],
        outputs=[
            (shape_of(tokens, DV), val_block, 0),
            (shape_of(tokens, DV, dtype=LOW), val_block, 0),
            (shape_of(count, DK, DV), (1, DK, DV), "state"),
        ],
        scratch=[state_scratch],
        flops=3 << 30,
    )
    resid = hidden + gathered_sum(dot(gated, full_o, NT))
    scale_mlp = lax.rsqrt(jnp.mean(resid * resid, axis=1, keepdims=True) + EPSILON)
    second = spread((resid * scale_mlp * gain_mlp).astype(LOW))
    ff_both = dot(second, full_f)
    ff_pre, up_pre = ff_both[:, :ff], ff_both[:, ff:]
    inner = (silu(ff_pre) * up_pre).astype(LOW)
    cot_own, _ = tied(cot_own, done)
    cot = spread(cot_own)

    def reduced(tokens_left, tokens_right):
        def part(k):
            return dot(tokens_left[:, k * wide : (k + 1) * wide], tokens_right, TN)

        turn = [(p + 1) % laps for p in range(laps)]
        sent = {p: side(part(laps + p).astype(LOW)) for p in turn}
        own = {p: part(p) + sent[p] for p in turn}
        current = own[turn[0]]
        for p in turn[1:]:
            current = own[p] + ring(current.astype(LOW))
        high, low = current[: wide // 2], current[wide // 2 :]
        mine = jnp.where(left, high, low)
        got = pair(jnp.where(left, low, high).astype(LOW)).astype(FULL)
        return jnp.where(left, mine, got), jnp.where(left, got, mine)

    down_halves = reduced(cot, inner)
    out_own = (resid + gathered_sum(dot(inner, full_d, NT))).astype(LOW)
    block_out = columns_out(out_own, twin(out_own), order, inverse, core, wide)

    grad_inner = dot(cot, full_d)
    soft = jax.nn.sigmoid(ff_pre)
    ff_back = (grad_inner * up_pre * (soft * (1.0 + ff_pre * (1.0 - soft)))).astype(LOW)
    up_back = (grad_inner * (ff_pre * soft)).astype(LOW)
    both_back = jnp.concatenate([ff_back, up_back], axis=1)
    grad_second = gathered_sum(dot(both_back, full_f, NT))
    gate_halves = reduced(second, both_back[:, :ff])
    up_halves = reduced(second, both_back[:, ff:])

    def norm_back(grad, value, scale, gains):
        normed = value * scale
        scaled = grad * gains
        gain_grad = jnp.sum(grad * normed, axis=0, keepdims=True)
        return scale * (scaled - normed * jnp.mean(scaled * normed, axis=1, keepdims=True)), gain_grad

    resid_norm, grad_gain_mlp = norm_back(grad_second, resid, scale_mlp, gain_mlp)
    grad_resid = cot_own.astype(FULL) + resid_norm
    resid_back = spread(grad_resid.astype(LOW))
    grad_gated = dot(resid_back, full_o)
    gate_back, dmixed, summary_back, grad_gain_head = call(
        gate_back_kernel,
        reverse=False,
        inputs=[
            (mixes, key_block, 0),
            (mixes, val_block, 2),
            (decay, key_block, 0),
            (mixed, val_block, 0),
            (grad_gated, val_block, 0),
            (gain, (1, DV), None),
        ],
        outputs=[
            (shape_of(tokens, DV, dtype=LOW), val_block, 0),
            (shape_of(tokens, DV), val_block, 0),
            (shape_of(DK, DV), state_shape, None),
            (shape_of(1, DV), (1, DV), None),
        ],
        scratch=[state_scratch, row_scratch],
        flops=1 << 30,
    )
    out_halves = reduced(resid_back, gated)
    leaving = carried(turned(summary_back).reshape(groups, slab, DV), True)
    mixes_back, grad_logits, grad_bias = call(
        mix_back_kernel,
        reverse=True,
        inputs=[
            (mixes, key_block, 0),
            (mixes, key_block, 1),
            (mixes, val_block, 1),
            (decay, key_block, 0),
            (logits, key_block, 0),
            (states, (1, DK, DV), "state"),
            (dmixed, val_block, 0),
            (gate_back, val_block, 0),
            (leaving, state_shape, None),
        ],
        outputs=[
            (shape_of(tokens, mixes.shape[1], dtype=LOW), (BLOCK, mixes.shape[1]), 0),
            (shape_of(tokens, DK), key_block, 0),
            (shape_of(1, DK), (1, DK), None),
        ],
        scratch=[state_scratch],
        flops=8 << 30,
    )
    mix_halves = reduced(first, mixes_back)
    precise = lax.Precision.HIGHEST
    grad_rank_out = lax.dot_general(
        rank_in.astype(FULL), grad_logits, (TN, ((), ())), precision=precise
    )
    grad_rank = lax.dot_general(
        grad_logits, rank_out.astype(FULL), (NT, ((), ())), precision=precise
    )
    rank_high = grad_rank.astype(LOW)
    rank_low = (grad_rank - rank_high.astype(FULL)).astype(LOW)
    first_parts = dot(mixes_back, full_q, NT) + (
        dot(rank_high, rank_weight, NT) + dot(rank_low, rank_weight, NT)
    )
    grad_rank_in = dot(rank_high, first, TN) + dot(rank_low, first, TN)
    grad_first = gathered_sum(first_parts)
    hidden_norm, grad_gain_attn = norm_back(grad_first, hidden, scale_attn, gain_attn)
    input_own = grad_resid + hidden_norm
    grad_input = columns_out(input_own, twin(input_own), order, inverse, core, wide)

    def unordered(x):
        return jnp.concatenate(
            [lax.dynamic_slice_in_dim(x, inverse[i] * wide, wide, 1) for i in range(groups)], axis=1
        )

    wide_part = jnp.concatenate(
        [grad_rank_in, grad_gain_attn, grad_gain_mlp, jnp.zeros((6, width), FULL)], axis=0
    )
    wide_part = unordered(wide_part + twin(wide_part))
    empty = jnp.zeros_like(grad_rank_out)
    rank_part = jnp.concatenate(
        [jnp.where(left, grad_rank_out, empty), jnp.where(left, empty, grad_rank_out)], axis=1
    )
    bias_part = jnp.concatenate(
        [jnp.where(left, grad_bias, 0.0), jnp.where(left, 0.0, grad_bias)], axis=1
    )
    head_part = grad_gain_head + twin(grad_gain_head)
    narrow_part = jnp.concatenate(
        [rank_part, bias_part, head_part, jnp.zeros((6, 2 * DK), FULL)], axis=0
    )
    small = jnp.concatenate([wide_part, narrow_part], axis=1)
    hop = 1
    while hop < peers:
        small = small + lax.ppermute(small, "seq", [(i, i ^ hop) for i in range(peers)])
        hop *= 2

    def beside(pieces, start, stop):
        return jnp.concatenate([half[:, start:stop] for half in pieces], axis=1)

    return (
        block_out,
        grad_input,
        small[16, :width],
        beside(mix_halves, 0, DK),
        beside(mix_halves, DK, 2 * DK),
        beside(mix_halves, 2 * DK, 2 * DK + DV),
        small[:16, :width].T,
        small[:16, width:],
        small[16, width:],
        beside(mix_halves, 2 * DK + DV, 2 * DK + 2 * DV),
        small[17, width:],
        jnp.concatenate(out_halves, axis=1).T,
        small[17, :width],
        jnp.concatenate(gate_halves, axis=1),
        jnp.concatenate(up_halves, axis=1),
        jnp.concatenate(down_halves, axis=1).T,
    )


def solution(mesh):
    return jax.shard_map(
        shards,
        mesh=mesh,
        in_specs=(
            P("seq", None),
            P("seq", None),
            P(),
            P(),
            P(),
            P("seq", "head"),
            P("seq", "head"),
            P("seq", "head"),
            P(),
            P(None, "head"),
            P("head"),
            P("seq", "head"),
            P(),
            P("head", "seq"),
            P(),
            P("seq", "head"),
            P("seq", "head"),
            P("head", "seq"),
        ),
        out_specs=(
            P("seq", None),
            P("seq", None),
            P(),
            P("seq", "head"),
            P("seq", "head"),
            P("seq", "head"),
            P(),
            P(None, "head"),
            P("head"),
            P("seq", "head"),
            P(),
            P("head", "seq"),
            P(),
            P("seq", "head"),
            P("seq", "head"),
            P("head", "seq"),
        ),
        check_vma=False,
    )
```

time: 4640 us -> 1020 us (0.22)
  waiting for transfers between devices: 3850 us -> 519 us
  matrix products: 337 us -> 183 us
  blocking collectives: 125 us -> 0 us
  starting transfers between devices: 1.85 us -> 100 us
  other arithmetic: 143 us -> 59.6 us
  local copies, waits for them, and re-layouts: 132 us -> 74.4 us
  Pallas kernels: 0 us -> 53.8 us
    reduce_scatter x8 -> x0, waiting for transfers between devices: 2050 us -> none  [the longest x1 483 us: shards(): lax.psum_scatter(grad_w_ff_up, 'seq', scatter_dimension=0, tiled=True)]
    all_gather x18 -> x0, waiting for transfers between devices: 1610 us -> none  [the longest x2 328 us: carried_in(): everything = jax.tree.map(lambda part: lax.all_gather(part, axis), x)]
    ppermute x0 -> x104, waiting for transfers between devices: none -> 517 us  [the longest x27 209 us: ring(): return lax.ppermute(x, 'seq', [(i, (i + 4) % peers) for i in range(peers)])]
    psum x5 -> x0, waiting for transfers between devices: 189 us -> none  [the longest x1 112 us: shards(): lax.psum((grad_norm_attn_local, grad_norm_mlp_local, grad_rank_in_heads,...]
    dot_general x143 -> x56, matrix products: 336 us -> 183 us  [the longest x54 182 us: dot(): lax.dot_general(left, right, (dims, ((), ())), preferred_element_type=FULL)]
    psum x2 -> x0, blocking collectives: 85.9 us -> none  [the longest x1 83.4 us: shards(): lax.psum((grad_norm_attn_local, grad_norm_mlp_local, grad_rank_in_heads,...]
    ppermute x0 -> x104, starting transfers between devices: none -> 82.1 us  [the longest x36 40.5 us: side(): return lax.ppermute(x, 'seq', [(i, i ^ 2) for i in range(peers)])]
    pallas_call x0 -> x7, Pallas kernels: none -> 53.8 us  [the longest x4 44.3 us: token_call(): pl.pallas_call(kernel, grid_spec=pltpu.PrefetchScalarGridSpec(num_scalar_...]
  transfers between devices with their start and end apart: 31 -> 108, of which waited for: 27 -> 43; matrix products, arithmetic and copies ran while one was open for 10% -> 20% of each run, Pallas kernels for 0% -> 3%
where the time goes in v1:
time: 1020 us; the launch traced here: 1000 us
  waiting for transfers between devices  519 us (51%)
  matrix products  183 us (18%)
  starting transfers between devices  100 us (10%)
  local copies, waits for them, and re-layouts  74.4 us (7%)
  other arithmetic  59.6 us (6%)
  Pallas kernels  53.8 us (5%)
  between operations  14.1 us (1%)
    ppermute x27, waiting for transfers between devices, ring(): return lax.ppermute(x, 'seq', [(i, (i + 4) % peers) for i in range(peers)])  209 us
    ppermute x36, waiting for transfers between devices, side(): return lax.ppermute(x, 'seq', [(i, i ^ 2) for i in range(peers)])  203 us
    dot_general x54, matrix products, dot(): lax.dot_general(left, right, (dims, ((), ())), preferred_element_type=FULL)  182 us
    ppermute x17, waiting for transfers between devices, pair(): return lax.ppermute(x, 'seq', [(i, i ^ 1) for i in range(peers)])  63.9 us
    unnamed x269, local copies, waits for them, and re-layouts  58 us
    pallas_call x4, Pallas kernels, token_call(): pl.pallas_call(kernel, grid_spec=pltpu.PrefetchScalarGridSpec(num_scalar_...  44.3 us
    ppermute x36, starting transfers between devices, side(): return lax.ppermute(x, 'seq', [(i, i ^ 2) for i in range(peers)])  40.5 us
    ppermute x4, waiting for transfers between devices, shards(): lax.ppermute(small, 'seq', [(i, i ^ hop) for i in range(peers)])  40.4 us
  transfers between devices with their start and end apart: 108, of which 43 were waited for; matrix products, arithmetic and copies ran while one was open for 20% of the time, Pallas kernels for 3%

profile of v1, /device:TPU:0, one launch (start us, length us, event | category | flops | bytes accessed | tf_op | source)
XLA Modules:
  0.0 1003.9 jit_solution(5752916104969128691)
XLA Ops:
  8.4 2.9 collective-permute-start.1
  32.1 11.2 %collective-permute-done.3 = bf16[128,1536]{1,0:T(8,128)(2,1)} collective-permute-done((bf16[128,1536]{1,0:T(8,128)(2,1)}, bf16[128,1536]{1,0:T(8,128)(2,1)}, u32[]{:S(2)}, u32[]{:S(2)}) %collective-permute-start.3) | collective-permute-done | bytes 393248 | tf_op jit(solution)/shard_map/ppermute | solution.py:374
  50.5 15.8 %collective-permute-done.4 = bf16[256,1536]{1,0:T(8,128)(2,1)S(1)} collective-permute-done((bf16[256,1536]{1,0:T(8,128)(2,1)S(1)}, bf16[256,1536]{1,0:T(8,128)(2,1)S(1)}, u32[]{:S(2)}, u32[]{:S(2)}) %collective-permute-start.4) | collective-permute-done | bytes 786464 | tf_op jit(solution)/shard_map/ppermute | solution.py:380
  70.4 15.5 %collective-permute-done.6 = bf16[256,1536]{1,0:T(8,128)(2,1)S(1)} collective-permute-done((bf16[256,1536]{1,0:T(8,128)(2,1)S(1)}, bf16[256,1536]{1,0:T(8,128)(2,1)S(1)}, u32[]{:S(2)}, u32[]{:S(2)}) %collective-permute-start.6) | collective-permute-done | bytes 786464 | tf_op jit(solution)/shard_map/ppermute | solution.py:380
  95.1 9.5 collective-permute-done.8
  105.9 14.6 %collective-permute-done.10 = bf16[256,1536]{1,0:T(8,128)(2,1)S(1)} collective-permute-done((bf16[256,1536]{1,0:T(8,128)(2,1)S(1)}, bf16[256,1536]{1,0:T(8,128)(2,1)S(1)}, u32[]{:S(2)}, u32[]{:S(2)}) %collective-permute-start.10) | collective-permute-done | bytes 786464 | tf_op jit(solution)/shard_map/ppermute | solution.py:377
  120.6 6.7 fusion.166.k_ref.v_ref.q_ref.g_ref
  127.3 7.4 shard_map.298
  135.5 4.5 all-to-all-start
  147.4 8.9 collective-permute-done.12
  162.3 3.1 collective-permute-done.14
  181.3 4.1 all-to-all-start.1
  200.2 29.2 %collective-permute-done.18 = bf16[256,512]{1,0:T(8,128)(2,1)S(1)} collective-permute-done((bf16[256,512]{1,0:T(8,128)(2,1)}, bf16[256,512]{1,0:T(8,128)(2,1)S(1)}, u32[]{:S(2)}, u32[]{:S(2)}) %collective-permute-start.18) | collective-permute-done | bytes 262176 | tf_op jit(solution)/shard_map/ppermute | solution.py:377
  230.1 10.7 %shard_map.299 = (f32[1024,512]{1,0:T(8,128)S(1)}, bf16[1024,512]{1,0:T(8,128)(2,1)S(1)}, f32[8,256,512]{2,1,0:T(8,128)S(1)}) custom-call(s32[26]{0:T(128)S(1)} %concatenate.103.info, f32[1024,1536]{1,0:T(8,128)} %copy-done, f32[1024,1536]{1,0:T(8,128)} %copy-done, f32[1024,1536]{1,0:T(8,128)} %copy-done, f32[1024,1536]{1,0:T(8,128)} %copy-done, ...), custom_call_target="tpu_custom_call" | custom-call | flops 3221225472 | bytes 16777216 | tf_op jit(solution)/shard_map/pallas_call | solution.py:233
  240.8 8.8 fusion.162
  267.1 28.0 %collective-permute-done.28 = bf16[256,2816]{1,0:T(8,128)(2,1)S(1)} collective-permute-done((bf16[256,2816]{1,0:T(8,128)(2,1)}, bf16[256,2816]{1,0:T(8,128)(2,1)S(1)}, u32[]{:S(2)}, u32[]{:S(2)}) %collective-permute-start.28) | collective-permute-done | bytes 1441824 | tf_op jit(solution)/shard_map/ppermute | solution.py:380
  299.8 30.2 %collective-permute-done.30 = bf16[256,2816]{1,0:T(8,128)(2,1)S(1)} collective-permute-done((bf16[256,2816]{1,0:T(8,128)(2,1)S(1)}, bf16[256,2816]{1,0:T(8,128)(2,1)S(1)}, u32[]{:S(2)}, u32[]{:S(2)}) %collective-permute-start.30) | collective-permute-done | bytes 1441824 | tf_op jit(solution)/shard_map/ppermute | solution.py:380
  333.8 14.9 %collective-permute-done.34 = bf16[256,1408]{1,0:T(8,128)(2,1)S(1)} collective-permute-done((bf16[256,1408]{1,0:T(8,128)(2,1)S(1)}, bf16[256,1408]{1,0:T(8,128)(2,1)S(1)}, u32[]{:S(2)}, u32[]{:S(2)}) %collective-permute-start.34) | collective-permute-done | bytes 720928 | tf_op jit(solution)/shard_map/ppermute | solution.py:380
  350.5 29.5 %collective-permute-done.32 = bf16[256,2816]{1,0:T(8,128)(2,1)S(1)} collective-permute-done((bf16[256,2816]{1,0:T(8,128)(2,1)S(1)}, bf16[256,2816]{1,0:T(8,128)(2,1)S(1)}, u32[]{:S(2)}, u32[]{:S(2)}) %collective-permute-start.32) | collective-permute-done | bytes 1441824 | tf_op jit(solution)/shard_map/ppermute | solution.py:377
  380.1 13.1 %collective-permute-done.37 = bf16[256,1408]{1,0:T(8,128)(2,1)S(1)} collective-permute-done((bf16[256,1408]{1,0:T(8,128)(2,1)S(1)}, bf16[256,1408]{1,0:T(8,128)(2,1)S(1)}, u32[]{:S(2)}, u32[]{:S(2)}) %collective-permute-start.37) | collective-permute-done | bytes 720928 | tf_op jit(solution)/shard_map/ppermute | solution.py:377
  396.8 17.5 %fusion.136 = f32[1024,2816]{1,0:T(8,128)} fusion(bf16[2048,2816]{1,0:T(8,128)(2,1)} %copy-done.71, bf16[256,2048]{1,0:T(8,128)(2,1)S(1)} %collective-permute-done.24, bf16[256,2048]{1,0:T(8,128)(2,1)S(1)} %collective-permute-done.23, bf16[256,2048]{1,0:T(8,128)(2,1)S(1)} %collective-permute-done.22, bf16[256,2048]{1,0:T(8,128)(2,1)S(1)} %multiply_convert_fusion.3), kind=kOutput, calls=%fused_computation.383 | convolution fusion | flops 11827937280 | bytes 27262976 | tf_op jit(solution)/shard_map/dot_general | solution.py:25
  421.9 16.8 %collective-permute-done.46 = bf16[256,2048]{1,0:T(8,128)(2,1)S(1)} collective-permute-done((bf16[256,2048]{1,0:T(8,128)(2,1)S(1)}, bf16[256,2048]{1,0:T(8,128)(2,1)S(1)}, u32[]{:S(2)}, u32[]{:S(2)}) %collective-permute-start.46) | collective-permute-done | bytes 1048608 | tf_op jit(solution)/shard_map/ppermute | solution.py:374
  444.6 14.5 %multiply_convert_fusion.1 = (bf16[1024,1408]{1,0:T(8,128)(2,1)S(1)}, bf16[1024,1408]{1,0:T(8,128)(2,1)S(1)}, bf16[1024,1408]{1,0:T(8,128)(2,1)S(1)}) fusion(f32[1024,2816]{1,0:T(8,128)} %fusion.136, bf16[1024,2048]{1,0:T(8,128)(2,1)} %constant_dynamic-update-slice_fusion.49, bf16[2048,1408]{1,0:T(8,128)(2,1)} %constant_dynamic-update-slice_fusion.41), kind=kOutput, calls=%fused_computation.6 | convolution fusion | flops 5927206912 | bytes 30146560 | tf_op jit(solution)/shard_map/dot_general | solution.py:25
  459.1 3.6 convolution_convert_fusion.3
  462.8 3.0 convolution_convert_fusion.2
  465.7 2.9 convolution_convert_fusion.1
  468.6 2.9 convolution_convert_fusion
  484.7 9.6 fusion.164
  494.3 19.7 %fusion.163 = (bf16[1024,2048]{1,0:T(8,128)(2,1)}, f32[1024,2048]{1,0:T(8,128)}) fusion(bf16[2048,2816]{1,0:T(8,128)(2,1)} %copy-done.71, bf16[1024,1408]{1,0:T(8,128)(2,1)} %copy-done.30, bf16[1024,1408]{1,0:T(8,128)(2,1)} %copy-done.28), kind=kOutput, calls=%fused_computation.404 | convolution fusion | flops 11824791552 | bytes 29884416 | tf_op jit(solution)/shard_map/dot_general | solution.py:25
  525.2 23.4 %collective-permute-done.99 = bf16[256,1408]{1,0:T(8,128)(2,1)S(1)} collective-permute-done((bf16[256,1408]{1,0:T(8,128)(2,1)}, bf16[256,1408]{1,0:T(8,128)(2,1)S(1)}, u32[]{:S(2)}, u32[]{:S(2)}) %collective-permute-start.99) | collective-permute-done | bytes 720928 | tf_op jit(solution)/shard_map/ppermute | solution.py:377
  550.7 28.8 %collective-permute-done.91 = bf16[256,1408]{1,0:T(8,128)(2,1)S(1)} collective-permute-done((bf16[256,1408]{1,0:T(8,128)(2,1)}, bf16[256,1408]{1,0:T(8,128)(2,1)S(1)}, u32[]{:S(2)}, u32[]{:S(2)}) %collective-permute-start.91) | collective-permute-done | bytes 720928 | tf_op jit(solution)/shard_map/ppermute | solution.py:377
  580.6 14.0 %collective-permute-done.83 = bf16[256,1408]{1,0:T(8,128)(2,1)S(1)} collective-permute-done((bf16[256,1408]{1,0:T(8,128)(2,1)}, bf16[256,1408]{1,0:T(8,128)(2,1)S(1)}, u32[]{:S(2)}, u32[]{:S(2)}) %collective-permute-start.83) | collective-permute-done | bytes 720928 | tf_op jit(solution)/shard_map/ppermute | solution.py:377
  604.0 13.8 %collective-permute-done.100 = bf16[256,1408]{1,0:T(8,128)(2,1)S(1)} collective-permute-done((bf16[256,1408]{1,0:T(8,128)(2,1)S(1)}, bf16[256,1408]{1,0:T(8,128)(2,1)S(1)}, u32[]{:S(2)}, u32[]{:S(2)}) %collective-permute-start.100) | collective-permute-done | bytes 720928 | tf_op jit(solution)/shard_map/ppermute | solution.py:380
  618.9 3.0 fusion.27
  621.9 11.3 %collective-permute-done.92 = bf16[256,1408]{1,0:T(8,128)(2,1)S(1)} collective-permute-done((bf16[256,1408]{1,0:T(8,128)(2,1)S(1)}, bf16[256,1408]{1,0:T(8,128)(2,1)S(1)}, u32[]{:S(2)}, u32[]{:S(2)}) %collective-permute-start.92) | collective-permute-done | bytes 720928 | tf_op jit(solution)/shard_map/ppermute | solution.py:380
  636.3 10.8 %collective-permute-done.84 = bf16[256,1408]{1,0:T(8,128)(2,1)S(1)} collective-permute-done((bf16[256,1408]{1,0:T(8,128)(2,1)S(1)}, bf16[256,1408]{1,0:T(8,128)(2,1)S(1)}, u32[]{:S(2)}, u32[]{:S(2)}) %collective-permute-start.84) | collective-permute-done | bytes 720928 | tf_op jit(solution)/shard_map/ppermute | solution.py:380
  653.0 9.2 collective-permute-done.43
  663.2 5.7 fusion.140
  669.0 13.0 %collective-permute-done.97 = bf16[256,1408]{1,0:T(8,128)(2,1)} collective-permute-done((bf16[256,1408]{1,0:T(8,128)(2,1)}, bf16[256,1408]{1,0:T(8,128)(2,1)}, u32[]{:S(2)}, u32[]{:S(2)}) %collective-permute-start.97) | collective-permute-done | bytes 720928 | tf_op jit(solution)/shard_map/ppermute | solution.py:377
  685.1 12.3 %collective-permute-done.89 = bf16[256,1408]{1,0:T(8,128)(2,1)} collective-permute-done((bf16[256,1408]{1,0:T(8,128)(2,1)}, bf16[256,1408]{1,0:T(8,128)(2,1)}, u32[]{:S(2)}, u32[]{:S(2)}) %collective-permute-start.89) | collective-permute-done | bytes 720928 | tf_op jit(solution)/shard_map/ppermute | solution.py:377
  700.5 12.2 %collective-permute-done.81 = bf16[256,1408]{1,0:T(8,128)(2,1)S(1)} collective-permute-done((bf16[256,1408]{1,0:T(8,128)(2,1)}, bf16[256,1408]{1,0:T(8,128)(2,1)S(1)}, u32[]{:S(2)}, u32[]{:S(2)}) %collective-permute-start.81) | collective-permute-done | bytes 720928 | tf_op jit(solution)/shard_map/ppermute | solution.py:377
  719.5 8.7 collective-permute-done.88
  728.2 7.9 collective-permute-done.94
  737.2 4.0 collective-permute-done.80
  742.3 11.8 %collective-permute-done.86 = bf16[256,1408]{1,0:T(8,128)(2,1)S(1)} collective-permute-done((bf16[256,1408]{1,0:T(8,128)(2,1)S(1)}, bf16[256,1408]{1,0:T(8,128)(2,1)S(1)}, u32[]{:S(2)}, u32[]{:S(2)}) %collective-permute-start.86) | collective-permute-done | bytes 720928 | tf_op jit(solution)/shard_map/ppermute | solution.py:380
  757.3 3.8 shard_map.300
  761.2 4.3 collective-permute-done.95
  772.3 4.9 fusion.167.grad_ref
  780.5 9.3 shard_map.301
  792.2 3.7 all-to-all-start.2
  802.5 8.6 collective-permute-done.76
  817.0 4.0 collective-permute-done.77
  824.4 6.0 all-to-all-start.3
  850.9 16.9 %shard_map.302 = (bf16[1024,1536]{1,0:T(8,128)(2,1)S(1)}, f32[1024,256]{1,0:T(8,128)S(1)}, f32[1,256]{1,0:T(1,128)S(1)}) custom-call(s32[26]{0:T(128)S(1)} %concatenate.103.info, f32[1024,1536]{1,0:T(8,128)} %copy-done, f32[1024,1536]{1,0:T(8,128)} %copy-done, f32[1024,1536]{1,0:T(8,128)} %copy-done, f32[1024,256]{1,0:T(8,128)S(1)} %get-tuple-element.276.decay_ref, ...), custom_call_target="tpu_custom_call" | custom-call | flops 8589934592 | bytes 16777216 | tf_op jit(solution)/shard_map/pallas_call | solution.py:233
  868.4 4.6 fusion.134
  873.0 4.5 fusion.131
  881.0 15.1 %fusion.165 = (bf16[1024,2048]{1,0:T(8,128)(2,1)}, f32[1024,2048]{1,0:T(8,128)}) fusion(f32[1024,2048]{1,0:T(8,128)} %fusion.131, f32[1024,2048]{1,0:T(8,128)} %fusion.134, bf16[1024,1536]{1,0:T(8,128)(2,1)S(1)} %get-tuple-element.102, bf16[2048,1536]{1,0:T(8,128)(2,1)} %copy-done.77), kind=kOutput, calls=%fused_computation.406 | convolution fusion | flops 6448742400 | bytes 38797312 | tf_op jit(solution)/shard_map/dot_general | solution.py:25
  907.7 21.0 %collective-permute-done.56 = bf16[256,2048]{1,0:T(8,128)(2,1)S(1)} collective-permute-done((bf16[256,2048]{1,0:T(8,128)(2,1)S(1)}, bf16[256,2048]{1,0:T(8,128)(2,1)S(1)}, u32[]{:S(2)}, u32[]{:S(2)}) %collective-permute-start.56) | collective-permute-done | bytes 1048608 | tf_op jit(solution)/shard_map/ppermute | solution.py:374
  934.7 5.1 collective-permute-done.60
  940.9 11.9 %collective-permute-done.69 = bf16[256,1536]{1,0:T(8,128)(2,1)S(1)} collective-permute-done((bf16[256,1536]{1,0:T(8,128)(2,1)S(1)}, bf16[256,1536]{1,0:T(8,128)(2,1)S(1)}, u32[]{:S(2)}, u32[]{:S(2)}) %collective-permute-start.69) | collective-permute-done | bytes 786464 | tf_op jit(solution)/shard_map/ppermute | solution.py:380
  953.9 4.4 collective-permute-done.61
  959.6 20.5 %collective-permute-done.62 = f32[24,2560]{1,0:T(8,128)S(1)} collective-permute-done((f32[24,2560]{1,0:T(8,128)S(1)}, f32[24,2560]{1,0:T(8,128)S(1)}, u32[]{:S(2)}, u32[]{:S(2)}) %collective-permute-start.62) | collective-permute-done | bytes 245792 | tf_op jit(solution)/shard_map/ppermute | solution.py:654
  982.8 10.4 %collective-permute-done.63 = f32[24,2560]{1,0:T(8,128)S(1)} collective-permute-done((f32[24,2560]{1,0:T(8,128)S(1)}, f32[24,2560]{1,0:T(8,128)S(1)}, u32[]{:S(2)}, u32[]{:S(2)}) %collective-permute-start.63) | collective-permute-done | bytes 245792 | tf_op jit(solution)/shard_map/ppermute | solution.py:654
  999.2 4.3 shard_map.303
  (596 shorter events, 277.5 us)
Async XLA Ops:
  8.4 42.1 %collective-permute-start.1 = (bf16[256,2048]{1,0:T(8,128)(2,1)}, bf16[256,2048]{1,0:T(8,128)(2,1)}, u32[]{:S(2)}, u32[]{:S(2)}) collective-permute-start(bf16[256,2048]{1,0:T(8,128)(2,1)} %fusion.33), channel_id=1, source_target_pairs={{0,2},{2,0},{4,6},{6,4},{8,10},{10,8},{12,14},{14,12},{16,18},{18,... | collective-permute-start | bytes 3145736 | tf_op jit(solution)/shard_map/ppermute | solution.py:374
  11.4 76.4 %collective-permute-start = (bf16[256,2048]{1,0:T(8,128)(2,1)}, bf16[256,2048]{1,0:T(8,128)(2,1)}, u32[]{:S(2)}, u32[]{:S(2)}) collective-permute-start(bf16[256,2048]{1,0:T(8,128)(2,1)} %fusion.33), channel_id=1, source_target_pairs={{0,1},{1,0},{2,3},{3,2},{4,5},{5,4},{6,7},{7,6},{8,9},{9,8},{10,11... | collective-permute-start | bytes 3145736 | tf_op jit(solution)/shard_map/ppermute | solution.py:383
  12.4 30.9 %collective-permute-start.3 = (bf16[128,1536]{1,0:T(8,128)(2,1)}, bf16[128,1536]{1,0:T(8,128)(2,1)}, u32[]{:S(2)}, u32[]{:S(2)}) collective-permute-start(bf16[128,1536]{1,0:T(8,128)(2,1)} %broadcast_select_fusion.6), channel_id=1, source_target_pairs={{0,2},{2,0},{4,6},{6,4},{8,10},{10,8},{12,14},{14,12},{16,18},{18,... | collective-permute-start | bytes 1179656 | tf_op jit(solution)/shard_map/ppermute | solution.py:374
  50.5 37.3 %collective-permute-start.2 = (bf16[256,2048]{1,0:T(8,128)(2,1)}, bf16[256,2048]{1,0:T(8,128)(2,1)S(1)}, u32[]{:S(2)}, u32[]{:S(2)}) collective-permute-start(bf16[256,2048]{1,0:T(8,128)(2,1)} %collective-permute-done.1), channel_id=1, source_target_pairs={{0,1},{1,0},{2,3},{3,2},{4,5},{5,4},{6,7},{7,6},{8,9},{9,8},{10,11... | collective-permute-start | bytes 3145736 | tf_op jit(solution)/shard_map/ppermute | solution.py:383
  90.0 49.9 %collective-permute-start.11 = (bf16[128,512]{1,0:T(8,128)(2,1)}, bf16[128,512]{1,0:T(8,128)(2,1)}, u32[]{:S(2)}, u32[]{:S(2)}) collective-permute-start(bf16[128,512]{1,0:T(8,128)(2,1)} %broadcast_select_fusion.14), channel_id=1, source_target_pairs={{0,2},{2,0},{4,6},{6,4},{8,10},{10,8},{12,14},{14,12},{16,18},{18,... | collective-permute-start | bytes 393224 | tf_op jit(solution)/shard_map/ppermute | solution.py:374
  91.6 67.8 %collective-permute-start.25 = (bf16[128,2816]{1,0:T(8,128)(2,1)}, bf16[128,2816]{1,0:T(8,128)(2,1)}, u32[]{:S(2)}, u32[]{:S(2)}) collective-permute-start(bf16[128,2816]{1,0:T(8,128)(2,1)} %broadcast_select_fusion.3), channel_id=1, source_target_pairs={{0,2},{2,0},{4,6},{6,4},{8,10},{10,8},{12,14},{14,12},{16,18},{18,... | collective-permute-start | bytes 2162696 | tf_op jit(solution)/shard_map/ppermute | solution.py:374
  135.5 33.4 %all-to-all-start = ((f32[8,32,640]{2,1,0:T(8,128)}), f32[8,32,640]{2,1,0:T(8,128)}, u32[]{:S(2)}, u32[]{:S(2)}) async-start(f32[8,32,640]{2,1,0:T(8,128)} %bitcast.214), calls=%async_computation | async-start | bytes 1310720 | tf_op jit(solution)/shard_map/all_to_all | solution.py:488
  145.2 112.4 %collective-permute-start.33 = (bf16[128,1408]{1,0:T(8,128)(2,1)}, bf16[128,1408]{1,0:T(8,128)(2,1)}, u32[]{:S(2)}, u32[]{:S(2)}) collective-permute-start(bf16[128,1408]{1,0:T(8,128)(2,1)} %broadcast_select_fusion.11), channel_id=1, source_target_pairs={{0,2},{2,0},{4,6},{6,4},{8,10},{10,8},{12,14},{14,12},{16,18},{18,... | collective-permute-start | bytes 1081352 | tf_op jit(solution)/shard_map/ppermute | solution.py:374
  165.4 25.1 %collective-permute-start.16 = (bf16[256,512]{1,0:T(8,128)(2,1)}, bf16[256,512]{1,0:T(8,128)(2,1)}, u32[]{:S(2)}, u32[]{:S(2)}) collective-permute-start(bf16[256,512]{1,0:T(8,128)(2,1)} %collective-permute-done.14), channel_id=1, source_target_pairs={{0,8},{2,10},{4,12},{6,14},{8,16},{10,18},{12,20},{14,22},{16,24},... | collective-permute-start | bytes 786440 | tf_op jit(solution)/shard_map/ppermute | solution.py:380
  167.3 23.1 %collective-permute-start.17 = (bf16[256,512]{1,0:T(8,128)(2,1)}, bf16[256,512]{1,0:T(8,128)(2,1)}, u32[]{:S(2)}, u32[]{:S(2)}) collective-permute-start(bf16[256,512]{1,0:T(8,128)(2,1)} %collective-permute-done.14), channel_id=1, source_target_pairs={{0,4},{2,6},{4,0},{6,2},{8,12},{10,14},{12,8},{14,10},{16,20},{18,... | collective-permute-start | bytes 786440 | tf_op jit(solution)/shard_map/ppermute | solution.py:377
  181.3 48.7 %all-to-all-start.1 = ((f32[8,32,512]{2,1,0:T(8,128)}), f32[8,32,512]{2,1,0:T(8,128)}, u32[]{:S(2)}, u32[]{:S(2)}) async-start(f32[8,32,512]{2,1,0:T(8,128)} %bitcast.234), calls=%async_computation.1 | async-start | bytes 1048576 | tf_op jit(solution)/shard_map/all_to_all | solution.py:488
  190.5 68.5 %collective-permute-start.26 = (bf16[256,2816]{1,0:T(8,128)(2,1)}, bf16[256,2816]{1,0:T(8,128)(2,1)}, u32[]{:S(2)}, u32[]{:S(2)}) collective-permute-start(bf16[256,2816]{1,0:T(8,128)(2,1)} %pad_maximum_fusion.3), channel_id=1, source_target_pairs={{0,8},{2,10},{4,12},{6,14},{8,16},{10,18},{12,20},{14,22},{16,24},... | collective-permute-start | bytes 4325384 | tf_op jit(solution)/shard_map/ppermute | solution.py:380
  192.4 66.6 %collective-permute-start.27 = (bf16[256,2816]{1,0:T(8,128)(2,1)}, bf16[256,2816]{1,0:T(8,128)(2,1)}, u32[]{:S(2)}, u32[]{:S(2)}) collective-permute-start(bf16[256,2816]{1,0:T(8,128)(2,1)} %pad_maximum_fusion.3), channel_id=1, source_target_pairs={{0,4},{2,6},{4,0},{6,2},{8,12},{10,14},{12,8},{14,10},{16,20},{18,... | collective-permute-start | bytes 4325384 | tf_op jit(solution)/shard_map/ppermute | solution.py:377
  193.8 35.5 %collective-permute-start.18 = (bf16[256,512]{1,0:T(8,128)(2,1)}, bf16[256,512]{1,0:T(8,128)(2,1)S(1)}, u32[]{:S(2)}, u32[]{:S(2)}) collective-permute-start(bf16[256,512]{1,0:T(8,128)(2,1)} %collective-permute-done.16), channel_id=1, source_target_pairs={{0,4},{2,6},{4,0},{6,2},{8,12},{10,14},{12,8},{14,10},{16,20},{18,... | collective-permute-start | bytes 786440 | tf_op jit(solution)/shard_map/ppermute | solution.py:377
  259.0 36.1 %collective-permute-start.28 = (bf16[256,2816]{1,0:T(8,128)(2,1)}, bf16[256,2816]{1,0:T(8,128)(2,1)S(1)}, u32[]{:S(2)}, u32[]{:S(2)}) collective-permute-start(bf16[256,2816]{1,0:T(8,128)(2,1)} %collective-permute-done.26), channel_id=1, source_target_pairs={{0,8},{2,10},{4,12},{6,14},{8,16},{10,18},{12,20},{14,22},{16,24},... | collective-permute-start | bytes 4325384 | tf_op jit(solution)/shard_map/ppermute | solution.py:380
  260.5 34.5 %collective-permute-start.29 = (bf16[256,2816]{1,0:T(8,128)(2,1)}, bf16[256,2816]{1,0:T(8,128)(2,1)S(1)}, u32[]{:S(2)}, u32[]{:S(2)}) collective-permute-start(bf16[256,2816]{1,0:T(8,128)(2,1)} %collective-permute-done.26), channel_id=1, source_target_pairs={{0,4},{2,6},{4,0},{6,2},{8,12},{10,14},{12,8},{14,10},{16,20},{18,... | collective-permute-start | bytes 4325384 | tf_op jit(solution)/shard_map/ppermute | solution.py:377
  260.8 35.3 %collective-permute-start.19 = (bf16[256,2048]{1,0:T(8,128)(2,1)S(1)}, bf16[256,2048]{1,0:T(8,128)(2,1)S(1)}, u32[]{:S(2)}, u32[]{:S(2)}) collective-permute-start(bf16[256,2048]{1,0:T(8,128)(2,1)S(1)} %copy-done.51), channel_id=1, source_target_pairs={{0,1},{1,0},{2,3},{3,2},{4,5},{5,4},{6,7},{7,6},{8,9},{9,8},{10,11... | collective-permute-start | bytes 3145736 | tf_op jit(solution)/shard_map/ppermute | solution.py:383
  263.0 33.0 %collective-permute-start.21 = (bf16[256,2048]{1,0:T(8,128)(2,1)S(1)}, bf16[256,2048]{1,0:T(8,128)(2,1)S(1)}, u32[]{:S(2)}, u32[]{:S(2)}) collective-permute-start(bf16[256,2048]{1,0:T(8,128)(2,1)S(1)} %fusion.48), channel_id=1, source_target_pairs={{0,2},{2,0},{4,6},{6,4},{8,10},{10,8},{12,14},{14,12},{16,18},{18,... | collective-permute-start | bytes 3145736 | tf_op jit(solution)/shard_map/ppermute | solution.py:374
  295.0 35.0 %collective-permute-start.30 = (bf16[256,2816]{1,0:T(8,128)(2,1)S(1)}, bf16[256,2816]{1,0:T(8,128)(2,1)S(1)}, u32[]{:S(2)}, u32[]{:S(2)}) collective-permute-start(bf16[256,2816]{1,0:T(8,128)(2,1)S(1)} %collective-permute-done.28), channel_id=1, source_target_pairs={{0,8},{2,10},{4,12},{6,14},{8,16},{10,18},{12,20},{14,22},{16,24},... | collective-permute-start | bytes 4325384 | tf_op jit(solution)/shard_map/ppermute | solution.py:380
  295.2 34.8 %collective-permute-start.31 = (bf16[256,2816]{1,0:T(8,128)(2,1)S(1)}, bf16[256,2816]{1,0:T(8,128)(2,1)S(1)}, u32[]{:S(2)}, u32[]{:S(2)}) collective-permute-start(bf16[256,2816]{1,0:T(8,128)(2,1)S(1)} %collective-permute-done.28), channel_id=1, source_target_pairs={{0,4},{2,6},{4,0},{6,2},{8,12},{10,14},{12,8},{14,10},{16,20},{18,... | collective-permute-start | bytes 4325384 | tf_op jit(solution)/shard_map/ppermute | solution.py:377
  298.6 51.8 %collective-permute-start.23 = (bf16[256,2048]{1,0:T(8,128)(2,1)S(1)}, bf16[256,2048]{1,0:T(8,128)(2,1)S(1)}, u32[]{:S(2)}, u32[]{:S(2)}) collective-permute-start(bf16[256,2048]{1,0:T(8,128)(2,1)S(1)} %multiply_convert_fusion.3), channel_id=1, source_target_pairs={{0,2},{2,0},{4,6},{6,4},{8,10},{10,8},{12,14},{14,12},{16,18},{18,... | collective-permute-start | bytes 3145736 | tf_op jit(solution)/shard_map/ppermute | solution.py:374
  299.8 94.5 %collective-permute-start.22 = (bf16[256,2048]{1,0:T(8,128)(2,1)S(1)}, bf16[256,2048]{1,0:T(8,128)(2,1)S(1)}, u32[]{:S(2)}, u32[]{:S(2)}) collective-permute-start(bf16[256,2048]{1,0:T(8,128)(2,1)S(1)} %multiply_convert_fusion.3), channel_id=1, source_target_pairs={{0,1},{1,0},{2,3},{3,2},{4,5},{5,4},{6,7},{7,6},{8,9},{9,8},{10,11... | collective-permute-start | bytes 3145736 | tf_op jit(solution)/shard_map/ppermute | solution.py:383
  330.8 49.2 %collective-permute-start.32 = (bf16[256,2816]{1,0:T(8,128)(2,1)S(1)}, bf16[256,2816]{1,0:T(8,128)(2,1)S(1)}, u32[]{:S(2)}, u32[]{:S(2)}) collective-permute-start(bf16[256,2816]{1,0:T(8,128)(2,1)S(1)} %collective-permute-done.30), channel_id=1, source_target_pairs={{0,4},{2,6},{4,0},{6,2},{8,12},{10,14},{12,8},{14,10},{16,20},{18,... | collective-permute-start | bytes 4325384 | tf_op jit(solution)/shard_map/ppermute | solution.py:377
  349.1 31.0 %collective-permute-start.36 = (bf16[256,1408]{1,0:T(8,128)(2,1)S(1)}, bf16[256,1408]{1,0:T(8,128)(2,1)S(1)}, u32[]{:S(2)}, u32[]{:S(2)}) collective-permute-start(bf16[256,1408]{1,0:T(8,128)(2,1)S(1)} %collective-permute-done.34), channel_id=1, source_target_pairs={{0,8},{2,10},{4,12},{6,14},{8,16},{10,18},{12,20},{14,22},{16,24},... | collective-permute-start | bytes 2162696 | tf_op jit(solution)/shard_map/ppermute | solution.py:380
  349.6 43.7 %collective-permute-start.37 = (bf16[256,1408]{1,0:T(8,128)(2,1)S(1)}, bf16[256,1408]{1,0:T(8,128)(2,1)S(1)}, u32[]{:S(2)}, u32[]{:S(2)}) collective-permute-start(bf16[256,1408]{1,0:T(8,128)(2,1)S(1)} %collective-permute-done.34), channel_id=1, source_target_pairs={{0,4},{2,6},{4,0},{6,2},{8,12},{10,14},{12,8},{14,10},{16,20},{18,... | collective-permute-start | bytes 2162696 | tf_op jit(solution)/shard_map/ppermute | solution.py:377
  350.4 46.4 %collective-permute-start.24 = (bf16[256,2048]{1,0:T(8,128)(2,1)S(1)}, bf16[256,2048]{1,0:T(8,128)(2,1)S(1)}, u32[]{:S(2)}, u32[]{:S(2)}) collective-permute-start(bf16[256,2048]{1,0:T(8,128)(2,1)S(1)} %collective-permute-done.23), channel_id=1, source_target_pairs={{0,1},{1,0},{2,3},{3,2},{4,5},{5,4},{6,7},{7,6},{8,9},{9,8},{10,11... | collective-permute-start | bytes 3145736 | tf_op jit(solution)/shard_map/ppermute | solution.py:383
  415.9 22.7 %collective-permute-start.46 = (bf16[256,2048]{1,0:T(8,128)(2,1)S(1)}, bf16[256,2048]{1,0:T(8,128)(2,1)S(1)}, u32[]{:S(2)}, u32[]{:S(2)}) collective-permute-start(bf16[256,2048]{1,0:T(8,128)(2,1)S(1)} %get-tuple-element.96), channel_id=1, source_target_pairs={{0,2},{2,0},{4,6},{6,4},{8,10},{10,8},{12,14},{14,12},{16,18},{18,... | collective-permute-start | bytes 3145736 | tf_op jit(solution)/shard_map/ppermute | solution.py:374
  417.6 22.9 %collective-permute-start.40 = (bf16[256,1408]{1,0:T(8,128)(2,1)S(1)}, bf16[256,1408]{1,0:T(8,128)(2,1)S(1)}, u32[]{:S(2)}, u32[]{:S(2)}) collective-permute-start(bf16[256,1408]{1,0:T(8,128)(2,1)S(1)} %copy-done.55), channel_id=1, source_target_pairs={{0,4},{2,6},{4,0},{6,2},{8,12},{10,14},{12,8},{14,10},{16,20},{18,... | collective-permute-start | bytes 2162696 | tf_op jit(solution)/shard_map/ppermute | solution.py:377
  419.0 22.5 %collective-permute-start.45 = (bf16[256,2048]{1,0:T(8,128)(2,1)S(1)}, bf16[256,2048]{1,0:T(8,128)(2,1)S(1)}, u32[]{:S(2)}, u32[]{:S(2)}) collective-permute-start(bf16[256,2048]{1,0:T(8,128)(2,1)S(1)} %get-tuple-element.96), channel_id=1, source_target_pairs={{0,1},{1,0},{2,3},{3,2},{4,5},{5,4},{6,7},{7,6},{8,9},{9,8},{10,11... | collective-permute-start | bytes 3145736 | tf_op jit(solution)/shard_map/ppermute | solution.py:383
  514.0 89.3 %collective-permute-start.98 = (bf16[256,1408]{1,0:T(8,128)(2,1)}, bf16[256,1408]{1,0:T(8,128)(2,1)S(1)}, u32[]{:S(2)}, u32[]{:S(2)}) collective-permute-start(bf16[256,1408]{1,0:T(8,128)(2,1)} %convolution_convert_fusion.1), channel_id=1, source_target_pairs={{0,4},{2,6},{4,0},{6,2},{8,12},{10,14},{12,8},{14,10},{16,20},{18,... | collective-permute-start | bytes 2162696 | tf_op jit(solution)/shard_map/ppermute | solution.py:377
  515.3 33.3 %collective-permute-start.99 = (bf16[256,1408]{1,0:T(8,128)(2,1)}, bf16[256,1408]{1,0:T(8,128)(2,1)S(1)}, u32[]{:S(2)}, u32[]{:S(2)}) collective-permute-start(bf16[256,1408]{1,0:T(8,128)(2,1)} %convolution_convert_fusion), channel_id=1, source_target_pairs={{0,4},{2,6},{4,0},{6,2},{8,12},{10,14},{12,8},{14,10},{16,20},{18,... | collective-permute-start | bytes 2162696 | tf_op jit(solution)/shard_map/ppermute | solution.py:377
  516.1 87.3 %collective-permute-start.90 = (bf16[256,1408]{1,0:T(8,128)(2,1)}, bf16[256,1408]{1,0:T(8,128)(2,1)S(1)}, u32[]{:S(2)}, u32[]{:S(2)}) collective-permute-start(bf16[256,1408]{1,0:T(8,128)(2,1)} %convolution_convert_fusion.5), channel_id=1, source_target_pairs={{0,4},{2,6},{4,0},{6,2},{8,12},{10,14},{12,8},{14,10},{16,20},{18,... | collective-permute-start | bytes 2162696 | tf_op jit(solution)/shard_map/ppermute | solution.py:377
  517.3 62.2 %collective-permute-start.91 = (bf16[256,1408]{1,0:T(8,128)(2,1)}, bf16[256,1408]{1,0:T(8,128)(2,1)S(1)}, u32[]{:S(2)}, u32[]{:S(2)}) collective-permute-start(bf16[256,1408]{1,0:T(8,128)(2,1)} %convolution_convert_fusion.4), channel_id=1, source_target_pairs={{0,4},{2,6},{4,0},{6,2},{8,12},{10,14},{12,8},{14,10},{16,20},{18,... | collective-permute-start | bytes 2162696 | tf_op jit(solution)/shard_map/ppermute | solution.py:377
  518.1 76.5 %collective-permute-start.83 = (bf16[256,1408]{1,0:T(8,128)(2,1)}, bf16[256,1408]{1,0:T(8,128)(2,1)S(1)}, u32[]{:S(2)}, u32[]{:S(2)}) collective-permute-start(bf16[256,1408]{1,0:T(8,128)(2,1)} %convolution_convert_fusion.8), channel_id=1, source_target_pairs={{0,4},{2,6},{4,0},{6,2},{8,12},{10,14},{12,8},{14,10},{16,20},{18,... | collective-permute-start | bytes 2162696 | tf_op jit(solution)/shard_map/ppermute | solution.py:377
  548.6 48.2 %collective-permute-start.42 = (bf16[256,2048]{1,0:T(8,128)(2,1)S(1)}, bf16[256,2048]{1,0:T(8,128)(2,1)S(1)}, u32[]{:S(2)}, u32[]{:S(2)}) collective-permute-start(bf16[256,2048]{1,0:T(8,128)(2,1)S(1)} %get-tuple-element.208), channel_id=1, source_target_pairs={{0,1},{1,0},{2,3},{3,2},{4,5},{5,4},{6,7},{7,6},{8,9},{9,8},{10,11... | collective-permute-start | bytes 3145736 | tf_op jit(solution)/shard_map/ppermute | solution.py:383
  594.6 27.3 %collective-permute-start.82 = (bf16[256,1408]{1,0:T(8,128)(2,1)S(1)}, bf16[256,1408]{1,0:T(8,128)(2,1)S(1)}, u32[]{:S(2)}, u32[]{:S(2)}) collective-permute-start(bf16[256,1408]{1,0:T(8,128)(2,1)S(1)} %convolution_convert_fusion.9), channel_id=1, source_target_pairs={{0,4},{2,6},{4,0},{6,2},{8,12},{10,14},{12,8},{14,10},{16,20},{18,... | collective-permute-start | bytes 2162696 | tf_op jit(solution)/shard_map/ppermute | solution.py:377
  600.2 33.1 %collective-permute-start.92 = (bf16[256,1408]{1,0:T(8,128)(2,1)S(1)}, bf16[256,1408]{1,0:T(8,128)(2,1)S(1)}, u32[]{:S(2)}, u32[]{:S(2)}) collective-permute-start(bf16[256,1408]{1,0:T(8,128)(2,1)S(1)} %fusion.23), channel_id=1, source_target_pairs={{0,8},{2,10},{4,12},{6,14},{8,16},{10,18},{12,20},{14,22},{16,24},... | collective-permute-start | bytes 2162696 | tf_op jit(solution)/shard_map/ppermute | solution.py:380
  603.3 46.5 %collective-permute-start.48 = (bf16[256,2048]{1,0:T(8,128)(2,1)S(1)}, bf16[256,2048]{1,0:T(8,128)(2,1)S(1)}, u32[]{:S(2)}, u32[]{:S(2)}) collective-permute-start(bf16[256,2048]{1,0:T(8,128)(2,1)S(1)} %get-tuple-element.205), channel_id=1, source_target_pairs={{0,1},{1,0},{2,3},{3,2},{4,5},{5,4},{6,7},{7,6},{8,9},{9,8},{10,11... | collective-permute-start | bytes 3145736 | tf_op jit(solution)/shard_map/ppermute | solution.py:383
  603.4 43.7 %collective-permute-start.84 = (bf16[256,1408]{1,0:T(8,128)(2,1)S(1)}, bf16[256,1408]{1,0:T(8,128)(2,1)S(1)}, u32[]{:S(2)}, u32[]{:S(2)}) collective-permute-start(bf16[256,1408]{1,0:T(8,128)(2,1)S(1)} %fusion.22), channel_id=1, source_target_pairs={{0,8},{2,10},{4,12},{6,14},{8,16},{10,18},{12,20},{14,22},{16,24},... | collective-permute-start | bytes 2162696 | tf_op jit(solution)/shard_map/ppermute | solution.py:380
  617.8 33.3 %collective-permute-start.50 = (bf16[256,2048]{1,0:T(8,128)(2,1)S(1)}, bf16[256,2048]{1,0:T(8,128)(2,1)S(1)}, u32[]{:S(2)}, u32[]{:S(2)}) collective-permute-start(bf16[256,2048]{1,0:T(8,128)(2,1)S(1)} %fusion.42), channel_id=1, source_target_pairs={{0,2},{2,0},{4,6},{6,4},{8,10},{10,8},{12,14},{14,12},{16,18},{18,... | collective-permute-start | bytes 3145736 | tf_op jit(solution)/shard_map/ppermute | solution.py:374
  621.9 30.9 %collective-permute-start.41 = (bf16[256,2048]{1,0:T(8,128)(2,1)S(1)}, bf16[256,2048]{1,0:T(8,128)(2,1)S(1)}, u32[]{:S(2)}, u32[]{:S(2)}) collective-permute-start(bf16[256,2048]{1,0:T(8,128)(2,1)S(1)} %get-tuple-element.207), channel_id=1, source_target_pairs={{0,1},{1,0},{2,3},{3,2},{4,5},{5,4},{6,7},{7,6},{8,9},{9,8},{10,11... | collective-permute-start | bytes 3145736 | tf_op jit(solution)/shard_map/ppermute | solution.py:383
  633.2 29.0 %collective-permute-start.43 = (bf16[256,2048]{1,0:T(8,128)(2,1)S(1)}, bf16[256,2048]{1,0:T(8,128)(2,1)S(1)}, u32[]{:S(2)}, u32[]{:S(2)}) collective-permute-start(bf16[256,2048]{1,0:T(8,128)(2,1)S(1)} %fusion.44), channel_id=1, source_target_pairs={{0,2},{2,0},{4,6},{6,4},{8,10},{10,8},{12,14},{14,12},{16,18},{18,... | collective-permute-start | bytes 3145736 | tf_op jit(solution)/shard_map/ppermute | solution.py:374
  647.1 68.5 %collective-permute-start.96 = (bf16[256,1408]{1,0:T(8,128)(2,1)}, bf16[256,1408]{1,0:T(8,128)(2,1)}, u32[]{:S(2)}, u32[]{:S(2)}) collective-permute-start(bf16[256,1408]{1,0:T(8,128)(2,1)} %convolution_convert_fusion.3), channel_id=1, source_target_pairs={{0,4},{2,6},{4,0},{6,2},{8,12},{10,14},{12,8},{14,10},{16,20},{18,... | collective-permute-start | bytes 2162696 | tf_op jit(solution)/shard_map/ppermute | solution.py:377
  649.8 32.1 %collective-permute-start.97 = (bf16[256,1408]{1,0:T(8,128)(2,1)}, bf16[256,1408]{1,0:T(8,128)(2,1)}, u32[]{:S(2)}, u32[]{:S(2)}) collective-permute-start(bf16[256,1408]{1,0:T(8,128)(2,1)} %convolution_convert_fusion.2), channel_id=1, source_target_pairs={{0,4},{2,6},{4,0},{6,2},{8,12},{10,14},{12,8},{14,10},{16,20},{18,... | collective-permute-start | bytes 2162696 | tf_op jit(solution)/shard_map/ppermute | solution.py:377
  651.1 46.3 %collective-permute-start.89 = (bf16[256,1408]{1,0:T(8,128)(2,1)}, bf16[256,1408]{1,0:T(8,128)(2,1)}, u32[]{:S(2)}, u32[]{:S(2)}) collective-permute-start(bf16[256,1408]{1,0:T(8,128)(2,1)} %convolution_convert_fusion.6), channel_id=1, source_target_pairs={{0,4},{2,6},{4,0},{6,2},{8,12},{10,14},{12,8},{14,10},{16,20},{18,... | collective-permute-start | bytes 2162696 | tf_op jit(solution)/shard_map/ppermute | solution.py:377
  652.8 29.9 %collective-permute-start.101 = (bf16[256,1408]{1,0:T(8,128)(2,1)}, bf16[256,1408]{1,0:T(8,128)(2,1)S(1)}, u32[]{:S(2)}, u32[]{:S(2)}) collective-permute-start(bf16[256,1408]{1,0:T(8,128)(2,1)} %fusion.27), channel_id=1, source_target_pairs={{0,8},{2,10},{4,12},{6,14},{8,16},{10,18},{12,20},{14,22},{16,24},... | collective-permute-start | bytes 2162696 | tf_op jit(solution)/shard_map/ppermute | solution.py:380
  663.2 34.9 %collective-permute-start.93 = (bf16[256,1408]{1,0:T(8,128)(2,1)}, bf16[256,1408]{1,0:T(8,128)(2,1)}, u32[]{:S(2)}, u32[]{:S(2)}) collective-permute-start(bf16[256,1408]{1,0:T(8,128)(2,1)} %fusion.29), channel_id=1, source_target_pairs={{0,8},{2,10},{4,12},{6,14},{8,16},{10,18},{12,20},{14,22},{16,24},... | collective-permute-start | bytes 2162696 | tf_op jit(solution)/shard_map/ppermute | solution.py:380
  681.9 30.8 %collective-permute-start.81 = (bf16[256,1408]{1,0:T(8,128)(2,1)}, bf16[256,1408]{1,0:T(8,128)(2,1)S(1)}, u32[]{:S(2)}, u32[]{:S(2)}) collective-permute-start(bf16[256,1408]{1,0:T(8,128)(2,1)} %convolution_convert_fusion.10), channel_id=1, source_target_pairs={{0,4},{2,6},{4,0},{6,2},{8,12},{10,14},{12,8},{14,10},{16,20},{18,... | collective-permute-start | bytes 2162696 | tf_op jit(solution)/shard_map/ppermute | solution.py:377
  682.7 30.8 %collective-permute-start.85 = (bf16[256,1408]{1,0:T(8,128)(2,1)}, bf16[256,1408]{1,0:T(8,128)(2,1)S(1)}, u32[]{:S(2)}, u32[]{:S(2)}) collective-permute-start(bf16[256,1408]{1,0:T(8,128)(2,1)} %fusion.31), channel_id=1, source_target_pairs={{0,8},{2,10},{4,12},{6,14},{8,16},{10,18},{12,20},{14,22},{16,24},... | collective-permute-start | bytes 2162696 | tf_op jit(solution)/shard_map/ppermute | solution.py:380
  697.4 30.8 %collective-permute-start.88 = (bf16[256,1408]{1,0:T(8,128)(2,1)S(1)}, bf16[256,1408]{1,0:T(8,128)(2,1)S(1)}, u32[]{:S(2)}, u32[]{:S(2)}) collective-permute-start(bf16[256,1408]{1,0:T(8,128)(2,1)S(1)} %copy-done.99), channel_id=1, source_target_pairs={{0,4},{2,6},{4,0},{6,2},{8,12},{10,14},{12,8},{14,10},{16,20},{18,... | collective-permute-start | bytes 2162696 | tf_op jit(solution)/shard_map/ppermute | solution.py:377
  712.7 28.4 %collective-permute-start.80 = (bf16[256,1408]{1,0:T(8,128)(2,1)S(1)}, bf16[256,1408]{1,0:T(8,128)(2,1)S(1)}, u32[]{:S(2)}, u32[]{:S(2)}) collective-permute-start(bf16[256,1408]{1,0:T(8,128)(2,1)S(1)} %copy-done.98), channel_id=1, source_target_pairs={{0,4},{2,6},{4,0},{6,2},{8,12},{10,14},{12,8},{14,10},{16,20},{18,... | collective-permute-start | bytes 2162696 | tf_op jit(solution)/shard_map/ppermute | solution.py:377
  713.5 42.6 %collective-permute-start.52 = (bf16[256,2048]{1,0:T(8,128)(2,1)S(1)}, bf16[256,2048]{1,0:T(8,128)(2,1)S(1)}, u32[]{:S(2)}, u32[]{:S(2)}) collective-permute-start(bf16[256,2048]{1,0:T(8,128)(2,1)S(1)} %get-tuple-element.186), channel_id=1, source_target_pairs={{0,2},{2,0},{4,6},{6,4},{8,10},{10,8},{12,14},{14,12},{16,18},{18,... | collective-permute-start | bytes 3145736 | tf_op jit(solution)/shard_map/ppermute | solution.py:374
  715.6 55.0 %collective-permute-start.51 = (bf16[256,2048]{1,0:T(8,128)(2,1)S(1)}, bf16[256,2048]{1,0:T(8,128)(2,1)S(1)}, u32[]{:S(2)}, u32[]{:S(2)}) collective-permute-start(bf16[256,2048]{1,0:T(8,128)(2,1)S(1)} %get-tuple-element.186), channel_id=1, source_target_pairs={{0,1},{1,0},{2,3},{3,2},{4,5},{5,4},{6,7},{7,6},{8,9},{9,8},{10,11... | collective-permute-start | bytes 3145736 | tf_op jit(solution)/shard_map/ppermute | solution.py:383
  728.2 29.1 %collective-permute-start.44 = (bf16[256,2048]{1,0:T(8,128)(2,1)S(1)}, bf16[256,2048]{1,0:T(8,128)(2,1)S(1)}, u32[]{:S(2)}, u32[]{:S(2)}) collective-permute-start(bf16[256,2048]{1,0:T(8,128)(2,1)S(1)} %get-tuple-element.213.mine), channel_id=1, source_target_pairs={{0,1},{1,0},{2,3},{3,2},{4,5},{5,4},{6,7},{7,6},{8,9},{9,8},{10,11... | collective-permute-start | bytes 3145736 | tf_op jit(solution)/shard_map/ppermute | solution.py:383
  780.0 22.5 %collective-permute-start.74 = (bf16[256,512]{1,0:T(8,128)(2,1)}, bf16[256,512]{1,0:T(8,128)(2,1)S(1)}, u32[]{:S(2)}, u32[]{:S(2)}) collective-permute-start(bf16[256,512]{1,0:T(8,128)(2,1)} %convolution_convert_fusion.17), channel_id=1, source_target_pairs={{0,4},{2,6},{4,0},{6,2},{8,12},{10,14},{12,8},{14,10},{16,20},{18,... | collective-permute-start | bytes 786440 | tf_op jit(solution)/shard_map/ppermute | solution.py:377
  792.2 31.0 %all-to-all-start.2 = ((f32[8,32,512]{2,1,0:T(8,128)}), f32[8,32,512]{2,1,0:T(8,128)S(1)}, u32[]{:S(2)}, u32[]{:S(2)}) async-start(f32[8,32,512]{2,1,0:T(8,128)} %bitcast.34), calls=%async_computation.2 | async-start | bytes 1048576 | tf_op jit(solution)/shard_map/all_to_all | solution.py:488
  817.0 22.5 %collective-permute-start.59 = (f32[1,512]{1,0:T(1,128)S(1)}, f32[1,512]{1,0:T(1,128)S(1)}, u32[]{:S(2)}, u32[]{:S(2)}) collective-permute-start(f32[1,512]{1,0:T(1,128)S(1)} %get-tuple-element.105), channel_id=1, source_target_pairs={{0,1},{1,0},{2,3},{3,2},{4,5},{5,4},{6,7},{7,6},{8,9},{9,8},{10,11... | collective-permute-start | bytes 6152 | tf_op jit(solution)/shard_map/ppermute | solution.py:383
  879.4 26.0 %collective-permute-start.67 = (bf16[256,1536]{1,0:T(8,128)(2,1)}, bf16[256,1536]{1,0:T(8,128)(2,1)}, u32[]{:S(2)}, u32[]{:S(2)}) collective-permute-start(bf16[256,1536]{1,0:T(8,128)(2,1)} %convolution_convert_fusion.12), channel_id=1, source_target_pairs={{0,4},{2,6},{4,0},{6,2},{8,12},{10,14},{12,8},{14,10},{16,20},{18,... | collective-permute-start | bytes 2359304 | tf_op jit(solution)/shard_map/ppermute | solution.py:377
  899.1 30.8 %collective-permute-start.66 = (bf16[256,1536]{1,0:T(8,128)(2,1)S(1)}, bf16[256,1536]{1,0:T(8,128)(2,1)S(1)}, u32[]{:S(2)}, u32[]{:S(2)}) collective-permute-start(bf16[256,1536]{1,0:T(8,128)(2,1)S(1)} %convolution_convert_fusion.13), channel_id=1, source_target_pairs={{0,4},{2,6},{4,0},{6,2},{8,12},{10,14},{12,8},{14,10},{16,20},{18,... | collective-permute-start | bytes 2359304 | tf_op jit(solution)/shard_map/ppermute | solution.py:377
  900.6 40.2 %collective-permute-start.65 = (bf16[256,1536]{1,0:T(8,128)(2,1)S(1)}, bf16[256,1536]{1,0:T(8,128)(2,1)S(1)}, u32[]{:S(2)}, u32[]{:S(2)}) collective-permute-start(bf16[256,1536]{1,0:T(8,128)(2,1)S(1)} %convolution_convert_fusion.14), channel_id=1, source_target_pairs={{0,4},{2,6},{4,0},{6,2},{8,12},{10,14},{12,8},{14,10},{16,20},{18,... | collective-permute-start | bytes 2359304 | tf_op jit(solution)/shard_map/ppermute | solution.py:377
  903.1 25.6 %collective-permute-start.56 = (bf16[256,2048]{1,0:T(8,128)(2,1)S(1)}, bf16[256,2048]{1,0:T(8,128)(2,1)S(1)}, u32[]{:S(2)}, u32[]{:S(2)}) collective-permute-start(bf16[256,2048]{1,0:T(8,128)(2,1)S(1)} %fusion.40), channel_id=1, source_target_pairs={{0,2},{2,0},{4,6},{6,4},{8,10},{10,8},{12,14},{14,12},{16,18},{18,... | collective-permute-start | bytes 3145736 | tf_op jit(solution)/shard_map/ppermute | solution.py:374
  933.6 47.2 %collective-permute-start.64 = (bf16[256,1536]{1,0:T(8,128)(2,1)S(1)}, bf16[256,1536]{1,0:T(8,128)(2,1)S(1)}, u32[]{:S(2)}, u32[]{:S(2)}) collective-permute-start(bf16[256,1536]{1,0:T(8,128)(2,1)S(1)} %convolution_convert_fusion.15), channel_id=1, source_target_pairs={{0,4},{2,6},{4,0},{6,2},{8,12},{10,14},{12,8},{14,10},{16,20},{18,... | collective-permute-start | bytes 2359304 | tf_op jit(solution)/shard_map/ppermute | solution.py:377
  953.8 26.9 %collective-permute-start.70 = (bf16[256,1536]{1,0:T(8,128)(2,1)S(1)}, bf16[256,1536]{1,0:T(8,128)(2,1)S(1)}, u32[]{:S(2)}, u32[]{:S(2)}) collective-permute-start(bf16[256,1536]{1,0:T(8,128)(2,1)S(1)} %fusion.26), channel_id=1, source_target_pairs={{0,8},{2,10},{4,12},{6,14},{8,16},{10,18},{12,20},{14,22},{16,24},... | collective-permute-start | bytes 2359304 | tf_op jit(solution)/shard_map/ppermute | solution.py:380
  959.5 39.7 %collective-permute-start.57 = (f32[256,2048]{1,0:T(8,128)S(1)}, f32[256,2048]{1,0:T(8,128)S(1)}, u32[]{:S(2)}, u32[]{:S(2)}) collective-permute-start(f32[256,2048]{1,0:T(8,128)S(1)} %fusion.37.mine), channel_id=1, source_target_pairs={{0,1},{1,0},{2,3},{3,2},{4,5},{5,4},{6,7},{7,6},{8,9},{9,8},{10,11... | collective-permute-start | bytes 6291464 | tf_op jit(solution)/shard_map/ppermute | solution.py:383
  (152 other events, 2342.1 us)

commit v2 on v1

--- a/solution.py
+++ b/solution.py
@@ -4,6 +4,7 @@
 import jax.numpy as jnp
 from jax import lax
 from jax.experimental import pallas as pl
+from jax.experimental.layout import Layout, with_layout_constraint
 from jax.experimental.pallas import tpu as pltpu
 from jax.sharding import PartitionSpec as P
 
@@ -85,8 +86,30 @@
 
     @pl.when(step == count - 1)
     def _():
-        out_ref[:, :DV] = state[...]
-        out_ref[:, DV:] = jnp.exp(total[...]) * info[1 + 3 * count].astype(FULL)
+        out_ref[:, :DV] = state[...].astype(LOW)
+        lane = lax.broadcasted_iota(jnp.int32, (DK, LANES), 1)
+        high, middle, low = thirds(jnp.exp(total[...]) * info[1 + 3 * count].astype(FULL))
+        high, middle, low = high.astype(FULL), middle.astype(FULL), low.astype(FULL)
+        out_ref[:, DV:] = jnp.where(lane == 0, high, jnp.where(lane == 1, middle, low)).astype(LOW)
+
+
+def chain_kernel(backwards, pieces_ref, local_ref, out_ref):
+    groups, slab = local_ref.shape[0], local_ref.shape[1]
+    current = jnp.zeros((slab, DV), FULL)
+    for j in reversed(range(groups)) if backwards else range(groups):
+        out_ref[j] = current.astype(LOW)
+        through = pieces_ref[j][:, DV:].astype(FULL)
+        through = through[:, 0:1] + through[:, 1:2] + through[:, 2:3]
+        current = through * current + local_ref[j][:, :DV].astype(FULL)
+
+
+def chain_call(pieces, local, backwards):
+    groups, slab, _ = pieces.shape
+    return pl.pallas_call(
+        functools.partial(chain_kernel, backwards),
+        out_shape=shape_of(groups, slab, DV, dtype=LOW),
+        compiler_params=pltpu.CompilerParams(vmem_limit_bytes=40 * 1024 * 1024),
+    )(pieces, local)
 
 
 def mix_kernel(
@@ -96,7 +119,7 @@
 
     @pl.when(step == 0)
     def _():
-        state[...] = enter_ref[...]
+        state[...] = enter_ref[...].astype(FULL)
 
     begin = jnp.where(info[1 + step] > 0, jnp.zeros_like(state), state[...])
     states_ref[0] = begin
@@ -146,7 +169,7 @@
 
     @pl.when(step == count - 1)
     def _():
-        out_ref[...] = state[...]
+        out_ref[...] = state[...].astype(LOW)
 
 
 def mix_back_kernel(
@@ -158,7 +181,6 @@
     logits_ref,
     states_ref,
     dmixed_ref,
-    gate_ref,
     leave_ref,
     back_ref,
     dlogits_ref,
@@ -170,7 +192,7 @@
 
     @pl.when(step == 0)
     def _():
-        state[...] = leave_ref[...]
+        state[...] = leave_ref[...].astype(FULL)
         dbias_ref[...] = jnp.zeros_like(dbias_ref)
 
     after, begin = state[...], states_ref[0]
@@ -199,10 +221,9 @@
     dlogits = ddecay * jax.nn.sigmoid(-logits_ref[...]) * (1.0 / 16.0)
     dlogits_ref[...] = dlogits
     dbias_ref[...] += jnp.sum(dlogits, axis=0, keepdims=True)
-    back_ref[:, :DK] = (dq * DK ** (-0.5)).astype(LOW)
-    back_ref[:, DK : 2 * DK] = dk.astype(LOW)
-    back_ref[:, 2 * DK : 2 * DK + DV] = dv.astype(LOW)
-    back_ref[:, 2 * DK + DV :] = gate_ref[...]
+    back_ref[:, :DV] = dv.astype(LOW)
+    back_ref[:, DV : DV + DK] = dk.astype(LOW)
+    back_ref[:, DV + DK :] = (dq * DK ** (-0.5)).astype(LOW)
     before = widen(jnp.exp(column_sum(decay)), DV) * after + fine(halves(q * from_start), dout, TN)
     state[...] = jnp.where(info[1 + at] > 0, jnp.zeros_like(before), before)
 
@@ -210,9 +231,10 @@
 PARAMS = pltpu.CompilerParams(
     dimension_semantics=("arbitrary",), vmem_limit_bytes=40 * 1024 * 1024
 )
-
-
-def token_call(kernel, info, count, quarter, reverse, inputs, outputs, scratch, flops):
+QUICK = pl.CostEstimate(flops=1, bytes_accessed=1, transcendentals=0)
+
+
+def token_call(kernel, info, count, quarter, reverse, inputs, outputs, scratch):
     per = quarter // BLOCK
 
     def place(i):
@@ -241,12 +263,159 @@
         ),
         out_shape=[out for out, _, _ in outputs],
         compiler_params=PARAMS,
-        cost_estimate=pl.CostEstimate(flops=flops, bytes_accessed=1 << 24, transcendentals=1 << 20),
+        cost_estimate=QUICK,
     )(info, *[array for array, _, _ in inputs])
 
 
 def shape_of(*extent, dtype=FULL):
     return jax.ShapeDtypeStruct(extent, dtype)
+
+
+def fill(piece_refs, places, weight_refs, spans):
+    for (piece, source, target, size), (start, stop), weight in (
+        (place, span, weight) for place in places for span, weight in zip(spans, weight_refs)
+    ):
+        weight[target : target + size, :] = piece_refs[piece][source : source + size, start:stop]
+
+
+def assemble_kernel(places, spans, dotted, x_ref, *refs):
+    number = 1 + max(p[0] for p in places)
+    pieces, y_ref, weights = refs[:number], refs[number], refs[number + 1 :]
+
+    @pl.when(pl.program_id(0) == 0)
+    def _():
+        fill(pieces, places, weights, spans)
+
+    for i in range(dotted):
+        start, stop = spans[i]
+        y_ref[:, start:stop] = dot(x_ref[...], weights[i][...])
+
+
+def assemble_back_kernel(places, x_ref, pre_ref, *refs):
+    number = 1 + max(p[0] for p in places)
+    pieces, back_ref, weight = refs[:number], refs[number], refs[number + 1]
+    ff = weight.shape[1]
+
+    @pl.when(pl.program_id(0) == 0)
+    def _():
+        fill(pieces, places, [weight], [(0, ff)])
+
+    grad = dot(x_ref[...], weight[...])
+    pre, up = pre_ref[:, :ff], pre_ref[:, ff:]
+    soft = jax.nn.sigmoid(pre)
+    back_ref[:, :ff] = (grad * up * (soft * (1.0 + pre * (1.0 - soft)))).astype(LOW)
+    back_ref[:, ff:] = (grad * (pre * soft)).astype(LOW)
+
+
+def assemble_gate_kernel(places, x_ref, *refs):
+    number = 1 + max(p[0] for p in places)
+    pieces, pre_ref, weight, inner_ref = refs[:number], *refs[number:]
+    ff = weight.shape[1] // 2
+
+    @pl.when(pl.program_id(0) == 0)
+    def _():
+        fill(pieces, places, [weight], [(0, 2 * ff)])
+
+    pre_ref[...] = dot(x_ref[...], weight[...])
+    gate = pre_ref[:, :ff]
+    inner_ref[...] = (gate * jax.nn.sigmoid(gate) * pre_ref[:, ff:]).astype(LOW)
+
+
+def product_kernel(number, *refs):
+    kept_ref, sent_ref = refs[2 * number :]
+    total = 0.0
+    for x_ref, w_ref in zip(refs[:number], refs[number : 2 * number]):
+        total = total + dot(x_ref[...], w_ref[...], NT)
+    half = kept_ref.shape[0]
+    kept_ref[...] = total[:half]
+    sent_ref[...] = total[half:].astype(LOW)
+
+
+def product_call(pairs, block, half):
+    tile = 512
+    width = pairs[0][1].shape[0]
+    out = pl.BlockSpec((half, tile), lambda i: (0, i))
+    return pl.pallas_call(
+        functools.partial(product_kernel, len(pairs)),
+        grid=(width // tile,),
+        in_specs=[
+            pl.BlockSpec((2 * half, x.shape[1]), lambda i: (block, 0), pipeline_mode=pl.Buffered(1))
+            for x, _ in pairs
+        ]
+        + [pl.BlockSpec((tile, w.shape[1]), lambda i: (i, 0)) for _, w in pairs],
+        out_specs=[out, out],
+        out_shape=[shape_of(half, width), shape_of(half, width, dtype=LOW)],
+        compiler_params=PARAMS,
+        cost_estimate=QUICK,
+    )(*[x for x, _ in pairs], *[w for _, w in pairs])
+
+
+def parts_kernel(number, targets, wide, table, *refs):
+    outs = refs[2 * number :]
+    values = [dot(l[...], r[...], TN) for l, r in zip(refs[:number], refs[number : 2 * number])]
+    for step, (target, row) in enumerate(targets):
+
+        @pl.when(pl.program_id(0) == step)
+        def _():
+            start = 0
+            for value in values:
+                stop = start + value.shape[1]
+                outs[target][row * wide : (row + 1) * wide, start:stop] = value.astype(outs[target].dtype)
+                start = stop
+
+
+def parts_call(pairs, groups, wide, dtype):
+    columns = sum(r.shape[1] for _, r in pairs)
+    if wide % LANES:
+        def part(k):
+            cut = slice(k * wide, (k + 1) * wide)
+            return jnp.concatenate([dot(l[:, cut], r, TN) for l, r in pairs], axis=1)
+
+        return [jnp.concatenate([part(k) for k in group], axis=0).astype(dtype) for group in groups]
+    flat = [(j, i, k) for j, group in enumerate(groups) for i, k in enumerate(group)]
+
+    def fixed(shape):
+        return pl.BlockSpec(shape, lambda i, table: (0, 0), pipeline_mode=pl.Buffered(1))
+
+    return pl.pallas_call(
+        functools.partial(parts_kernel, len(pairs), [(j, i) for j, i, _ in flat], wide),
+        grid_spec=pltpu.PrefetchScalarGridSpec(
+            num_scalar_prefetch=1,
+            grid=(len(flat),),
+            in_specs=[pl.BlockSpec((l.shape[0], wide), lambda i, table: (0, table[i])) for l, _ in pairs]
+            + [fixed(r.shape) for _, r in pairs],
+            out_specs=[fixed((len(g) * wide, columns)) for g in groups],
+        ),
+        out_shape=[shape_of(len(g) * wide, columns, dtype=dtype) for g in groups],
+        compiler_params=PARAMS,
+        cost_estimate=QUICK,
+    )(jnp.asarray([k for _, _, k in flat], jnp.int32), *[l for l, _ in pairs], *[r for _, r in pairs])
+
+
+def once(shape):
+    return pl.BlockSpec(shape, lambda i: (0, 0), pipeline_mode=pl.Buffered(1))
+
+
+def assemble_call(kernel, x, extra, pieces, out_width, out_dtype, spans, depth, also=None):
+    tile = 256
+    rows = lambda width: pl.BlockSpec((tile, width), lambda i: (i, 0))
+    return pl.pallas_call(
+        kernel,
+        grid=(x.shape[0] // tile,),
+        in_specs=[rows(x.shape[1])]
+        + [rows(e.shape[1]) for e in extra]
+        + [once(p.shape) for p in pieces],
+        out_specs=[rows(out_width)]
+        + [once((depth, stop - start)) for start, stop in spans]
+        + ([rows(also)] if also else []),
+        out_shape=[shape_of(x.shape[0], out_width, dtype=out_dtype)]
+        + [shape_of(depth, stop - start, dtype=LOW) for start, stop in spans]
+        + ([shape_of(x.shape[0], also, dtype=LOW)] if also else []),
+        compiler_params=pltpu.CompilerParams(
+            dimension_semantics=("arbitrary",), vmem_limit_bytes=52 * 1024 * 1024
+        ),
+        cost_estimate=QUICK,
+    )(x, *extra, *pieces)
 
 
 def columns_in_kernel(order, core, a, b, c, d, oa, ob, oc, od):
@@ -404,69 +573,215 @@
         high = jnp.concatenate([a[:, m:] for a, m in zip(arrays, mid)], axis=1)
         return jnp.where(left, low, high), jnp.where(left, high, low)
 
-    def exchanged(mine, other):
-        got = pair(other)
+    def turned_over(x):
+        return with_layout_constraint(x.T, Layout((0, 1)))
+
+    def joined(mine, got):
         return jnp.concatenate(
             [jnp.where(left, mine, got), jnp.where(left, got, mine)], axis=0
         )
 
-    def collected(own, after):
-        if after is not None:
-            own, _ = tied(own, after)
-        blocks, others = [own], []
-        for step in range(laps):
-            if step < laps - 1:
-                new, other = tied(ring(blocks[-1]), side(blocks[-1]))
-                blocks.append(new)
-                others.append(other)
+    class Gather:
+        def __init__(self, own):
+            self.blocks, self.others = [own], []
+
+        def ring(self):
+            if len(self.blocks) < laps:
+                self.blocks.append(ring(self.blocks[-1]))
+
+        def side(self, number=1):
+            for _ in range(number):
+                if len(self.others) < min(laps, len(self.blocks)):
+                    self.others.append(side(self.blocks[len(self.others)]))
+
+        def rest(self):
+            while len(self.blocks) < laps:
+                self.ring()
+
+        def pieces(self):
+            arrays = self.blocks + self.others
+            return arrays, [(i, 0, i * wide, wide) for i in range(len(arrays))]
+
+    class GatherSide(Gather):
+        def begin(self):
+            self.got = side(self.blocks[0])
+
+        def join(self):
+            self.blocks = [jnp.concatenate([self.blocks[0], self.got], axis=0)]
+
+        def pieces(self):
+            places = [(i, 0, i * wide, wide) for i in range(laps)]
+            places += [(i, wide, (laps + i) * wide, wide) for i in range(laps)]
+            return self.blocks, places
+
+    class Reduce:
+        def __init__(self, *pairs):
+            self.pairs = pairs
+            self.turn = [(p + 1) % laps for p in range(laps)]
+            self.parts, self.owns, self.sent, self.flown = [], [], [], None
+            self.done = 0
+
+        def make(self):
+            self.parts = list(parts_call(self.pairs, [[laps + p] for p in self.turn], wide, LOW))
+
+        def make_own(self):
+            self.owns = list(parts_call(self.pairs, [[p] for p in self.turn], wide, FULL))
+
+        def send(self, number=1):
+            for _ in range(number):
+                if len(self.sent) < laps:
+                    self.sent.append(side(self.parts[len(self.sent)]))
+
+        def add(self):
+            while len(self.sent) <= self.done:
+                self.send()
+            value = self.owns[self.done] + self.sent[self.done]
+            if self.flown is not None:
+                value = value + self.flown
+            self.done += 1
+            return value
+
+        def hop(self):
+            if self.done < laps - 1:
+                self.flown = ring(self.add().astype(LOW))
+
+        def last(self):
+            while self.done < laps - 1:
+                self.hop()
+            self.total = self.add()
+
+        def halve(self):
+            total = self.total
+            top, low = total[: wide // 2], total[wide // 2 :]
+            self.mine = jnp.where(left, top, low)
+            self.got = pair(jnp.where(left, low, top).astype(LOW))
+
+        def out(self):
+            got = self.got.astype(FULL)
+            return jnp.where(left, self.mine, got), jnp.where(left, got, self.mine)
+
+    class ReduceSide(Reduce):
+        def make(self):
+            p = self.turn[0]
+            (self.value,) = parts_call(self.pairs, [[p, laps + p]], wide, LOW)
+
+        def make_own(self):
+            self.owns = [None] + list(
+                parts_call(self.pairs, [[p, laps + p] for p in self.turn[1:]], wide, FULL)
+            )
+
+        def fly(self):
+            self.done = 1
+            self.flown = ring(self.value)
+
+        def add(self):
+            value = self.owns[self.done] + self.flown
+            self.done += 1
+            return value
+
+        def cross(self):
+            while self.done < laps - 1:
+                self.hop()
+            total = self.add()
+            self.kept = total[:wide]
+            self.come = side(total[wide:].astype(LOW))
+
+        def last(self):
+            self.total = self.kept + self.come
+
+    def together(*things):
+        def read(holder, key):
+            return holder[key] if isinstance(key, int) else getattr(holder, key)
+
+        values = [read(*t) if isinstance(t, tuple) else t for t in things]
+        values = lax.optimization_barrier(values)
+        back = []
+        for thing, value in zip(things, values):
+            if not isinstance(thing, tuple):
+                back.append(value)
+            elif isinstance(thing[1], int):
+                thing[0][thing[1]] = value
             else:
-                others.append(side(blocks[-1]))
-        return jnp.concatenate(blocks + others, axis=0), blocks[-1]
-
-    mine_q, other_q = split(w_query, w_key, w_value, w_gate_out)
-    mine_o, other_o = split(w_out.T)
-    mine_f, other_f = split(w_ff_gate, w_ff_up)
-    mine_d, other_d = split(w_ff_down.T)
-    pair_q = exchanged(mine_q, other_q)
-
+                setattr(*thing, value)
+        return back[0] if len(back) == 1 else back
+
+    def spread_near(x):
+        return pair(x), twin(x)
+
+    def spread_all(x, far, near, other):
+        return jnp.concatenate([x, near, far, other], axis=0)
+
+    q2 = 2 * quarter
+
+    def far_part(*pairs):
+        return list(product_call(pairs, 1, quarter))
+
+    def near_part(*pairs):
+        return list(product_call(pairs, 0, quarter))
+
+    def summed_pair(kept, sent):
+        return kept + twin(sent)
+
+    mine, other = split(w_value, w_key)
+    got = pair(other)
     hidden_low, cot_own, gain_attn, gain_mlp = columns_in(
         hidden_in, cotangent, norm_attn[None], norm_mlp[None], order, core, quarter, wide
     )
+    hidden = hidden_low.astype(FULL)
+    scale_attn = lax.rsqrt(jnp.mean(hidden * hidden, axis=1, keepdims=True) + EPSILON)
+    first_own = (hidden * scale_attn * gain_attn).astype(LOW)
+    got, first_own, cot_own, w_rank_in, w_gate_out, w_query, w_out = together(
+        got, first_own, cot_own, w_rank_in, w_gate_out, w_query, w_out
+    )
+    keys = Gather(joined(mine, got))
+    keys.ring()
+    keys.side()
+    far, near = spread_near(first_own)
+    mine, other = split(w_gate_out, w_query, turned_over(w_out))
+    mine, other, w_ff_gate, w_ff_up, w_ff_down, w_rank_in = together(
+        mine, other, (keys.blocks, 1), w_ff_gate, w_ff_up, w_ff_down, w_rank_in
+    )
+    keys.ring()
+    keys.side()
+    got = pair(other)
+    mine_b, other_b = split(w_ff_gate, w_ff_up, turned_over(w_ff_down))
     rank_weight = jnp.concatenate(
         [lax.dynamic_slice_in_dim(w_rank_in, order[i] * wide, wide, 0) for i in range(groups)], axis=0
     )
-
-    def spread(x):
-        near, far = twin(x), pair(x)
-        return jnp.concatenate([x, near, far, twin(far)], axis=0)
-
-    def gathered_sum(parts):
-        q = quarter
-        far = parts[2 * q : 3 * q] + twin(parts[3 * q :].astype(LOW))
-        got = pair(far.astype(LOW))
-        return parts[:q] + twin(parts[q : 2 * q].astype(LOW)) + got
-
-    hidden = hidden_low.astype(FULL)
-    scale_attn = lax.rsqrt(jnp.mean(hidden * hidden, axis=1, keepdims=True) + EPSILON)
-    first = spread((hidden * scale_attn * gain_attn).astype(LOW))
-
-    full_q, done = collected(pair_q, None)
-    other_o, other_f, other_d, _ = tied(other_o, other_f, other_d, first)
-    pair_o, pair_f, pair_d = (
-        exchanged(mine_o, other_o),
-        exchanged(mine_f, other_f),
-        exchanged(mine_d, other_d),
-    )
-    full_o, done = collected(pair_o, done)
-    full_f, done = collected(pair_f, done)
-    full_d, done = collected(pair_d, done)
-
-    mixes = dot(first, full_q)
+    far, near, mine_b, other_b, rank_weight = together(
+        (keys.blocks, 2), (keys.others, 0), far, near, mine_b, other_b, rank_weight
+    )
+    keys.rest()
+    keys.side()
+    other = twin(far)
+    got_b = pair(other_b)
+    first = spread_all(first_own, far, near, other)
+    first, got = together((keys.blocks, laps - 1), (keys.others, 1), first, got)
+    keys.side(laps)
+    gates = Gather(joined(mine, got))
+    gates.ring()
     rank_in = dot(first, rank_weight).astype(LOW)
     rank_out = jnp.where(left, w_rank_out[:, :DK], w_rank_out[:, DK:])
     bias = jnp.where(left, decay_bias[:DK], decay_bias[DK:])
     logits = dot(rank_in, rank_out) + bias
     decay = jax.nn.log_sigmoid(logits) / 16.0
+    first, rank_in, decay, logits = together(
+        *[(keys.others, i) for i in range(2, laps)],
+        (gates.blocks, 0),
+        (gates.blocks, 1),
+        first,
+        rank_in,
+        decay,
+        logits,
+
+    )
+    gates.ring()
+    gates.side()
+    arrays, places = keys.pieces()
+    span = [(0, DV + DK)]
+    keyed, full_k = assemble_call(
+        functools.partial(assemble_kernel, places, span, 1), first, [], arrays, DV + DK, FULL, span, width
+    )
     gain = head_gain[None]
     state_scratch = pltpu.VMEM((DK, DV), FULL)
     row_scratch = pltpu.VMEM((8, DK), FULL)
@@ -476,11 +791,13 @@
     (summary,) = call(
         summary_kernel,
         reverse=True,
-        inputs=[(mixes, key_block, 1), (mixes, val_block, 1), (decay, key_block, 0)],
-        outputs=[(shape_of(DK, DV + LANES), (DK, DV + LANES), None)],
+        inputs=[(keyed, key_block, 2), (keyed, val_block, 0), (decay, key_block, 0)],
+        outputs=[(shape_of(DK, DV + LANES, dtype=LOW), (DK, DV + LANES), None)],
         scratch=[state_scratch, row_scratch, pltpu.VMEM((DK, LANES), FULL)],
-        flops=1 << 30,
-    )
+    )
+    summary, got_b = together((gates.blocks, 2), (gates.others, 0), summary, got_b)
+    gates.rest()
+    gates.side()
     halves_of_seq = [[i for i in range(peers) if i % 2 == k] for k in range(2)]
     slab = DK // groups
 
@@ -488,24 +805,50 @@
         return lax.all_to_all(x, "seq", 0, 0, axis_index_groups=halves_of_seq, tiled=True)
 
     pieces = turned(summary).reshape(groups, slab, DV + LANES)
-    through = pieces[:, :, DV : DV + 1]
-
-    def carried(local, backwards):
-        current, out = jnp.zeros((slab, DV), FULL), [None] * groups
-        for j in reversed(range(groups)) if backwards else range(groups):
-            out[j] = current
-            current = through[j] * current + local[j]
-        return turned(jnp.concatenate(out, axis=0))
-
-    entering = carried(pieces[:, :, :DV], False)
+    pair_b = joined(mine_b, got_b)
+    ffs = Gather(pair_b[:, : 2 * ff])
+    downs = GatherSide(pair_b[:, 2 * ff :])
+    downs.begin()
+    cot_far, cot_near = spread_near(cot_own)
+    pieces, ffs.blocks[0], cot_far, cot_near = together(
+        (gates.blocks, laps - 1),
+        (gates.others, 1),
+        (downs, "got"),
+        pieces,
+        ffs.blocks[0],
+        cot_far,
+        cot_near,
+    )
+    gates.side(laps)
+    downs.join()
+    ffs.ring()
+    cot_other = twin(cot_far)
+    entering = turned(chain_call(pieces, pieces, False).reshape(DK, DV))
+    entering, keyed, first, cot_other, downs.blocks[0] = together(
+        *[(gates.others, i) for i in range(2, laps)],
+        (ffs.blocks, 1),
+        entering,
+        keyed,
+        first,
+        cot_other,
+        downs.blocks[0],
+    )
+    ffs.ring()
+    ffs.side()
+    cot = spread_all(cot_own, cot_far, cot_near, cot_other)
+    arrays, places = gates.pieces()
+    span = [(0, DV), (DV, DV + DK), (DV + DK, 2 * DV + DK)]
+    gated_in, full_g, full_q, full_o = assemble_call(
+        functools.partial(assemble_kernel, places, span, 2), first, [], arrays, DV + DK, FULL, span, width
+    )
     mixed, gated, states = call(
         mix_kernel,
         reverse=False,
         inputs=[
-            (mixes, key_block, 0),
-            (mixes, key_block, 1),
-            (mixes, val_block, 1),
-            (mixes, val_block, 2),
+            (gated_in, key_block, 2),
+            (keyed, key_block, 2),
+            (keyed, val_block, 0),
+            (gated_in, val_block, 0),
             (decay, key_block, 0),
             (entering, state_shape, None),
             (gain, (1, DV), None),
@@ -516,44 +859,78 @@
             (shape_of(count, DK, DV), (1, DK, DV), "state"),
         ],
         scratch=[state_scratch],
-        flops=3 << 30,
-    )
-    resid = hidden + gathered_sum(dot(gated, full_o, NT))
+    )
+
+    gated, cot = together((ffs.blocks, 2), (ffs.others, 0), gated, cot)
+    far, gated = together(summed_pair(*far_part((gated, full_o))).astype(LOW), gated)
+    ffs.rest()
+    ffs.side()
+    got = pair(far)
+    near = near_part((gated, full_o))
+    got, near = together((ffs.blocks, laps - 1), (ffs.others, 1), got, near)
+    resid = hidden + (summed_pair(*near) + got)
     scale_mlp = lax.rsqrt(jnp.mean(resid * resid, axis=1, keepdims=True) + EPSILON)
-    second = spread((resid * scale_mlp * gain_mlp).astype(LOW))
-    ff_both = dot(second, full_f)
-    ff_pre, up_pre = ff_both[:, :ff], ff_both[:, ff:]
-    inner = (silu(ff_pre) * up_pre).astype(LOW)
-    cot_own, _ = tied(cot_own, done)
-    cot = spread(cot_own)
-
-    def reduced(tokens_left, tokens_right):
-        def part(k):
-            return dot(tokens_left[:, k * wide : (k + 1) * wide], tokens_right, TN)
-
-        turn = [(p + 1) % laps for p in range(laps)]
-        sent = {p: side(part(laps + p).astype(LOW)) for p in turn}
-        own = {p: part(p) + sent[p] for p in turn}
-        current = own[turn[0]]
-        for p in turn[1:]:
-            current = own[p] + ring(current.astype(LOW))
-        high, low = current[: wide // 2], current[wide // 2 :]
-        mine = jnp.where(left, high, low)
-        got = pair(jnp.where(left, low, high).astype(LOW)).astype(FULL)
-        return jnp.where(left, mine, got), jnp.where(left, got, mine)
-
-    down_halves = reduced(cot, inner)
-    out_own = (resid + gathered_sum(dot(inner, full_d, NT))).astype(LOW)
-    block_out = columns_out(out_own, twin(out_own), order, inverse, core, wide)
-
-    grad_inner = dot(cot, full_d)
-    soft = jax.nn.sigmoid(ff_pre)
-    ff_back = (grad_inner * up_pre * (soft * (1.0 + ff_pre * (1.0 - soft)))).astype(LOW)
-    up_back = (grad_inner * (ff_pre * soft)).astype(LOW)
-    both_back = jnp.concatenate([ff_back, up_back], axis=1)
-    grad_second = gathered_sum(dot(both_back, full_f, NT))
-    gate_halves = reduced(second, both_back[:, :ff])
-    up_halves = reduced(second, both_back[:, ff:])
+    second_own = together((resid * scale_mlp * gain_mlp).astype(LOW))
+    ffs.side()
+    downs.ring()
+    far, near = spread_near(second_own)
+    far, near, second_own = together(
+        (ffs.others, 2), (downs.blocks, 1), far, near, second_own
+    )
+    ffs.side(laps)
+    downs.ring()
+    other = twin(far)
+    second = spread_all(second_own, far, near, other)
+    second, cot = together(*[(ffs.others, i) for i in range(3, laps)], (downs.blocks, 2), second, cot)
+    downs.rest()
+    arrays, places = ffs.pieces()
+    span = [(0, 2 * ff)]
+    ff_both, full_f, inner = assemble_call(
+        functools.partial(assemble_gate_kernel, places), second, [], arrays, 2 * ff, FULL, span, width, ff
+    )
+    down_grad = ReduceSide((cot, inner))
+    down_grad.make()
+    inner, ff_both, cot, second = together(
+        (downs.blocks, laps - 1), (down_grad, "value"), inner, ff_both, cot, second
+    )
+    down_grad.fly()
+    down_grad.pairs = ((cot, inner),)
+    arrays, places = downs.pieces()
+    both_back, full_d = assemble_call(
+        functools.partial(assemble_back_kernel, places), cot, [ff_both], arrays, 2 * ff, LOW, [(0, ff)], width
+    )
+
+    gate_grad = Reduce((second, both_back[:, :ff]))
+    gate_grad.make()
+    far = far_part((both_back, full_f))
+    far, both_back, second, full_d, full_f, inner, cot = together(
+        (down_grad, "flown"), (gate_grad, "parts"), far, both_back, second, full_d, full_f, inner, cot
+    )
+    far, both_back, second, full_f, inner, cot, down_grad.flown = together(
+        summed_pair(*far).astype(LOW), both_back, second, full_f, inner, cot, down_grad.flown
+    )
+    down_grad.pairs = ((cot, inner),)
+    gate_grad.pairs = ((second, both_back[:, :ff]),)
+    got = pair(far)
+    gate_grad.send(2)
+    down_grad.make_own()
+    down_grad.hop()
+    near = near_part((both_back, full_f))
+    up_grad = Reduce((second, both_back[:, ff:]))
+    up_grad.make()
+    got, near, both_back, second = together(
+        (down_grad, "flown"),
+        (down_grad, "owns"),
+        (up_grad, "parts"),
+        (gate_grad.sent, 0),
+        (gate_grad.sent, 1),
+        got,
+        near,
+        both_back,
+        second,
+    )
+    gate_grad.pairs = ((second, both_back[:, :ff]),)
+    up_grad.pairs = ((second, both_back[:, ff:]),)
 
     def norm_back(grad, value, scale, gains):
         normed = value * scale
@@ -561,16 +938,34 @@
         gain_grad = jnp.sum(grad * normed, axis=0, keepdims=True)
         return scale * (scaled - normed * jnp.mean(scaled * normed, axis=1, keepdims=True)), gain_grad
 
-    resid_norm, grad_gain_mlp = norm_back(grad_second, resid, scale_mlp, gain_mlp)
+    resid_norm, grad_gain_mlp = norm_back(summed_pair(*near) + got, resid, scale_mlp, gain_mlp)
     grad_resid = cot_own.astype(FULL) + resid_norm
-    resid_back = spread(grad_resid.astype(LOW))
+    back_own, both_back, second, down_grad.owns, down_grad.flown = together(
+        grad_resid.astype(LOW), both_back, second, down_grad.owns, down_grad.flown
+    )
+    gate_grad.pairs = ((second, both_back[:, :ff]),)
+    up_grad.pairs = ((second, both_back[:, ff:]),)
+    far, near = spread_near(back_own)
+    gate_grad.send(laps)
+    down_grad.hop()
+    gate_grad.make_own()
+    up_grad.make_own()
+    far, near, back_own = together(
+        (gate_grad, "owns"), (up_grad, "owns"), (gate_grad.sent, 2), far, near, back_own
+    )
+    other = twin(far)
+    resid_back, full_d, inner, full_o, gate_grad.sent[0] = together(
+        spread_all(back_own, far, near, other), full_d, inner, full_o, gate_grad.sent[0]
+    )
+    up_grad.send()
+    gate_grad.hop()
     grad_gated = dot(resid_back, full_o)
     gate_back, dmixed, summary_back, grad_gain_head = call(
         gate_back_kernel,
         reverse=False,
         inputs=[
-            (mixes, key_block, 0),
-            (mixes, val_block, 2),
+            (gated_in, key_block, 2),
+            (gated_in, val_block, 0),
             (decay, key_block, 0),
             (mixed, val_block, 0),
             (grad_gated, val_block, 0),
@@ -579,54 +974,160 @@
         outputs=[
             (shape_of(tokens, DV, dtype=LOW), val_block, 0),
             (shape_of(tokens, DV), val_block, 0),
-            (shape_of(DK, DV), state_shape, None),
+            (shape_of(DK, DV, dtype=LOW), state_shape, None),
             (shape_of(1, DV), (1, DV), None),
         ],
         scratch=[state_scratch, row_scratch],
-        flops=1 << 30,
-    )
-    out_halves = reduced(resid_back, gated)
-    leaving = carried(turned(summary_back).reshape(groups, slab, DV), True)
+    )
+    summary_back, resid_back, gate_back, first, gated = together(
+        (up_grad.sent, 0),
+        (down_grad, "flown"),
+        *[(gate_grad.sent, i) for i in range(3, laps)],
+        (gate_grad, "flown"),
+        summary_back,
+        resid_back,
+        gate_back,
+        first,
+        gated,
+    )
+    up_grad.send()
+    gate_grad.hop()
+    pieces_back = turned(summary_back).reshape(groups, slab, DV)
+    out_grad = Reduce((resid_back, gated), (first, gate_back))
+    out_grad.make()
+    pieces_back, full_d, inner, resid_back, gate_back, first, gated = together(
+        (up_grad.sent, 1),
+        (gate_grad, "flown"),
+        (out_grad, "parts"),
+        pieces_back,
+        full_d,
+        inner,
+        resid_back,
+        gate_back,
+        first,
+        gated,
+    )
+    leaving, gate_grad.flown, up_grad.sent[0] = together(
+        chain_call(pieces, pieces_back, True), gate_grad.flown, up_grad.sent[0]
+    )
+    out_grad.pairs = ((resid_back, gated), (first, gate_back))
+    up_grad.send(laps)
+    gate_grad.hop()
+    up_grad.hop()
+    leaving = turned(leaving.reshape(DK, DV))
+    out_far, out_near = far_part((inner, full_d)), near_part((inner, full_d))
+    leaving, keyed, out_far, out_near = together(
+        (gate_grad, "flown"),
+        (up_grad, "flown"),
+        *[(up_grad.sent, i) for i in range(2, laps)],
+        leaving,
+        keyed,
+        out_far,
+        out_near,
+    )
+    down_grad.cross()
+    out_grad.send()
+    up_grad.hop()
     mixes_back, grad_logits, grad_bias = call(
         mix_back_kernel,
         reverse=True,
         inputs=[
-            (mixes, key_block, 0),
-            (mixes, key_block, 1),
-            (mixes, val_block, 1),
+            (gated_in, key_block, 2),
+            (keyed, key_block, 2),
+            (keyed, val_block, 0),
             (decay, key_block, 0),
             (logits, key_block, 0),
             (states, (1, DK, DV), "state"),
             (dmixed, val_block, 0),
-            (gate_back, val_block, 0),
             (leaving, state_shape, None),
         ],
         outputs=[
-            (shape_of(tokens, mixes.shape[1], dtype=LOW), (BLOCK, mixes.shape[1]), 0),
+            (shape_of(tokens, DV + 2 * DK, dtype=LOW), (BLOCK, DV + 2 * DK), 0),
             (shape_of(tokens, DK), key_block, 0),
             (shape_of(1, DK), (1, DK), None),
         ],
         scratch=[state_scratch],
-        flops=8 << 30,
-    )
-    mix_halves = reduced(first, mixes_back)
+    )
+    mixes_back, grad_logits, first, resid_back, gate_back, full_k, full_q, full_g = together(
+        (up_grad, "flown"),
+        (out_grad.sent, 0),
+        (down_grad, "come"),
+        mixes_back,
+        grad_logits,
+        first,
+        resid_back,
+        gate_back,
+        full_k,
+        full_q,
+        full_g,
+    )
+    out_grad.pairs = ((resid_back, gated), (first, gate_back))
+    out_grad.send(2)
+    mix_grad = Reduce((first, mixes_back))
+    mix_grad.make()
+    full_vkq = jnp.concatenate([full_k, full_q], axis=1)
     precise = lax.Precision.HIGHEST
+    grad_rank = lax.dot_general(
+        grad_logits, rank_out.astype(FULL), (NT, ((), ())), precision=precise
+    )
+    rank_high = grad_rank.astype(LOW)
+    rank_low = (grad_rank - rank_high.astype(FULL)).astype(LOW)
+
+    back_pairs = (
+        (mixes_back, full_vkq),
+        (gate_back, full_g),
+        (rank_high, rank_weight),
+        (rank_low, rank_weight),
+    )
+    far = far_part(*back_pairs)
+    far, first, back_pairs, resid_back, gate_back, gated = together(
+        (out_grad.sent, 1), (mix_grad, "parts"), far, first, list(back_pairs), resid_back, gate_back, gated
+    )
+    far, first, back_pairs, resid_back, gate_back, gated, grad_logits, up_grad.flown = together(
+        summed_pair(*far).astype(LOW), first, back_pairs, resid_back, gate_back, gated, grad_logits, up_grad.flown
+    )
+    mixes_back, rank_high, rank_low = back_pairs[0][0], back_pairs[2][0], back_pairs[3][0]
+    mix_grad.pairs = ((first, mixes_back),)
+    out_grad.pairs = ((resid_back, gated), (first, gate_back))
+    got = pair(far)
+    out_grad.send(laps)
+    mix_grad.send()
+    out_grad.make_own()
+    out_grad.hop()
+    up_grad.hop()
+    near = near_part(*back_pairs)
+    mix_grad.make_own()
+    grad_rank_in = dot(rank_high, first, TN) + dot(rank_low, first, TN)
     grad_rank_out = lax.dot_general(
         rank_in.astype(FULL), grad_logits, (TN, ((), ())), precision=precise
     )
-    grad_rank = lax.dot_general(
-        grad_logits, rank_out.astype(FULL), (NT, ((), ())), precision=precise
-    )
-    rank_high = grad_rank.astype(LOW)
-    rank_low = (grad_rank - rank_high.astype(FULL)).astype(LOW)
-    first_parts = dot(mixes_back, full_q, NT) + (
-        dot(rank_high, rank_weight, NT) + dot(rank_low, rank_weight, NT)
-    )
-    grad_rank_in = dot(rank_high, first, TN) + dot(rank_low, first, TN)
-    grad_first = gathered_sum(first_parts)
-    hidden_norm, grad_gain_attn = norm_back(grad_first, hidden, scale_attn, gain_attn)
+    got, near, grad_rank_in, grad_rank_out, out_far, out_near = together(
+        *[(out_grad.sent, i) for i in range(2, laps)],
+        (mix_grad.sent, 0),
+        (mix_grad, "owns"),
+        (out_grad, "flown"),
+        (up_grad, "flown"),
+        got,
+        near,
+        grad_rank_in,
+        grad_rank_out,
+        summed_pair(*out_far).astype(LOW),
+        summed_pair(*out_near),
+    )
+    mix_grad.send()
+    mix_grad.hop()
+    out_grad.hop()
+    out_got = pair(out_far)
+    hidden_norm, grad_gain_attn = norm_back(summed_pair(*near) + got, hidden, scale_attn, gain_attn)
     input_own = grad_resid + hidden_norm
-    grad_input = columns_out(input_own, twin(input_own), order, inverse, core, wide)
+    input_own, grad_gain_attn = together(
+        (mix_grad.sent, 1), (mix_grad, "flown"), (out_grad, "flown"), input_own, grad_gain_attn
+    )
+    mix_grad.send()
+    mix_grad.hop()
+    down_grad.last()
+    down_grad.halve()
+    input_near = twin(input_own)
 
     def unordered(x):
         return jnp.concatenate(
@@ -649,10 +1150,46 @@
         [rank_part, bias_part, head_part, jnp.zeros((6, 2 * DK), FULL)], axis=0
     )
     small = jnp.concatenate([wide_part, narrow_part], axis=1)
-    hop = 1
-    while hop < peers:
-        small = small + lax.ppermute(small, "seq", [(i, i ^ hop) for i in range(peers)])
-        hop *= 2
+    input_near, small, out_got = together(
+        (mix_grad.sent, 2), (mix_grad, "flown"), (down_grad, "got"), input_near, small, out_got
+    )
+    hops = [1 << k for k in (0, *range(2, peers.bit_length() - 1), 1)]
+
+    def summed(small):
+        hop = hops.pop(0)
+        return small + lax.ppermute(small, "seq", [(i, i ^ hop) for i in range(peers)])
+
+    mix_grad.send(laps)
+    mix_grad.hop()
+    out_grad.hop()
+    small = summed(small)
+    gate_grad.last()
+    gate_grad.halve()
+    grad_input = columns_out(input_own, input_near, order, inverse, core, wide)
+    small, grad_input = together(
+        *[(mix_grad.sent, i) for i in range(3, laps)],
+        (mix_grad, "flown"),
+        (out_grad, "flown"),
+        (gate_grad, "got"),
+        small,
+        grad_input,
+    )
+    mix_grad.last()
+    mix_grad.halve()
+    small = summed(small)
+    small = together((mix_grad, "got"), small)
+    small = summed(small)
+    up_grad.last()
+    up_grad.halve()
+    small = together((up_grad, "got"), small)
+    out_grad.last()
+    out_grad.halve()
+    out_own = (resid + (out_near + out_got)).astype(LOW)
+    block_out = columns_out(out_own, twin(out_own), order, inverse, core, wide)
+    while hops:
+        small = summed(small)
+    down_halves, gate_halves, up_halves = down_grad.out(), gate_grad.out(), up_grad.out()
+    out_halves, mix_halves = out_grad.out(), mix_grad.out()
 
     def beside(pieces, start, stop):
         return jnp.concatenate([half[:, start:stop] for half in pieces], axis=1)
@@ -661,15 +1198,15 @@
         block_out,
         grad_input,
         small[16, :width],
-        beside(mix_halves, 0, DK),
-        beside(mix_halves, DK, 2 * DK),
-        beside(mix_halves, 2 * DK, 2 * DK + DV),
+        beside(mix_halves, DV + DK, DV + 2 * DK),
+        beside(mix_halves, DV, DV + DK),
+        beside(mix_halves, 0, DV),
         small[:16, :width].T,
         small[:16, width:],
         small[16, width:],
-        beside(mix_halves, 2 * DK + DV, 2 * DK + 2 * DV),
+        beside(out_halves, DV, 2 * DV),
         small[17, width:],
-        jnp.concatenate(out_halves, axis=1).T,
+        beside(out_halves, 0, DV).T,
         small[17, :width],
         jnp.concatenate(gate_halves, axis=1),
         jnp.concatenate(up_halves, axis=1),

time: 1020 us -> 838 us (0.82)
  waiting for transfers between devices: 519 us -> 318 us
  matrix products: 183 us -> 10.8 us
  Pallas kernels: 53.8 us -> 204 us
  other arithmetic: 59.6 us -> 95.1 us
  local copies, waits for them, and re-layouts: 74.4 us -> 98.2 us
  starting transfers between devices: 100 us -> 88.3 us
    dot_general x54 -> x5, matrix products: 182 us -> 9.8 us  [dot(): lax.dot_general(left, right, (dims, ((), ())), preferred_element_type=FULL)]
    pallas_call x0 -> x24, Pallas kernels: none -> 151 us  [the longest x10 55.7 us: parts_call(): pl.pallas_call(functools.partial(parts_kernel, len(pairs), [(j, i) for j,...]
    ppermute x36 -> x30, waiting for transfers between devices: 203 us -> 121 us  [side(): return lax.ppermute(x, 'seq', [(i, i ^ 2) for i in range(peers)])]
    ppermute x27, waiting for transfers between devices: 209 us -> 137 us  [ring(): return lax.ppermute(x, 'seq', [(i, (i + 4) % peers) for i in range(peers)])]
    ppermute x17 -> x16, waiting for transfers between devices: 63.9 us -> 18.5 us  [pair(): return lax.ppermute(x, 'seq', [(i, i ^ 1) for i in range(peers)])]
    ppermute x4, waiting for transfers between devices: 40.4 us -> 2.36 us  [summed(): lax.ppermute(small, 'seq', [(i, i ^ hop) for i in range(peers)])]
    all_to_all x4, waiting for transfers between devices: 2.15 us -> 28.7 us  [turned(): lax.all_to_all(x, 'seq', 0, 0, axis_index_groups=halves_of_seq, tiled=True)]
    convert_element_type x12 -> x27, other arithmetic: 12.3 us -> 36.9 us  [the longest x14 26 us: hop(): self.flown = ring(self.add().astype(LOW))]
  transfers between devices with their start and end apart: 108 -> 101, of which waited for: 43 -> 40; matrix products, arithmetic and copies ran while one was open for 20% -> 15% of each run, Pallas kernels for 3% -> 23%
where the time goes in v2:
time: 838 us; the launch traced here: 828 us
  waiting for transfers between devices  318 us (38%)
  Pallas kernels  204 us (24%)
  local copies, waits for them, and re-layouts  98.2 us (12%)
  other arithmetic  95.1 us (11%)
  starting transfers between devices  88.3 us (11%)
  between operations  13.9 us (2%)
  matrix products  10.8 us (1%)
    ppermute x27, waiting for transfers between devices, ring(): return lax.ppermute(x, 'seq', [(i, (i + 4) % peers) for i in range(peers)])  137 us
    ppermute x30, waiting for transfers between devices, side(): return lax.ppermute(x, 'seq', [(i, i ^ 2) for i in range(peers)])  121 us
    unnamed x382, local copies, waits for them, and re-layouts  77.2 us
    pallas_call x10, Pallas kernels, parts_call(): pl.pallas_call(functools.partial(parts_kernel, len(pairs), [(j, i) for j,...  55.7 us
    pallas_call x4, Pallas kernels, assemble_call(): pl.pallas_call(kernel, grid=(x.shape[0] // tile,), in_specs=[rows(x.shape...  52.7 us
    pallas_call x4, Pallas kernels, token_call(): pl.pallas_call(kernel, grid_spec=pltpu.PrefetchScalarGridSpec(num_scalar_...  42.9 us
    pallas_call x8, Pallas kernels, product_call(): pl.pallas_call(functools.partial(product_kernel, len(pairs)), grid=(width...  40.9 us
    ppermute x30, starting transfers between devices, side(): return lax.ppermute(x, 'seq', [(i, i ^ 2) for i in range(peers)])  30.8 us
  transfers between devices with their start and end apart: 101, of which 40 were waited for; matrix products, arithmetic and copies ran while one was open for 15% of the time, Pallas kernels for 23%

profile of v2, /device:TPU:0, one launch (start us, length us, event | category | flops | bytes accessed | tf_op | source)
XLA Modules:
  0.0 828.2 jit_solution(3057882367145216825)
XLA Ops:
  2.6 3.0 collective-permute-start
  27.2 4.9 collective-permute-done.1.refs_1_
  38.8 9.6 %collective-permute-done.2.refs_2_ = bf16[256,768]{1,0:T(8,128)(2,1)} collective-permute-done((bf16[256,768]{1,0:T(8,128)(2,1)S(1)}, bf16[256,768]{1,0:T(8,128)(2,1)}, u32[]{:S(2)}, u32[]{:S(2)}) %collective-permute-start.2) | collective-permute-done | bytes 393248 | tf_op jit(solution)/shard_map/ppermute | solution.py:549
  51.4 3.6 pad_maximum_fusion.x_ref.refs_1_.refs_0_
  55.0 5.9 collective-permute-done.10
  60.9 2.9 collective-permute-done.7.refs_3_
  67.2 3.4 fusion.53
  72.4 4.5 collective-permute-done.6.refs_6_
  76.9 6.8 collective-permute-done.11.refs_7_
  93.0 7.8 shard_map.388
  102.7 8.1 shard_map.389
  116.2 5.5 all-to-all-start
  124.1 25.1 %collective-permute-done.18.refs_5_ = bf16[256,1280]{1,0:T(8,128)(2,1)} collective-permute-done((bf16[256,1280]{1,0:T(8,128)(2,1)}, bf16[256,1280]{1,0:T(8,128)(2,1)}, u32[]{:S(2)}, u32[]{:S(2)}) %collective-permute-start.18) | collective-permute-done | bytes 655392 | tf_op jit(solution)/shard_map/ppermute | solution.py:546
  153.5 5.5 all-to-all-start.1
  163.5 4.8 collective-permute-done.16.refs_6_
  168.4 22.3 %all-to-all-done.1 = bf16[8,32,512]{2,1,0:T(8,128)(2,1)S(1)} async-done(((bf16[8,32,512]{2,1,0:T(8,128)(2,1)}), bf16[8,32,512]{2,1,0:T(8,128)(2,1)S(1)}, u32[]{:S(2)}, u32[]{:S(2)}) %all-to-all-start.1) | async-done | bytes 262176 | tf_op jit(solution)/shard_map/all_to_all | solution.py:805
  194.6 9.5 %shard_map.391 = (f32[1024,768]{1,0:T(8,128)}, bf16[2048,512]{1,0:T(8,128)(2,1)}, bf16[2048,256]{1,0:T(8,128)(2,1)}, bf16[2048,512]{1,0:T(8,128)(2,1)}) custom-call(bf16[1024,2048]{1,0:T(8,128)(2,1)} %pad_maximum_fusion.x_ref.refs_1_.refs_0_, bf16[256,1280]{1,0:T(8,128)(2,1)S(1)} %copy-done.55, bf16[256,1280]{1,0:T(8,128)(2,1)} %collective-permute-done.12.refs_1_, ...), custom_call_target="tpu_custom_call" | custom-call | flops 1 | bytes 1 | tf_op jit(solution)/shard_map/pallas_call | solution.py:402
  206.0 10.4 %shard_map.392 = (f32[1024,512]{1,0:T(8,128)S(1)}, bf16[1024,512]{1,0:T(8,128)(2,1)S(1)}, f32[8,256,512]{2,1,0:T(8,128)}) custom-call(s32[26]{0:T(128)S(1)} %copy-done.104, f32[1024,768]{1,0:T(8,128)S(1)} %copy-done.9, f32[1024,768]{1,0:T(8,128)S(1)} %copy-done.6, f32[1024,768]{1,0:T(8,128)S(1)} %copy-done.6, f32[1024,768]{1,0:T(8,128)S(1)} %copy-done.9, ...), custom_call_target="tpu_custom_call" | custom-call | flops 1 | bytes 1 | tf_op jit(solution)/shard_map/pallas_call | solution.py:255
  216.4 3.0 pad_maximum_fusion.1.refs_0_.x_ref
  219.4 9.0 %collective-permute-done.25.refs_2_ = bf16[256,2816]{1,0:T(8,128)(2,1)} collective-permute-done((bf16[256,2816]{1,0:T(8,128)(2,1)}, bf16[256,2816]{1,0:T(8,128)(2,1)}, u32[]{:S(2)}, u32[]{:S(2)}) %collective-permute-start.25) | collective-permute-done | bytes 1441824 | tf_op jit(solution)/shard_map/ppermute | solution.py:549
  236.9 27.9 %collective-permute-done.28.refs_5_ = bf16[256,2816]{1,0:T(8,128)(2,1)S(1)} collective-permute-done((bf16[256,2816]{1,0:T(8,128)(2,1)}, bf16[256,2816]{1,0:T(8,128)(2,1)S(1)}, u32[]{:S(2)}, u32[]{:S(2)}) %collective-permute-start.28) | collective-permute-done | bytes 1441824 | tf_op jit(solution)/shard_map/ppermute | solution.py:546
  273.3 30.1 %collective-permute-done.34.refs_1_ = bf16[512,1408]{1,0:T(8,128)(2,1)S(1)} collective-permute-done((bf16[512,1408]{1,0:T(8,128)(2,1)S(1)}, bf16[512,1408]{1,0:T(8,128)(2,1)S(1)}, u32[]{:S(2)}, u32[]{:S(2)}) %collective-permute-start.34) | collective-permute-done | bytes 1441824 | tf_op jit(solution)/shard_map/ppermute | solution.py:549
  308.5 24.2 %collective-permute-done.32.refs_7_ = bf16[256,2816]{1,0:T(8,128)(2,1)S(1)} collective-permute-done((bf16[256,2816]{1,0:T(8,128)(2,1)S(1)}, bf16[256,2816]{1,0:T(8,128)(2,1)S(1)}, u32[]{:S(2)}, u32[]{:S(2)}) %collective-permute-start.32) | collective-permute-done | bytes 1441824 | tf_op jit(solution)/shard_map/ppermute | solution.py:546
  332.7 5.8 collective-permute-done.37.refs_2_
  338.5 21.4 %shard_map.395 = (f32[1024,2816]{1,0:T(8,128)}, bf16[2048,2816]{1,0:T(8,128)(2,1)}, bf16[1024,1408]{1,0:T(8,128)(2,1)}) custom-call(bf16[1024,2048]{1,0:T(8,128)(2,1)} %pad_maximum_fusion.2.x_ref.refs_0_, bf16[256,2816]{1,0:T(8,128)(2,1)} %pad_maximum_fusion.4.refs_0_, bf16[256,2816]{1,0:T(8,128)(2,1)} %collective-permute-done.23.refs_1_, ...), custom_call_target="tpu_custom_call" | custom-call | flops 1 | bytes 1 | tf_op jit(solution)/shard_map/pallas_call | solution.py:402
  361.8 4.0 shard_map.396
  365.8 7.1 collective-permute-done.39.refs_3_
  373.4 14.0 %shard_map.397 = (bf16[1024,2816]{1,0:T(8,128)(2,1)}, bf16[2048,1408]{1,0:T(8,128)(2,1)}) custom-call(bf16[1024,2048]{1,0:T(8,128)(2,1)} %copy-done.12, f32[1024,2816]{1,0:T(8,128)} %get-tuple-element.431.pre_ref, bf16[512,1408]{1,0:T(8,128)(2,1)S(1)} %copy-done.42, bf16[512,1408]{1,0:T(8,128)(2,1)} %copy-done.144, ...), custom_call_target="tpu_custom_call" | custom-call | flops 1 | bytes 1 | tf_op jit(solution)/shard_map/pallas_call | solution.py:402
  390.1 8.8 %shard_map.399 = (f32[256,2048]{1,0:T(8,128)S(1)}, bf16[256,2048]{1,0:T(8,128)(2,1)S(1)}) custom-call(bf16[1024,2816]{1,0:T(8,128)(2,1)S(1)} %copy-done.7, bf16[2048,2816]{1,0:T(8,128)(2,1)} %get-tuple-element.466.refs_1_), custom_call_target="tpu_custom_call" | custom-call | flops 1 | bytes 1 | tf_op jit(solution)/shard_map/pallas_call | solution.py:338
  401.1 6.2 shard_map.398
  411.2 8.4 %shard_map.400 = (f32[512,1408]{1,0:T(8,128)S(1)}, f32[512,1408]{1,0:T(8,128)S(1)}, f32[512,1408]{1,0:T(8,128)S(1)}) custom-call(s32[6]{0:T(128)S(1)} %copy-done.110, bf16[1024,2048]{1,0:T(8,128)(2,1)} %copy-done.12, bf16[1024,1408]{1,0:T(8,128)(2,1)S(1)} %copy-done.14), custom_call_target="tpu_custom_call" | custom-call | flops 1 | bytes 1 | tf_op jit(solution)/shard_map/pallas_call | solution.py:380
  428.9 8.8 %shard_map.402 = (f32[256,2048]{1,0:T(8,128)S(1)}, bf16[256,2048]{1,0:T(8,128)(2,1)S(1)}) custom-call(bf16[1024,2816]{1,0:T(8,128)(2,1)S(1)} %copy-done.8, bf16[2048,2816]{1,0:T(8,128)(2,1)} %get-tuple-element.466.refs_1_), custom_call_target="tpu_custom_call" | custom-call | flops 1 | bytes 1 | tf_op jit(solution)/shard_map/pallas_call | solution.py:338
  438.0 6.1 shard_map.401
  444.2 13.5 %collective-permute-done.44 = bf16[256,1408]{1,0:T(8,128)(2,1)} collective-permute-done((bf16[256,1408]{1,0:T(8,128)(2,1)S(1)}, bf16[256,1408]{1,0:T(8,128)(2,1)}, u32[]{:S(2)}, u32[]{:S(2)}) %collective-permute-start.44) | collective-permute-done | bytes 720928 | tf_op jit(solution)/shard_map/ppermute | solution.py:546
  468.9 5.4 shard_map.404
  477.6 5.4 shard_map.403
  483.1 3.8 collective-permute-done.48
  486.8 5.1 collective-permute-done.49
  500.4 3.7 collective-permute-start.55
  506.9 7.0 shard_map.405
  516.3 10.1 %collective-permute-done.51 = bf16[256,1408]{1,0:T(8,128)(2,1)} collective-permute-done((bf16[256,1408]{1,0:T(8,128)(2,1)S(1)}, bf16[256,1408]{1,0:T(8,128)(2,1)}, u32[]{:S(2)}, u32[]{:S(2)}) %collective-permute-start.51) | collective-permute-done | bytes 720928 | tf_op jit(solution)/shard_map/ppermute | solution.py:546
  526.5 5.6 collective-permute-done.52
  532.1 14.4 %collective-permute-done.55 = bf16[256,1408]{1,0:T(8,128)(2,1)} collective-permute-done((bf16[256,1408]{1,0:T(8,128)(2,1)}, bf16[256,1408]{1,0:T(8,128)(2,1)}, u32[]{:S(2)}, u32[]{:S(2)}) %collective-permute-start.55) | collective-permute-done | bytes 720928 | tf_op jit(solution)/shard_map/ppermute | solution.py:549
  548.9 5.5 all-to-all-start.2
  563.4 5.7 shard_map.406
  569.2 4.6 all-to-all-done.2.local_ref
  587.4 5.8 all-to-all-start.3
  602.2 4.2 shard_map.409
  608.8 4.2 shard_map.408
  625.1 17.4 %shard_map.410 = (bf16[1024,1024]{1,0:T(8,128)(2,1)S(1)}, f32[1024,256]{1,0:T(8,128)S(1)}, f32[1,256]{1,0:T(1,128)S(1)}) custom-call(s32[26]{0:T(128)S(1)} %copy-done.104, f32[1024,768]{1,0:T(8,128)S(1)} %copy-done.11, f32[1024,768]{1,0:T(8,128)S(1)} %copy-done.6, f32[1024,768]{1,0:T(8,128)S(1)} %copy-done.6, f32[1024,256]{1,0:T(8,128)S(1)} %copy-done.33, ...), custom_call_target="tpu_custom_call" | custom-call | flops 1 | bytes 1 | tf_op jit(solution)/shard_map/pallas_call | solution.py:255
  648.7 5.0 shard_map.411
  658.4 5.3 shard_map.412
  677.8 5.3 shard_map.414
  686.8 4.1 shard_map.413
  703.8 5.3 shard_map.415
  714.2 10.0 %collective-permute-done.69 = bf16[256,1024]{1,0:T(8,128)(2,1)S(1)} collective-permute-done((bf16[256,1024]{1,0:T(8,128)(2,1)S(1)}, bf16[256,1024]{1,0:T(8,128)(2,1)S(1)}, u32[]{:S(2)}, u32[]{:S(2)}) %collective-permute-start.69) | collective-permute-done | bytes 524320 | tf_op jit(solution)/shard_map/ppermute | solution.py:549
  736.9 6.7 collective-permute-done.77
  743.6 10.8 %collective-permute-done.76 = bf16[256,1024]{1,0:T(8,128)(2,1)S(1)} collective-permute-done((bf16[256,1024]{1,0:T(8,128)(2,1)S(1)}, bf16[256,1024]{1,0:T(8,128)(2,1)S(1)}, u32[]{:S(2)}, u32[]{:S(2)}) %collective-permute-start.76) | collective-permute-done | bytes 524320 | tf_op jit(solution)/shard_map/ppermute | solution.py:549
  764.6 9.7 %collective-permute-done.79 = bf16[256,1024]{1,0:T(8,128)(2,1)S(1)} collective-permute-done((bf16[256,1024]{1,0:T(8,128)(2,1)S(1)}, bf16[256,1024]{1,0:T(8,128)(2,1)S(1)}, u32[]{:S(2)}, u32[]{:S(2)}) %collective-permute-start.79) | collective-permute-done | bytes 524320 | tf_op jit(solution)/shard_map/ppermute | solution.py:549
  783.0 4.3 shard_map.417
  790.0 6.1 collective-permute-done.87
  803.1 3.9 collective-permute-done.92
  807.1 3.5 collective-permute-done.96
  821.7 3.8 shard_map.416
  (685 shorter events, 280.3 us)
Async XLA Ops:
  22.7 25.7 %collective-permute-start.4 = (bf16[256,2048]{1,0:T(8,128)(2,1)S(1)}, bf16[256,2048]{1,0:T(8,128)(2,1)}, u32[]{:S(2)}, u32[]{:S(2)}) collective-permute-start(bf16[256,2048]{1,0:T(8,128)(2,1)S(1)} %fusion.4), channel_id=1, source_target_pairs={{0,2},{2,0},{4,6},{6,4},{8,10},{10,8},{12,14},{14,12},{16,18},{18,... | collective-permute-start | bytes 3145736 | tf_op jit(solution)/shard_map/ppermute | solution.py:543
  23.2 25.1 %collective-permute-start.5 = (bf16[256,2048]{1,0:T(8,128)(2,1)S(1)}, bf16[256,2048]{1,0:T(8,128)(2,1)}, u32[]{:S(2)}, u32[]{:S(2)}) collective-permute-start(bf16[256,2048]{1,0:T(8,128)(2,1)S(1)} %fusion.4), channel_id=1, source_target_pairs={{0,1},{1,0},{2,3},{3,2},{4,5},{5,4},{6,7},{7,6},{8,9},{9,8},{10,11... | collective-permute-start | bytes 3145736 | tf_op jit(solution)/shard_map/ppermute | solution.py:552
  65.1 45.7 %collective-permute-start.15 = (bf16[128,4224]{1,0:T(8,128)(2,1)}, bf16[128,4224]{1,0:T(8,128)(2,1)}, u32[]{:S(2)}, u32[]{:S(2)}) collective-permute-start(bf16[128,4224]{1,0:T(8,128)(2,1)} %get-tuple-element.376), channel_id=1, source_target_pairs={{0,2},{2,0},{4,6},{6,4},{8,10},{10,8},{12,14},{14,12},{16,18},{18,... | collective-permute-start | bytes 3244040 | tf_op jit(solution)/shard_map/ppermute | solution.py:543
  83.7 27.1 %collective-permute-start.13 = (bf16[256,1280]{1,0:T(8,128)(2,1)}, bf16[256,1280]{1,0:T(8,128)(2,1)}, u32[]{:S(2)}, u32[]{:S(2)}) collective-permute-start(bf16[256,1280]{1,0:T(8,128)(2,1)} %collective-permute-done.12.refs_1_), channel_id=1, source_target_pairs={{0,8},{2,10},{4,12},{6,14},{8,16},{10,18},{12,20},{14,22},{16,24},... | collective-permute-start | bytes 1966088 | tf_op jit(solution)/shard_map/ppermute | solution.py:549
  83.7 27.1 %collective-permute-start.14 = (bf16[256,1280]{1,0:T(8,128)(2,1)S(1)}, bf16[256,1280]{1,0:T(8,128)(2,1)}, u32[]{:S(2)}, u32[]{:S(2)}) collective-permute-start(bf16[256,1280]{1,0:T(8,128)(2,1)S(1)} %pad_maximum_fusion.11.refs_0_), channel_id=1, source_target_pairs={{0,4},{2,6},{4,0},{6,2},{8,12},{10,14},{12,8},{14,10},{16,20},{18,... | collective-permute-start | bytes 1966088 | tf_op jit(solution)/shard_map/ppermute | solution.py:546
  91.3 32.7 %collective-permute-start.20 = (bf16[256,2048]{1,0:T(8,128)(2,1)S(1)}, bf16[256,2048]{1,0:T(8,128)(2,1)}, u32[]{:S(2)}, u32[]{:S(2)}) collective-permute-start(bf16[256,2048]{1,0:T(8,128)(2,1)S(1)} %get-tuple-element.381), channel_id=1, source_target_pairs={{0,2},{2,0},{4,6},{6,4},{8,10},{10,8},{12,14},{14,12},{16,18},{18,... | collective-permute-start | bytes 3145736 | tf_op jit(solution)/shard_map/ppermute | solution.py:543
  92.0 32.1 %collective-permute-start.21 = (bf16[256,2048]{1,0:T(8,128)(2,1)S(1)}, bf16[256,2048]{1,0:T(8,128)(2,1)}, u32[]{:S(2)}, u32[]{:S(2)}) collective-permute-start(bf16[256,2048]{1,0:T(8,128)(2,1)S(1)} %get-tuple-element.381), channel_id=1, source_target_pairs={{0,1},{1,0},{2,3},{3,2},{4,5},{5,4},{6,7},{7,6},{8,9},{9,8},{10,11... | collective-permute-start | bytes 3145736 | tf_op jit(solution)/shard_map/ppermute | solution.py:552
  113.2 36.3 %collective-permute-start.19 = (bf16[256,1408]{1,0:T(8,128)(2,1)}, bf16[256,1408]{1,0:T(8,128)(2,1)}, u32[]{:S(2)}, u32[]{:S(2)}) collective-permute-start(bf16[256,1408]{1,0:T(8,128)(2,1)} %pad_maximum_fusion.10), channel_id=1, source_target_pairs={{0,4},{2,6},{4,0},{6,2},{8,12},{10,14},{12,8},{14,10},{16,20},{18,... | collective-permute-start | bytes 2162696 | tf_op jit(solution)/shard_map/ppermute | solution.py:546
  114.5 34.7 %collective-permute-start.18 = (bf16[256,1280]{1,0:T(8,128)(2,1)}, bf16[256,1280]{1,0:T(8,128)(2,1)}, u32[]{:S(2)}, u32[]{:S(2)}) collective-permute-start(bf16[256,1280]{1,0:T(8,128)(2,1)} %collective-permute-done.12.refs_1_), channel_id=1, source_target_pairs={{0,4},{2,6},{4,0},{6,2},{8,12},{10,14},{12,8},{14,10},{16,20},{18,... | collective-permute-start | bytes 1966088 | tf_op jit(solution)/shard_map/ppermute | solution.py:546
  115.3 34.3 %collective-permute-start.17 = (bf16[256,1280]{1,0:T(8,128)(2,1)}, bf16[256,1280]{1,0:T(8,128)(2,1)}, u32[]{:S(2)}, u32[]{:S(2)}) collective-permute-start(bf16[256,1280]{1,0:T(8,128)(2,1)} %collective-permute-done.13.refs_2_), channel_id=1, source_target_pairs={{0,8},{2,10},{4,12},{6,14},{8,16},{10,18},{12,20},{14,22},{16,24},... | collective-permute-start | bytes 1966088 | tf_op jit(solution)/shard_map/ppermute | solution.py:549
  116.2 33.3 %all-to-all-start = ((bf16[8,32,640]{2,1,0:T(8,128)(2,1)}), bf16[8,32,640]{2,1,0:T(8,128)(2,1)S(1)}, u32[]{:S(2)}, u32[]{:S(2)}) async-start(bf16[8,32,640]{2,1,0:T(8,128)(2,1)} %bitcast.22), calls=%async_computation | async-start | bytes 655360 | tf_op jit(solution)/shard_map/all_to_all | solution.py:805
  149.6 41.8 %collective-permute-start.23 = (bf16[256,2816]{1,0:T(8,128)(2,1)}, bf16[256,2816]{1,0:T(8,128)(2,1)}, u32[]{:S(2)}, u32[]{:S(2)}) collective-permute-start(bf16[256,2816]{1,0:T(8,128)(2,1)} %pad_maximum_fusion.4.refs_0_), channel_id=1, source_target_pairs={{0,8},{2,10},{4,12},{6,14},{8,16},{10,18},{12,20},{14,22},{16,24},... | collective-permute-start | bytes 4325384 | tf_op jit(solution)/shard_map/ppermute | solution.py:549
  150.5 40.8 %collective-permute-start.24 = (bf16[256,2048]{1,0:T(8,128)(2,1)}, bf16[256,2048]{1,0:T(8,128)(2,1)S(1)}, u32[]{:S(2)}, u32[]{:S(2)}) collective-permute-start(bf16[256,2048]{1,0:T(8,128)(2,1)} %collective-permute-done.20), channel_id=1, source_target_pairs={{0,1},{1,0},{2,3},{3,2},{4,5},{5,4},{6,7},{7,6},{8,9},{9,8},{10,11... | collective-permute-start | bytes 3145736 | tf_op jit(solution)/shard_map/ppermute | solution.py:552
  151.8 39.5 %collective-permute-start.22 = (bf16[256,1280]{1,0:T(8,128)(2,1)}, bf16[256,1280]{1,0:T(8,128)(2,1)S(1)}, u32[]{:S(2)}, u32[]{:S(2)}) collective-permute-start(bf16[256,1280]{1,0:T(8,128)(2,1)} %collective-permute-done.17.refs_3_), channel_id=1, source_target_pairs={{0,4},{2,6},{4,0},{6,2},{8,12},{10,14},{12,8},{14,10},{16,20},{18,... | collective-permute-start | bytes 1966088 | tf_op jit(solution)/shard_map/ppermute | solution.py:546
  153.5 37.2 %all-to-all-start.1 = ((bf16[8,32,512]{2,1,0:T(8,128)(2,1)}), bf16[8,32,512]{2,1,0:T(8,128)(2,1)S(1)}, u32[]{:S(2)}, u32[]{:S(2)}) async-start(bf16[8,32,512]{2,1,0:T(8,128)(2,1)} %shard_map.390), calls=%async_computation.1 | async-start | bytes 524288 | tf_op jit(solution)/shard_map/all_to_all | solution.py:805
  159.0 60.5 %collective-permute-start.26 = (bf16[256,2816]{1,0:T(8,128)(2,1)}, bf16[256,2816]{1,0:T(8,128)(2,1)}, u32[]{:S(2)}, u32[]{:S(2)}) collective-permute-start(bf16[256,2816]{1,0:T(8,128)(2,1)} %pad_maximum_fusion.4.refs_0_), channel_id=1, source_target_pairs={{0,4},{2,6},{4,0},{6,2},{8,12},{10,14},{12,8},{14,10},{16,20},{18,... | collective-permute-start | bytes 4325384 | tf_op jit(solution)/shard_map/ppermute | solution.py:546
  192.5 35.9 %collective-permute-start.25 = (bf16[256,2816]{1,0:T(8,128)(2,1)}, bf16[256,2816]{1,0:T(8,128)(2,1)}, u32[]{:S(2)}, u32[]{:S(2)}) collective-permute-start(bf16[256,2816]{1,0:T(8,128)(2,1)} %collective-permute-done.23.refs_1_), channel_id=1, source_target_pairs={{0,8},{2,10},{4,12},{6,14},{8,16},{10,18},{12,20},{14,22},{16,24},... | collective-permute-start | bytes 4325384 | tf_op jit(solution)/shard_map/ppermute | solution.py:549
  230.6 34.2 %collective-permute-start.28 = (bf16[256,2816]{1,0:T(8,128)(2,1)}, bf16[256,2816]{1,0:T(8,128)(2,1)S(1)}, u32[]{:S(2)}, u32[]{:S(2)}) collective-permute-start(bf16[256,2816]{1,0:T(8,128)(2,1)} %collective-permute-done.23.refs_1_), channel_id=1, source_target_pairs={{0,4},{2,6},{4,0},{6,2},{8,12},{10,14},{12,8},{14,10},{16,20},{18,... | collective-permute-start | bytes 4325384 | tf_op jit(solution)/shard_map/ppermute | solution.py:546
  231.9 35.7 %collective-permute-start.27 = (bf16[256,2816]{1,0:T(8,128)(2,1)}, bf16[256,2816]{1,0:T(8,128)(2,1)S(1)}, u32[]{:S(2)}, u32[]{:S(2)}) collective-permute-start(bf16[256,2816]{1,0:T(8,128)(2,1)} %collective-permute-done.25.refs_2_), channel_id=1, source_target_pairs={{0,8},{2,10},{4,12},{6,14},{8,16},{10,18},{12,20},{14,22},{16,24},... | collective-permute-start | bytes 4325384 | tf_op jit(solution)/shard_map/ppermute | solution.py:549
  233.5 34.1 %collective-permute-start.30 = (bf16[256,2048]{1,0:T(8,128)(2,1)S(1)}, bf16[256,2048]{1,0:T(8,128)(2,1)S(1)}, u32[]{:S(2)}, u32[]{:S(2)}) collective-permute-start(bf16[256,2048]{1,0:T(8,128)(2,1)S(1)} %add_convert_fusion.6), channel_id=1, source_target_pairs={{0,2},{2,0},{4,6},{6,4},{8,10},{10,8},{12,14},{14,12},{16,18},{18,... | collective-permute-start | bytes 3145736 | tf_op jit(solution)/shard_map/ppermute | solution.py:543
  267.6 35.8 %collective-permute-start.34 = (bf16[512,1408]{1,0:T(8,128)(2,1)S(1)}, bf16[512,1408]{1,0:T(8,128)(2,1)S(1)}, u32[]{:S(2)}, u32[]{:S(2)}) collective-permute-start(bf16[512,1408]{1,0:T(8,128)(2,1)S(1)} %copy-done.42), channel_id=1, source_target_pairs={{0,8},{2,10},{4,12},{6,14},{8,16},{10,18},{12,20},{14,22},{16,24},... | collective-permute-start | bytes 4325384 | tf_op jit(solution)/shard_map/ppermute | solution.py:549
  267.7 35.7 %collective-permute-start.33 = (bf16[256,2816]{1,0:T(8,128)(2,1)}, bf16[256,2816]{1,0:T(8,128)(2,1)S(1)}, u32[]{:S(2)}, u32[]{:S(2)}) collective-permute-start(bf16[256,2816]{1,0:T(8,128)(2,1)} %collective-permute-done.25.refs_2_), channel_id=1, source_target_pairs={{0,4},{2,6},{4,0},{6,2},{8,12},{10,14},{12,8},{14,10},{16,20},{18,... | collective-permute-start | bytes 4325384 | tf_op jit(solution)/shard_map/ppermute | solution.py:546
  271.2 32.2 %collective-permute-start.35 = (bf16[256,2048]{1,0:T(8,128)(2,1)S(1)}, bf16[256,2048]{1,0:T(8,128)(2,1)S(1)}, u32[]{:S(2)}, u32[]{:S(2)}) collective-permute-start(bf16[256,2048]{1,0:T(8,128)(2,1)S(1)} %multiply_convert_fusion), channel_id=1, source_target_pairs={{0,2},{2,0},{4,6},{6,4},{8,10},{10,8},{12,14},{14,12},{16,18},{18,... | collective-permute-start | bytes 3145736 | tf_op jit(solution)/shard_map/ppermute | solution.py:543
  272.8 30.6 %collective-permute-start.36 = (bf16[256,2048]{1,0:T(8,128)(2,1)S(1)}, bf16[256,2048]{1,0:T(8,128)(2,1)S(1)}, u32[]{:S(2)}, u32[]{:S(2)}) collective-permute-start(bf16[256,2048]{1,0:T(8,128)(2,1)S(1)} %multiply_convert_fusion), channel_id=1, source_target_pairs={{0,1},{1,0},{2,3},{3,2},{4,5},{5,4},{6,7},{7,6},{8,9},{9,8},{10,11... | collective-permute-start | bytes 3145736 | tf_op jit(solution)/shard_map/ppermute | solution.py:552
  272.8 59.9 %collective-permute-start.32 = (bf16[256,2816]{1,0:T(8,128)(2,1)S(1)}, bf16[256,2816]{1,0:T(8,128)(2,1)S(1)}, u32[]{:S(2)}, u32[]{:S(2)}) collective-permute-start(bf16[256,2816]{1,0:T(8,128)(2,1)S(1)} %collective-permute-done.27.refs_3_), channel_id=1, source_target_pairs={{0,4},{2,6},{4,0},{6,2},{8,12},{10,14},{12,8},{14,10},{16,20},{18,... | collective-permute-start | bytes 4325384 | tf_op jit(solution)/shard_map/ppermute | solution.py:546
  303.4 35.1 %collective-permute-start.37 = (bf16[512,1408]{1,0:T(8,128)(2,1)S(1)}, bf16[512,1408]{1,0:T(8,128)(2,1)}, u32[]{:S(2)}, u32[]{:S(2)}) collective-permute-start(bf16[512,1408]{1,0:T(8,128)(2,1)S(1)} %collective-permute-done.34.refs_1_), channel_id=1, source_target_pairs={{0,8},{2,10},{4,12},{6,14},{8,16},{10,18},{12,20},{14,22},{16,24},... | collective-permute-start | bytes 4325384 | tf_op jit(solution)/shard_map/ppermute | solution.py:549
  338.5 34.4 %collective-permute-start.39 = (bf16[512,1408]{1,0:T(8,128)(2,1)}, bf16[512,1408]{1,0:T(8,128)(2,1)}, u32[]{:S(2)}, u32[]{:S(2)}) collective-permute-start(bf16[512,1408]{1,0:T(8,128)(2,1)} %collective-permute-done.37.refs_2_), channel_id=1, source_target_pairs={{0,8},{2,10},{4,12},{6,14},{8,16},{10,18},{12,20},{14,22},{16,24},... | collective-permute-start | bytes 4325384 | tf_op jit(solution)/shard_map/ppermute | solution.py:549
  372.9 34.4 %collective-permute-start.40 = (bf16[512,1408]{1,0:T(8,128)(2,1)}, bf16[512,1408]{1,0:T(8,128)(2,1)S(1)}, u32[]{:S(2)}, u32[]{:S(2)}) collective-permute-start(bf16[512,1408]{1,0:T(8,128)(2,1)} %shard_map.396), channel_id=1, source_target_pairs={{0,8},{2,10},{4,12},{6,14},{8,16},{10,18},{12,20},{14,22},{16,24},... | collective-permute-start | bytes 4325384 | tf_op jit(solution)/shard_map/ppermute | solution.py:549
  422.6 36.0 %collective-permute-start.42 = (bf16[512,1408]{1,0:T(8,128)(2,1)}, bf16[512,1408]{1,0:T(8,128)(2,1)S(1)}, u32[]{:S(2)}, u32[]{:S(2)}) collective-permute-start(bf16[512,1408]{1,0:T(8,128)(2,1)} %add_convert_fusion.1), channel_id=1, source_target_pairs={{0,8},{2,10},{4,12},{6,14},{8,16},{10,18},{12,20},{14,22},{16,24},... | collective-permute-start | bytes 4325384 | tf_op jit(solution)/shard_map/ppermute | solution.py:549
  422.7 35.0 %collective-permute-start.45 = (bf16[256,2048]{1,0:T(8,128)(2,1)}, bf16[256,2048]{1,0:T(8,128)(2,1)S(1)}, u32[]{:S(2)}, u32[]{:S(2)}) collective-permute-start(bf16[256,2048]{1,0:T(8,128)(2,1)} %add_convert_fusion.5), channel_id=1, source_target_pairs={{0,2},{2,0},{4,6},{6,4},{8,10},{10,8},{12,14},{14,12},{16,18},{18,... | collective-permute-start | bytes 3145736 | tf_op jit(solution)/shard_map/ppermute | solution.py:543
  424.7 33.0 %collective-permute-start.44 = (bf16[256,1408]{1,0:T(8,128)(2,1)S(1)}, bf16[256,1408]{1,0:T(8,128)(2,1)}, u32[]{:S(2)}, u32[]{:S(2)}) collective-permute-start(bf16[256,1408]{1,0:T(8,128)(2,1)S(1)} %get-tuple-element.464), channel_id=1, source_target_pairs={{0,4},{2,6},{4,0},{6,2},{8,12},{10,14},{12,8},{14,10},{16,20},{18,... | collective-permute-start | bytes 2162696 | tf_op jit(solution)/shard_map/ppermute | solution.py:546
  466.5 25.5 %collective-permute-start.49 = (bf16[256,2048]{1,0:T(8,128)(2,1)}, bf16[256,2048]{1,0:T(8,128)(2,1)}, u32[]{:S(2)}, u32[]{:S(2)}) collective-permute-start(bf16[256,2048]{1,0:T(8,128)(2,1)} %get-tuple-element.497), channel_id=1, source_target_pairs={{0,2},{2,0},{4,6},{6,4},{8,10},{10,8},{12,14},{14,12},{16,18},{18,... | collective-permute-start | bytes 3145736 | tf_op jit(solution)/shard_map/ppermute | solution.py:543
  468.0 24.0 %collective-permute-start.50 = (bf16[256,2048]{1,0:T(8,128)(2,1)}, bf16[256,2048]{1,0:T(8,128)(2,1)}, u32[]{:S(2)}, u32[]{:S(2)}) collective-permute-start(bf16[256,2048]{1,0:T(8,128)(2,1)} %get-tuple-element.497), channel_id=1, source_target_pairs={{0,1},{1,0},{2,3},{3,2},{4,5},{5,4},{6,7},{7,6},{8,9},{9,8},{10,11... | collective-permute-start | bytes 3145736 | tf_op jit(solution)/shard_map/ppermute | solution.py:552
  492.0 24.3 %collective-permute-start.53 = (bf16[256,1408]{1,0:T(8,128)(2,1)S(1)}, bf16[256,1408]{1,0:T(8,128)(2,1)}, u32[]{:S(2)}, u32[]{:S(2)}) collective-permute-start(bf16[256,1408]{1,0:T(8,128)(2,1)S(1)} %get-tuple-element.495), channel_id=1, source_target_pairs={{0,4},{2,6},{4,0},{6,2},{8,12},{10,14},{12,8},{14,10},{16,20},{18,... | collective-permute-start | bytes 2162696 | tf_op jit(solution)/shard_map/ppermute | solution.py:546
  492.7 33.8 %collective-permute-start.51 = (bf16[256,1408]{1,0:T(8,128)(2,1)S(1)}, bf16[256,1408]{1,0:T(8,128)(2,1)}, u32[]{:S(2)}, u32[]{:S(2)}) collective-permute-start(bf16[256,1408]{1,0:T(8,128)(2,1)S(1)} %copy-done.119), channel_id=1, source_target_pairs={{0,4},{2,6},{4,0},{6,2},{8,12},{10,14},{12,8},{14,10},{16,20},{18,... | collective-permute-start | bytes 2162696 | tf_op jit(solution)/shard_map/ppermute | solution.py:546
  495.5 36.6 %collective-permute-start.52 = (bf16[512,1408]{1,0:T(8,128)(2,1)}, bf16[512,1408]{1,0:T(8,128)(2,1)}, u32[]{:S(2)}, u32[]{:S(2)}) collective-permute-start(bf16[512,1408]{1,0:T(8,128)(2,1)} %add_convert_fusion), channel_id=1, source_target_pairs={{0,8},{2,10},{4,12},{6,14},{8,16},{10,18},{12,20},{14,22},{16,24},... | collective-permute-start | bytes 4325384 | tf_op jit(solution)/shard_map/ppermute | solution.py:549
  500.4 46.0 %collective-permute-start.55 = (bf16[256,1408]{1,0:T(8,128)(2,1)}, bf16[256,1408]{1,0:T(8,128)(2,1)}, u32[]{:S(2)}, u32[]{:S(2)}) collective-permute-start(bf16[256,1408]{1,0:T(8,128)(2,1)} %add_convert_fusion.12), channel_id=1, source_target_pairs={{0,8},{2,10},{4,12},{6,14},{8,16},{10,18},{12,20},{14,22},{16,24},... | collective-permute-start | bytes 2162696 | tf_op jit(solution)/shard_map/ppermute | solution.py:549
  504.1 65.0 %collective-permute-start.46 = (bf16[256,1408]{1,0:T(8,128)(2,1)}, bf16[256,1408]{1,0:T(8,128)(2,1)}, u32[]{:S(2)}, u32[]{:S(2)}) collective-permute-start(bf16[256,1408]{1,0:T(8,128)(2,1)} %get-tuple-element.469), channel_id=1, source_target_pairs={{0,4},{2,6},{4,0},{6,2},{8,12},{10,14},{12,8},{14,10},{16,20},{18,... | collective-permute-start | bytes 2162696 | tf_op jit(solution)/shard_map/ppermute | solution.py:546
  548.9 24.9 %collective-permute-start.56 = (bf16[256,1408]{1,0:T(8,128)(2,1)}, bf16[256,1408]{1,0:T(8,128)(2,1)}, u32[]{:S(2)}, u32[]{:S(2)}) collective-permute-start(bf16[256,1408]{1,0:T(8,128)(2,1)} %add_convert_fusion.11), channel_id=1, source_target_pairs={{0,8},{2,10},{4,12},{6,14},{8,16},{10,18},{12,20},{14,22},{16,24},... | collective-permute-start | bytes 2162696 | tf_op jit(solution)/shard_map/ppermute | solution.py:549
  548.9 24.9 %all-to-all-start.2 = ((bf16[8,32,512]{2,1,0:T(8,128)(2,1)}), bf16[8,32,512]{2,1,0:T(8,128)(2,1)}, u32[]{:S(2)}, u32[]{:S(2)}) async-start(bf16[8,32,512]{2,1,0:T(8,128)(2,1)} %bitcast.68), calls=%async_computation.2 | async-start | bytes 524288 | tf_op jit(solution)/shard_map/all_to_all | solution.py:805
  554.4 60.9 %collective-permute-start.62 = (bf16[256,1408]{1,0:T(8,128)(2,1)}, bf16[256,1408]{1,0:T(8,128)(2,1)}, u32[]{:S(2)}, u32[]{:S(2)}) collective-permute-start(bf16[256,1408]{1,0:T(8,128)(2,1)} %copy-done.117), channel_id=1, source_target_pairs={{0,4},{2,6},{4,0},{6,2},{8,12},{10,14},{12,8},{14,10},{16,20},{18,... | collective-permute-start | bytes 2162696 | tf_op jit(solution)/shard_map/ppermute | solution.py:546
  556.5 58.8 %collective-permute-start.63 = (bf16[256,1408]{1,0:T(8,128)(2,1)}, bf16[256,1408]{1,0:T(8,128)(2,1)}, u32[]{:S(2)}, u32[]{:S(2)}) collective-permute-start(bf16[256,1408]{1,0:T(8,128)(2,1)} %copy-done.116), channel_id=1, source_target_pairs={{0,4},{2,6},{4,0},{6,2},{8,12},{10,14},{12,8},{14,10},{16,20},{18,... | collective-permute-start | bytes 2162696 | tf_op jit(solution)/shard_map/ppermute | solution.py:546
  577.7 39.6 %collective-permute-start.61 = (bf16[256,1408]{1,0:T(8,128)(2,1)}, bf16[256,1408]{1,0:T(8,128)(2,1)}, u32[]{:S(2)}, u32[]{:S(2)}) collective-permute-start(bf16[256,1408]{1,0:T(8,128)(2,1)} %add_convert_fusion.9), channel_id=1, source_target_pairs={{0,8},{2,10},{4,12},{6,14},{8,16},{10,18},{12,20},{14,22},{16,24},... | collective-permute-start | bytes 2162696 | tf_op jit(solution)/shard_map/ppermute | solution.py:549
  580.3 38.5 %collective-permute-start.60 = (bf16[256,1408]{1,0:T(8,128)(2,1)}, bf16[256,1408]{1,0:T(8,128)(2,1)}, u32[]{:S(2)}, u32[]{:S(2)}) collective-permute-start(bf16[256,1408]{1,0:T(8,128)(2,1)} %add_convert_fusion.10), channel_id=1, source_target_pairs={{0,8},{2,10},{4,12},{6,14},{8,16},{10,18},{12,20},{14,22},{16,24},... | collective-permute-start | bytes 2162696 | tf_op jit(solution)/shard_map/ppermute | solution.py:549
  587.4 31.4 %all-to-all-start.3 = ((bf16[8,32,512]{2,1,0:T(8,128)(2,1)}), bf16[8,32,512]{2,1,0:T(8,128)(2,1)S(1)}, u32[]{:S(2)}, u32[]{:S(2)}) async-start(bf16[8,32,512]{2,1,0:T(8,128)(2,1)} %copy-done.96), calls=%async_computation.3 | async-start | bytes 524288 | tf_op jit(solution)/shard_map/all_to_all | solution.py:805
  597.6 46.8 %collective-permute-start.66 = (bf16[256,1408]{1,0:T(8,128)(2,1)}, bf16[256,1408]{1,0:T(8,128)(2,1)}, u32[]{:S(2)}, u32[]{:S(2)}) collective-permute-start(bf16[256,1408]{1,0:T(8,128)(2,1)} %slice.390), channel_id=1, source_target_pairs={{0,4},{2,6},{4,0},{6,2},{8,12},{10,14},{12,8},{14,10},{16,20},{18,... | collective-permute-start | bytes 2162696 | tf_op jit(solution)/shard_map/ppermute | solution.py:546
  615.3 30.3 %collective-permute-start.65 = (bf16[256,1024]{1,0:T(8,128)(2,1)}, bf16[256,1024]{1,0:T(8,128)(2,1)}, u32[]{:S(2)}, u32[]{:S(2)}) collective-permute-start(bf16[256,1024]{1,0:T(8,128)(2,1)} %get-tuple-element.543), channel_id=1, source_target_pairs={{0,4},{2,6},{4,0},{6,2},{8,12},{10,14},{12,8},{14,10},{16,20},{18,... | collective-permute-start | bytes 1572872 | tf_op jit(solution)/shard_map/ppermute | solution.py:546
  615.3 48.4 %collective-permute-start.59 = (bf16[256,1024]{1,0:T(8,128)(2,1)}, bf16[256,1024]{1,0:T(8,128)(2,1)}, u32[]{:S(2)}, u32[]{:S(2)}) collective-permute-start(bf16[256,1024]{1,0:T(8,128)(2,1)} %get-tuple-element.522), channel_id=1, source_target_pairs={{0,4},{2,6},{4,0},{6,2},{8,12},{10,14},{12,8},{14,10},{16,20},{18,... | collective-permute-start | bytes 1572872 | tf_op jit(solution)/shard_map/ppermute | solution.py:546
  617.3 91.8 %collective-permute-start.57 = (bf16[256,1024]{1,0:T(8,128)(2,1)}, bf16[256,1024]{1,0:T(8,128)(2,1)}, u32[]{:S(2)}, u32[]{:S(2)}) collective-permute-start(bf16[256,1024]{1,0:T(8,128)(2,1)} %get-tuple-element.520), channel_id=1, source_target_pairs={{0,4},{2,6},{4,0},{6,2},{8,12},{10,14},{12,8},{14,10},{16,20},{18,... | collective-permute-start | bytes 1572872 | tf_op jit(solution)/shard_map/ppermute | solution.py:546
  621.0 24.7 %collective-permute-start.64 = (bf16[256,1408]{1,0:T(8,128)(2,1)S(1)}, bf16[256,1408]{1,0:T(8,128)(2,1)S(1)}, u32[]{:S(2)}, u32[]{:S(2)}) collective-permute-start(bf16[256,1408]{1,0:T(8,128)(2,1)S(1)} %add_convert_fusion.8), channel_id=1, source_target_pairs={{0,8},{2,10},{4,12},{6,14},{8,16},{10,18},{12,20},{14,22},{16,24},... | collective-permute-start | bytes 2162696 | tf_op jit(solution)/shard_map/ppermute | solution.py:549
  644.4 67.5 %collective-permute-start.58 = (bf16[256,1024]{1,0:T(8,128)(2,1)}, bf16[256,1024]{1,0:T(8,128)(2,1)}, u32[]{:S(2)}, u32[]{:S(2)}) collective-permute-start(bf16[256,1024]{1,0:T(8,128)(2,1)} %get-tuple-element.521), channel_id=1, source_target_pairs={{0,4},{2,6},{4,0},{6,2},{8,12},{10,14},{12,8},{14,10},{16,20},{18,... | collective-permute-start | bytes 1572872 | tf_op jit(solution)/shard_map/ppermute | solution.py:546
  666.5 47.2 %collective-permute-start.67 = (bf16[256,1024]{1,0:T(8,128)(2,1)}, bf16[256,1024]{1,0:T(8,128)(2,1)}, u32[]{:S(2)}, u32[]{:S(2)}) collective-permute-start(bf16[256,1024]{1,0:T(8,128)(2,1)} %get-tuple-element.574), channel_id=1, source_target_pairs={{0,4},{2,6},{4,0},{6,2},{8,12},{10,14},{12,8},{14,10},{16,20},{18,... | collective-permute-start | bytes 1572872 | tf_op jit(solution)/shard_map/ppermute | solution.py:546
  674.6 51.0 %collective-permute-start.70 = (bf16[256,1408]{1,0:T(8,128)(2,1)}, bf16[256,1408]{1,0:T(8,128)(2,1)}, u32[]{:S(2)}, u32[]{:S(2)}) collective-permute-start(bf16[256,1408]{1,0:T(8,128)(2,1)} %add_convert_fusion.7), channel_id=1, source_target_pairs={{0,8},{2,10},{4,12},{6,14},{8,16},{10,18},{12,20},{14,22},{16,24},... | collective-permute-start | bytes 2162696 | tf_op jit(solution)/shard_map/ppermute | solution.py:549
  676.3 49.3 %collective-permute-start.71 = (bf16[256,2048]{1,0:T(8,128)(2,1)}, bf16[256,2048]{1,0:T(8,128)(2,1)}, u32[]{:S(2)}, u32[]{:S(2)}) collective-permute-start(bf16[256,2048]{1,0:T(8,128)(2,1)} %add_convert_fusion.4), channel_id=1, source_target_pairs={{0,2},{2,0},{4,6},{6,4},{8,10},{10,8},{12,14},{14,12},{16,18},{18,... | collective-permute-start | bytes 3145736 | tf_op jit(solution)/shard_map/ppermute | solution.py:543
  712.2 24.1 %collective-permute-start.75 = (bf16[256,1024]{1,0:T(8,128)(2,1)S(1)}, bf16[256,1024]{1,0:T(8,128)(2,1)S(1)}, u32[]{:S(2)}, u32[]{:S(2)}) collective-permute-start(bf16[256,1024]{1,0:T(8,128)(2,1)S(1)} %copy-done.123), channel_id=1, source_target_pairs={{0,4},{2,6},{4,0},{6,2},{8,12},{10,14},{12,8},{14,10},{16,20},{18,... | collective-permute-start | bytes 1572872 | tf_op jit(solution)/shard_map/ppermute | solution.py:546
  713.7 49.7 %collective-permute-start.80 = (bf16[128,1408]{1,0:T(8,128)(2,1)S(1)}, bf16[128,1408]{1,0:T(8,128)(2,1)S(1)}, u32[]{:S(2)}, u32[]{:S(2)}) collective-permute-start(bf16[128,1408]{1,0:T(8,128)(2,1)S(1)} %copy-done.163), channel_id=1, source_target_pairs={{0,2},{2,0},{4,6},{6,4},{8,10},{10,8},{12,14},{14,12},{16,18},{18,... | collective-permute-start | bytes 1081352 | tf_op jit(solution)/shard_map/ppermute | solution.py:543
  724.2 39.6 %collective-permute-start.74 = (bf16[256,1024]{1,0:T(8,128)(2,1)S(1)}, bf16[256,1024]{1,0:T(8,128)(2,1)S(1)}, u32[]{:S(2)}, u32[]{:S(2)}) collective-permute-start(bf16[256,1024]{1,0:T(8,128)(2,1)S(1)} %copy-done.121), channel_id=1, source_target_pairs={{0,4},{2,6},{4,0},{6,2},{8,12},{10,14},{12,8},{14,10},{16,20},{18,... | collective-permute-start | bytes 1572872 | tf_op jit(solution)/shard_map/ppermute | solution.py:546
  730.9 23.5 %collective-permute-start.76 = (bf16[256,1024]{1,0:T(8,128)(2,1)S(1)}, bf16[256,1024]{1,0:T(8,128)(2,1)S(1)}, u32[]{:S(2)}, u32[]{:S(2)}) collective-permute-start(bf16[256,1024]{1,0:T(8,128)(2,1)S(1)} %add_convert_fusion.17), channel_id=1, source_target_pairs={{0,8},{2,10},{4,12},{6,14},{8,16},{10,18},{12,20},{14,22},{16,24},... | collective-permute-start | bytes 1572872 | tf_op jit(solution)/shard_map/ppermute | solution.py:549
  736.3 28.2 %collective-permute-start.84 = (bf16[256,2048]{1,0:T(8,128)(2,1)S(1)}, bf16[256,2048]{1,0:T(8,128)(2,1)S(1)}, u32[]{:S(2)}, u32[]{:S(2)}) collective-permute-start(bf16[256,2048]{1,0:T(8,128)(2,1)S(1)} %copy-done.151), channel_id=1, source_target_pairs={{0,2},{2,0},{4,6},{6,4},{8,10},{10,8},{12,14},{14,12},{16,18},{18,... | collective-permute-start | bytes 3145736 | tf_op jit(solution)/shard_map/ppermute | solution.py:543
  763.4 26.5 %collective-permute-start.89 = (bf16[128,1408]{1,0:T(8,128)(2,1)}, bf16[128,1408]{1,0:T(8,128)(2,1)S(1)}, u32[]{:S(2)}, u32[]{:S(2)}) collective-permute-start(bf16[128,1408]{1,0:T(8,128)(2,1)} %select_convert_fusion.1), channel_id=1, source_target_pairs={{0,2},{2,0},{4,6},{6,4},{8,10},{10,8},{12,14},{14,12},{16,18},{18,... | collective-permute-start | bytes 1081352 | tf_op jit(solution)/shard_map/ppermute | solution.py:543
  763.9 26.1 %collective-permute-start.86 = (bf16[256,1024]{1,0:T(8,128)(2,1)}, bf16[256,1024]{1,0:T(8,128)(2,1)}, u32[]{:S(2)}, u32[]{:S(2)}) collective-permute-start(bf16[256,1024]{1,0:T(8,128)(2,1)} %get-tuple-element.643), channel_id=1, source_target_pairs={{0,4},{2,6},{4,0},{6,2},{8,12},{10,14},{12,8},{14,10},{16,20},{18,... | collective-permute-start | bytes 1572872 | tf_op jit(solution)/shard_map/ppermute | solution.py:546
  764.6 25.4 %collective-permute-start.88 = (bf16[256,1024]{1,0:T(8,128)(2,1)}, bf16[256,1024]{1,0:T(8,128)(2,1)}, u32[]{:S(2)}, u32[]{:S(2)}) collective-permute-start(bf16[256,1024]{1,0:T(8,128)(2,1)} %add_convert_fusion.13), channel_id=1, source_target_pairs={{0,8},{2,10},{4,12},{6,14},{8,16},{10,18},{12,20},{14,22},{16,24},... | collective-permute-start | bytes 1572872 | tf_op jit(solution)/shard_map/ppermute | solution.py:549
  787.3 30.9 %collective-permute-start.91 = (bf16[128,1408]{1,0:T(8,128)(2,1)}, bf16[128,1408]{1,0:T(8,128)(2,1)}, u32[]{:S(2)}, u32[]{:S(2)}) collective-permute-start(bf16[128,1408]{1,0:T(8,128)(2,1)} %select_convert_fusion), channel_id=1, source_target_pairs={{0,2},{2,0},{4,6},{6,4},{8,10},{10,8},{12,14},{14,12},{16,18},{18,... | collective-permute-start | bytes 1081352 | tf_op jit(solution)/shard_map/ppermute | solution.py:543
  789.9 31.8 %collective-permute-start.85 = (bf16[256,2048]{1,0:T(8,128)(2,1)S(1)}, bf16[256,2048]{1,0:T(8,128)(2,1)S(1)}, u32[]{:S(2)}, u32[]{:S(2)}) collective-permute-start(bf16[256,2048]{1,0:T(8,128)(2,1)S(1)} %add_convert_fusion.2.mine), channel_id=1, source_target_pairs={{0,1},{1,0},{2,3},{3,2},{4,5},{5,4},{6,7},{7,6},{8,9},{9,8},{10,11... | collective-permute-start | bytes 3145736 | tf_op jit(solution)/shard_map/ppermute | solution.py:552
  (219 other events, 2085.6 us)

commit v3 on v2

--- a/solution.py
+++ b/solution.py
@@ -641,9 +641,16 @@
             self.done += 1
             return value
 
+        def ready(self):
+            self.value = self.add().astype(LOW)
+
+        def fly(self):
+            self.flown = ring(self.value)
+
         def hop(self):
             if self.done < laps - 1:
-                self.flown = ring(self.add().astype(LOW))
+                self.ready()
+                self.fly()
 
         def last(self):
             while self.done < laps - 1:
@@ -670,9 +677,9 @@
                 parts_call(self.pairs, [[p, laps + p] for p in self.turn[1:]], wide, FULL)
             )
 
-        def fly(self):
+        def begin(self):
             self.done = 1
-            self.flown = ring(self.value)
+            self.fly()
 
         def add(self):
             value = self.owns[self.done] + self.flown
@@ -744,20 +751,23 @@
     keys.ring()
     keys.side()
     got = pair(other)
-    mine_b, other_b = split(w_ff_gate, w_ff_up, turned_over(w_ff_down))
+    mine_b, other_b = split(w_ff_gate, w_ff_up)
+    mine_d, other_d = split(turned_over(w_ff_down))
     rank_weight = jnp.concatenate(
         [lax.dynamic_slice_in_dim(w_rank_in, order[i] * wide, wide, 0) for i in range(groups)], axis=0
     )
-    far, near, mine_b, other_b, rank_weight = together(
-        (keys.blocks, 2), (keys.others, 0), far, near, mine_b, other_b, rank_weight
+    far, near, mine_b, other_b, mine_d, other_d, rank_weight = together(
+        (keys.blocks, 2), (keys.others, 0), far, near, mine_b, other_b, mine_d, other_d, rank_weight
     )
     keys.rest()
     keys.side()
     other = twin(far)
-    got_b = pair(other_b)
     first = spread_all(first_own, far, near, other)
-    first, got = together((keys.blocks, laps - 1), (keys.others, 1), first, got)
+    first, got, other_b, other_d = together(
+        (keys.blocks, laps - 1), (keys.others, 1), first, got, other_b, other_d
+    )
     keys.side(laps)
+    got_d = pair(other_d)
     gates = Gather(joined(mine, got))
     gates.ring()
     rank_in = dot(first, rank_weight).astype(LOW)
@@ -765,7 +775,7 @@
     bias = jnp.where(left, decay_bias[:DK], decay_bias[DK:])
     logits = dot(rank_in, rank_out) + bias
     decay = jax.nn.log_sigmoid(logits) / 16.0
-    first, rank_in, decay, logits = together(
+    first, rank_in, decay, logits, got_d = together(
         *[(keys.others, i) for i in range(2, laps)],
         (gates.blocks, 0),
         (gates.blocks, 1),
@@ -773,10 +783,14 @@
         rank_in,
         decay,
         logits,
-
-    )
+        got_d,
+
+    )
+    got_b = pair(other_b)
     gates.ring()
     gates.side()
+    downs = GatherSide(joined(mine_d, got_d))
+    downs.begin()
     arrays, places = keys.pieces()
     span = [(0, DV + DK)]
     keyed, full_k = assemble_call(
@@ -795,7 +809,9 @@
         outputs=[(shape_of(DK, DV + LANES, dtype=LOW), (DK, DV + LANES), None)],
         scratch=[state_scratch, row_scratch, pltpu.VMEM((DK, LANES), FULL)],
     )
-    summary, got_b = together((gates.blocks, 2), (gates.others, 0), summary, got_b)
+    summary, got_b, downs.blocks[0] = together(
+        (gates.blocks, 2), (gates.others, 0), (downs, "got"), summary, got_b, downs.blocks[0]
+    )
     gates.rest()
     gates.side()
     halves_of_seq = [[i for i in range(peers) if i % 2 == k] for k in range(2)]
@@ -805,22 +821,19 @@
         return lax.all_to_all(x, "seq", 0, 0, axis_index_groups=halves_of_seq, tiled=True)
 
     pieces = turned(summary).reshape(groups, slab, DV + LANES)
-    pair_b = joined(mine_b, got_b)
-    ffs = Gather(pair_b[:, : 2 * ff])
-    downs = GatherSide(pair_b[:, 2 * ff :])
-    downs.begin()
+    ffs = Gather(joined(mine_b, got_b))
+    downs.join()
     cot_far, cot_near = spread_near(cot_own)
     pieces, ffs.blocks[0], cot_far, cot_near = together(
         (gates.blocks, laps - 1),
         (gates.others, 1),
-        (downs, "got"),
+        (downs.blocks, 0),
         pieces,
         ffs.blocks[0],
         cot_far,
         cot_near,
     )
     gates.side(laps)
-    downs.join()
     ffs.ring()
     cot_other = twin(cot_far)
     entering = turned(chain_call(pieces, pieces, False).reshape(DK, DV))
@@ -890,10 +903,11 @@
     )
     down_grad = ReduceSide((cot, inner))
     down_grad.make()
+    down_grad.make_own()
     inner, ff_both, cot, second = together(
-        (downs.blocks, laps - 1), (down_grad, "value"), inner, ff_both, cot, second
-    )
-    down_grad.fly()
+        (downs.blocks, laps - 1), (down_grad, "value"), (down_grad, "owns"), inner, ff_both, cot, second
+    )
+    down_grad.begin()
     down_grad.pairs = ((cot, inner),)
     arrays, places = downs.pieces()
     both_back, full_d = assemble_call(
@@ -913,14 +927,12 @@
     gate_grad.pairs = ((second, both_back[:, :ff]),)
     got = pair(far)
     gate_grad.send(2)
-    down_grad.make_own()
     down_grad.hop()
     near = near_part((both_back, full_f))
     up_grad = Reduce((second, both_back[:, ff:]))
     up_grad.make()
     got, near, both_back, second = together(
         (down_grad, "flown"),
-        (down_grad, "owns"),
         (up_grad, "parts"),
         (gate_grad.sent, 0),
         (gate_grad.sent, 1),
@@ -951,7 +963,13 @@
     gate_grad.make_own()
     up_grad.make_own()
     far, near, back_own = together(
-        (gate_grad, "owns"), (up_grad, "owns"), (gate_grad.sent, 2), far, near, back_own
+        (gate_grad, "owns"),
+        (up_grad, "owns"),
+        (down_grad, "flown"),
+        *[(gate_grad.sent, i) for i in range(2, laps)],
+        far,
+        near,
+        back_own,
     )
     other = twin(far)
     resid_back, full_d, inner, full_o, gate_grad.sent[0] = together(
@@ -981,8 +999,8 @@
     )
     summary_back, resid_back, gate_back, first, gated = together(
         (up_grad.sent, 0),
+        (up_grad, "parts"),
         (down_grad, "flown"),
-        *[(gate_grad.sent, i) for i in range(3, laps)],
         (gate_grad, "flown"),
         summary_back,
         resid_back,
@@ -995,10 +1013,14 @@
     pieces_back = turned(summary_back).reshape(groups, slab, DV)
     out_grad = Reduce((resid_back, gated), (first, gate_back))
     out_grad.make()
+    up_grad.ready()
     pieces_back, full_d, inner, resid_back, gate_back, first, gated = together(
         (up_grad.sent, 1),
+        (up_grad, "parts"),
+        (down_grad, "flown"),
         (gate_grad, "flown"),
         (out_grad, "parts"),
+        (up_grad, "value"),
         pieces_back,
         full_d,
         inner,
@@ -1011,23 +1033,25 @@
         chain_call(pieces, pieces_back, True), gate_grad.flown, up_grad.sent[0]
     )
     out_grad.pairs = ((resid_back, gated), (first, gate_back))
-    up_grad.send(laps)
-    gate_grad.hop()
-    up_grad.hop()
+    up_grad.send()
+    up_grad.fly()
+    out_grad.make_own()
     leaving = turned(leaving.reshape(DK, DV))
     out_far, out_near = far_part((inner, full_d)), near_part((inner, full_d))
     leaving, keyed, out_far, out_near = together(
-        (gate_grad, "flown"),
         (up_grad, "flown"),
-        *[(up_grad.sent, i) for i in range(2, laps)],
+        (out_grad, "owns"),
+        (out_grad, "parts"),
+        (up_grad.sent, 2),
+        (up_grad, "parts"),
+        (down_grad, "flown"),
         leaving,
         keyed,
         out_far,
         out_near,
     )
-    down_grad.cross()
-    out_grad.send()
-    up_grad.hop()
+    out_grad.send(2)
+    gate_grad.hop()
     mixes_back, grad_logits, grad_bias = call(
         mix_back_kernel,
         reverse=True,
@@ -1049,9 +1073,10 @@
         scratch=[state_scratch],
     )
     mixes_back, grad_logits, first, resid_back, gate_back, full_k, full_q, full_g = together(
-        (up_grad, "flown"),
+        (gate_grad, "flown"),
         (out_grad.sent, 0),
-        (down_grad, "come"),
+        (up_grad, "parts"),
+        (down_grad, "flown"),
         mixes_back,
         grad_logits,
         first,
@@ -1062,7 +1087,9 @@
         full_g,
     )
     out_grad.pairs = ((resid_back, gated), (first, gate_back))
-    out_grad.send(2)
+    up_grad.send(laps)
+    up_grad.hop()
+    down_grad.cross()
     mix_grad = Reduce((first, mixes_back))
     mix_grad.make()
     full_vkq = jnp.concatenate([full_k, full_q], axis=1)
@@ -1081,49 +1108,71 @@
     )
     far = far_part(*back_pairs)
     far, first, back_pairs, resid_back, gate_back, gated = together(
-        (out_grad.sent, 1), (mix_grad, "parts"), far, first, list(back_pairs), resid_back, gate_back, gated
-    )
-    far, first, back_pairs, resid_back, gate_back, gated, grad_logits, up_grad.flown = together(
-        summed_pair(*far).astype(LOW), first, back_pairs, resid_back, gate_back, gated, grad_logits, up_grad.flown
+        (out_grad.sent, 1),
+        (up_grad, "flown"),
+        (mix_grad, "parts"),
+        far,
+        first,
+        list(back_pairs),
+        resid_back,
+        gate_back,
+        gated,
+    )
+    up_grad.ready()
+    out_grad.ready()
+    far, first, back_pairs, grad_logits, out_far, out_near = together(
+        (up_grad, "value"),
+        (out_grad, "value"),
+        summed_pair(*far).astype(LOW),
+        first,
+        back_pairs,
+        grad_logits,
+        out_far,
+        out_near,
     )
     mixes_back, rank_high, rank_low = back_pairs[0][0], back_pairs[2][0], back_pairs[3][0]
     mix_grad.pairs = ((first, mixes_back),)
-    out_grad.pairs = ((resid_back, gated), (first, gate_back))
     got = pair(far)
-    out_grad.send(laps)
+    out_grad.send()
     mix_grad.send()
-    out_grad.make_own()
-    out_grad.hop()
-    up_grad.hop()
+    out_grad.fly()
+    up_grad.fly()
     near = near_part(*back_pairs)
     mix_grad.make_own()
-    grad_rank_in = dot(rank_high, first, TN) + dot(rank_low, first, TN)
-    grad_rank_out = lax.dot_general(
-        rank_in.astype(FULL), grad_logits, (TN, ((), ())), precision=precise
-    )
-    got, near, grad_rank_in, grad_rank_out, out_far, out_near = together(
-        *[(out_grad.sent, i) for i in range(2, laps)],
+    got, near, rank_high, rank_low, first, rank_in, grad_logits, out_far, out_near = together(
+        *[(up_grad.sent, i) for i in range(3, laps)],
+        (down_grad, "come"),
+        (out_grad.sent, 2),
         (mix_grad.sent, 0),
         (mix_grad, "owns"),
         (out_grad, "flown"),
         (up_grad, "flown"),
         got,
         near,
-        grad_rank_in,
-        grad_rank_out,
-        summed_pair(*out_far).astype(LOW),
-        summed_pair(*out_near),
-    )
+        rank_high,
+        rank_low,
+        first,
+        rank_in,
+        grad_logits,
+        out_far,
+        out_near,
+    )
+    out_far, out_near = summed_pair(*out_far).astype(LOW), summed_pair(*out_near)
     mix_grad.send()
     mix_grad.hop()
+    out_grad.send(laps)
     out_grad.hop()
-    out_got = pair(out_far)
+    grad_rank_in = dot(rank_high, first, TN) + dot(rank_low, first, TN)
+    grad_rank_out = lax.dot_general(
+        rank_in.astype(FULL), grad_logits, (TN, ((), ())), precision=precise
+    )
     hidden_norm, grad_gain_attn = norm_back(summed_pair(*near) + got, hidden, scale_attn, gain_attn)
     input_own = grad_resid + hidden_norm
     input_own, grad_gain_attn = together(
         (mix_grad.sent, 1), (mix_grad, "flown"), (out_grad, "flown"), input_own, grad_gain_attn
     )
-    mix_grad.send()
+    out_got = pair(out_far)
+    mix_grad.send(laps)
     mix_grad.hop()
     down_grad.last()
     down_grad.halve()
@@ -1159,7 +1208,6 @@
         hop = hops.pop(0)
         return small + lax.ppermute(small, "seq", [(i, i ^ hop) for i in range(peers)])
 
-    mix_grad.send(laps)
     mix_grad.hop()
     out_grad.hop()
     small = summed(small)

time: 838 us -> 829 us (0.989)
  waiting for transfers between devices: 318 us -> 286 us
  starting transfers between devices: 88.3 us -> 106 us
  local copies, waits for them, and re-layouts: 98.2 us -> 112 us
    ppermute x27, waiting for transfers between devices: 137 us -> 85.6 us  [ring(): return lax.ppermute(x, 'seq', [(i, (i + 4) % peers) for i in range(peers)])]
    unnamed x382 -> x384, local copies, waits for them, and re-layouts: 77.2 us -> 93.2 us
    all_to_all x4, waiting for transfers between devices: 28.7 us -> 41.4 us  [turned(): lax.all_to_all(x, 'seq', 0, 0, axis_index_groups=halves_of_seq, tiled=True)]
    ppermute x30, starting transfers between devices: 30.8 us -> 40.7 us  [side(): return lax.ppermute(x, 'seq', [(i, i ^ 2) for i in range(peers)])]
    ppermute x16 -> x17, waiting for transfers between devices: 18.5 us -> 25.7 us  [pair(): return lax.ppermute(x, 'seq', [(i, i ^ 1) for i in range(peers)])]
    ppermute x16 -> x17, starting transfers between devices: 17.8 us -> 20.2 us  [pair(): return lax.ppermute(x, 'seq', [(i, i ^ 1) for i in range(peers)])]
  transfers between devices with their start and end apart: 101 -> 102, of which waited for: 40 -> 42; matrix products, arithmetic and copies ran while one was open for 15% -> 13% of each run, Pallas kernels for 23% -> 25%
where the time goes in v3:
time: 829 us; the launch traced here: 819 us
  waiting for transfers between devices  286 us (34%)
  Pallas kernels  203 us (24%)
  local copies, waits for them, and re-layouts  112 us (14%)
  starting transfers between devices  106 us (13%)
  other arithmetic  87.8 us (11%)
  between operations  14.1 us (2%)
  matrix products  9.92 us (1%)
    ppermute x30, waiting for transfers between devices, side(): return lax.ppermute(x, 'seq', [(i, i ^ 2) for i in range(peers)])  118 us
    unnamed x384, local copies, waits for them, and re-layouts  93.2 us
    ppermute x27, waiting for transfers between devices, ring(): return lax.ppermute(x, 'seq', [(i, (i + 4) % peers) for i in range(peers)])  85.6 us
    pallas_call x10, Pallas kernels, parts_call(): pl.pallas_call(functools.partial(parts_kernel, len(pairs), [(j, i) for j,...  55.2 us
    pallas_call x4, Pallas kernels, assemble_call(): pl.pallas_call(kernel, grid=(x.shape[0] // tile,), in_specs=[rows(x.shape...  52.8 us
    pallas_call x4, Pallas kernels, token_call(): pl.pallas_call(kernel, grid_spec=pltpu.PrefetchScalarGridSpec(num_scalar_...  42.7 us
    all_to_all x4, waiting for transfers between devices, turned(): lax.all_to_all(x, 'seq', 0, 0, axis_index_groups=halves_of_seq, tiled=True)  41.4 us
    pallas_call x8, Pallas kernels, product_call(): pl.pallas_call(functools.partial(product_kernel, len(pairs)), grid=(width...  40.9 us
  transfers between devices with their start and end apart: 102, of which 42 were waited for; matrix products, arithmetic and copies ran while one was open for 13% of the time, Pallas kernels for 25%

profile of v3, /device:TPU:0, one launch (start us, length us, event | category | flops | bytes accessed | tf_op | source)
XLA Modules:
  0.0 819.0 jit_solution(4551750526513901153)
XLA Ops:
  2.6 3.0 collective-permute-start
  27.5 4.9 collective-permute-done.1.refs_1_
  39.5 7.8 collective-permute-done.2.refs_2_
  50.3 3.4 pad_maximum_fusion.x_ref.refs_1_.refs_0_
  53.8 5.4 collective-permute-done.10
  66.8 3.4 fusion.52
  72.1 3.0 collective-permute-done.6.refs_6_
  76.4 5.4 collective-permute-done.11.refs_7_
  91.1 7.9 shard_map.388
  100.9 8.1 shard_map.389
  109.9 6.5 collective-permute-done.15.refs_4_
  117.5 4.1 all-to-all-start
  126.8 3.4 collective-permute-done.20.refs_5_
  130.2 7.5 all-to-all-done.pieces_ref.local_ref
  140.7 5.5 all-to-all-start.1
  148.2 7.4 collective-permute-done.18.refs_6_
  155.6 22.5 %all-to-all-done.1 = bf16[8,32,512]{2,1,0:T(8,128)(2,1)S(1)} async-done(((bf16[8,32,512]{2,1,0:T(8,128)(2,1)}), bf16[8,32,512]{2,1,0:T(8,128)(2,1)S(1)}, u32[]{:S(2)}, u32[]{:S(2)}) %all-to-all-start.1) | async-done | bytes 262176 | tf_op jit(solution)/shard_map/all_to_all | solution.py:821
  181.2 9.5 %shard_map.391 = (f32[1024,768]{1,0:T(8,128)}, bf16[2048,512]{1,0:T(8,128)(2,1)}, bf16[2048,256]{1,0:T(8,128)(2,1)}, bf16[2048,512]{1,0:T(8,128)(2,1)}) custom-call(bf16[1024,2048]{1,0:T(8,128)(2,1)} %pad_maximum_fusion.x_ref.refs_1_.refs_0_, bf16[256,1280]{1,0:T(8,128)(2,1)S(1)} %copy-done.56, bf16[256,1280]{1,0:T(8,128)(2,1)} %collective-permute-done.12.refs_1_, ...), custom_call_target="tpu_custom_call" | custom-call | flops 1 | bytes 1 | tf_op jit(solution)/shard_map/pallas_call | solution.py:402
  192.6 10.4 %shard_map.392 = (f32[1024,512]{1,0:T(8,128)S(1)}, bf16[1024,512]{1,0:T(8,128)(2,1)S(1)}, f32[8,256,512]{2,1,0:T(8,128)}) custom-call(s32[26]{0:T(128)S(1)} %concatenate.104.info, f32[1024,768]{1,0:T(8,128)S(1)} %copy-done.7, f32[1024,768]{1,0:T(8,128)S(1)} %copy-done.5, f32[1024,768]{1,0:T(8,128)S(1)} %copy-done.5, f32[1024,768]{1,0:T(8,128)S(1)} %copy-done.7, ...), custom_call_target="tpu_custom_call" | custom-call | flops 1 | bytes 1 | tf_op jit(solution)/shard_map/pallas_call | solution.py:255
  203.0 4.5 pad_maximum_fusion.1.refs_0_.x_ref
  207.5 8.1 collective-permute-done.26.refs_2_
  224.1 27.8 %collective-permute-done.29.refs_5_ = bf16[256,2816]{1,0:T(8,128)(2,1)S(1)} collective-permute-done((bf16[256,2816]{1,0:T(8,128)(2,1)}, bf16[256,2816]{1,0:T(8,128)(2,1)S(1)}, u32[]{:S(2)}, u32[]{:S(2)}) %collective-permute-start.29) | collective-permute-done | bytes 1441824 | tf_op jit(solution)/shard_map/ppermute | solution.py:546
  260.5 29.5 %collective-permute-done.35.refs_1_ = bf16[512,1408]{1,0:T(8,128)(2,1)S(1)} collective-permute-done((bf16[512,1408]{1,0:T(8,128)(2,1)S(1)}, bf16[512,1408]{1,0:T(8,128)(2,1)S(1)}, u32[]{:S(2)}, u32[]{:S(2)}) %collective-permute-start.35) | collective-permute-done | bytes 1441824 | tf_op jit(solution)/shard_map/ppermute | solution.py:549
  295.1 24.2 %collective-permute-done.33.refs_7_ = bf16[256,2816]{1,0:T(8,128)(2,1)S(1)} collective-permute-done((bf16[256,2816]{1,0:T(8,128)(2,1)S(1)}, bf16[256,2816]{1,0:T(8,128)(2,1)S(1)}, u32[]{:S(2)}, u32[]{:S(2)}) %collective-permute-start.33) | collective-permute-done | bytes 1441824 | tf_op jit(solution)/shard_map/ppermute | solution.py:546
  319.4 5.8 collective-permute-done.38.refs_2_
  325.2 21.4 %shard_map.395 = (f32[1024,2816]{1,0:T(8,128)}, bf16[2048,2816]{1,0:T(8,128)(2,1)}, bf16[1024,1408]{1,0:T(8,128)(2,1)}) custom-call(bf16[1024,2048]{1,0:T(8,128)(2,1)} %pad_maximum_fusion.2.x_ref.refs_0_, bf16[256,2816]{1,0:T(8,128)(2,1)} %pad_maximum_fusion.5.refs_0_, bf16[256,2816]{1,0:T(8,128)(2,1)} %collective-permute-done.24.refs_1_, ...), custom_call_target="tpu_custom_call" | custom-call | flops 1 | bytes 1 | tf_op jit(solution)/shard_map/pallas_call | solution.py:402
  348.4 8.6 %shard_map.397 = (f32[512,1408]{1,0:T(8,128)S(1)}, f32[512,1408]{1,0:T(8,128)S(1)}, f32[512,1408]{1,0:T(8,128)S(1)}) custom-call(s32[6]{0:T(128)S(1)} %copy-done.114, bf16[1024,2048]{1,0:T(8,128)(2,1)} %pad_maximum_fusion.1.refs_0_.x_ref, bf16[1024,1408]{1,0:T(8,128)(2,1)S(1)} %copy-done.11), custom_call_target="tpu_custom_call" | custom-call | flops 1 | bytes 1 | tf_op jit(solution)/shard_map/pallas_call | solution.py:380
  358.7 4.0 shard_map.396
  363.1 14.0 %shard_map.398 = (bf16[1024,2816]{1,0:T(8,128)(2,1)}, bf16[2048,1408]{1,0:T(8,128)(2,1)}) custom-call(bf16[1024,2048]{1,0:T(8,128)(2,1)} %pad_maximum_fusion.1.refs_0_.x_ref, f32[1024,2816]{1,0:T(8,128)} %get-tuple-element.469.pre_ref, bf16[512,1408]{1,0:T(8,128)(2,1)S(1)} %copy-done.40, bf16[512,1408]{1,0:T(8,128)(2,1)} %copy-done.145, ...), custom_call_target="tpu_custom_call" | custom-call | flops 1 | bytes 1 | tf_op jit(solution)/shard_map/pallas_call | solution.py:402
  379.8 8.8 %shard_map.400 = (f32[256,2048]{1,0:T(8,128)S(1)}, bf16[256,2048]{1,0:T(8,128)(2,1)S(1)}) custom-call(bf16[1024,2816]{1,0:T(8,128)(2,1)S(1)} %copy-done.6, bf16[2048,2816]{1,0:T(8,128)(2,1)} %get-tuple-element.498.refs_1_), custom_call_target="tpu_custom_call" | custom-call | flops 1 | bytes 1 | tf_op jit(solution)/shard_map/pallas_call | solution.py:338
  390.8 6.4 shard_map.399
  408.2 8.8 %shard_map.402 = (f32[256,2048]{1,0:T(8,128)S(1)}, bf16[256,2048]{1,0:T(8,128)(2,1)S(1)}) custom-call(bf16[1024,2816]{1,0:T(8,128)(2,1)S(1)} %bitcast.65, bf16[2048,2816]{1,0:T(8,128)(2,1)} %get-tuple-element.498.refs_1_), custom_call_target="tpu_custom_call" | custom-call | flops 1 | bytes 1 | tf_op jit(solution)/shard_map/pallas_call | solution.py:338
  417.3 6.4 shard_map.401
  425.6 13.9 %collective-permute-done.45 = bf16[256,1408]{1,0:T(8,128)(2,1)S(1)} collective-permute-done((bf16[256,1408]{1,0:T(8,128)(2,1)}, bf16[256,1408]{1,0:T(8,128)(2,1)S(1)}, u32[]{:S(2)}, u32[]{:S(2)}) %collective-permute-start.45) | collective-permute-done | bytes 720928 | tf_op jit(solution)/shard_map/ppermute | solution.py:546
  445.2 3.8 fusion.35
  451.8 4.2 collective-permute-start.48
  460.8 5.4 shard_map.404
  469.4 5.4 shard_map.403
  475.9 14.9 %collective-permute-done.50 = bf16[256,1408]{1,0:T(8,128)(2,1)} collective-permute-done((bf16[256,1408]{1,0:T(8,128)(2,1)S(1)}, bf16[256,1408]{1,0:T(8,128)(2,1)}, u32[]{:S(2)}, u32[]{:S(2)}) %collective-permute-start.50) | collective-permute-done | bytes 720928 | tf_op jit(solution)/shard_map/ppermute | solution.py:546
  501.3 7.0 shard_map.405
  510.6 7.0 collective-permute-done.55
  519.9 5.3 all-to-all-start.2
  532.1 4.4 shard_map.406
  540.7 3.0 all-to-all-done.2.local_ref
  557.4 4.2 shard_map.410
  564.0 4.2 shard_map.409
  572.4 5.2 all-to-all-start.3
  577.6 3.0 add_convert_fusion.9
  584.8 5.4 shard_map.408
  594.1 8.4 %all-to-all-done.3 = bf16[8,32,512]{2,1,0:T(8,128)(2,1)S(1)} async-done(((bf16[8,32,512]{2,1,0:T(8,128)(2,1)}), bf16[8,32,512]{2,1,0:T(8,128)(2,1)S(1)}, u32[]{:S(2)}, u32[]{:S(2)}) %all-to-all-start.3) | async-done | bytes 262176 | tf_op jit(solution)/shard_map/all_to_all | solution.py:821
  602.5 9.3 %collective-permute-start.61 = (bf16[256,1024]{1,0:T(8,128)(2,1)}, bf16[256,1024]{1,0:T(8,128)(2,1)S(1)}, u32[]{:S(2)}, u32[]{:S(2)}) collective-permute-start(bf16[256,1024]{1,0:T(8,128)(2,1)} %copy-done.128), channel_id=1, source_target_pairs={{0,4},{2,6},{4,0},{6,2},{8,12},{10,14},{12,8},{14,10},{16,20},{18,... | collective-permute-start | bytes 1572872 | tf_op jit(solution)/shard_map/ppermute | solution.py:546
  621.0 17.3 %shard_map.411 = (bf16[1024,1024]{1,0:T(8,128)(2,1)S(1)}, f32[1024,256]{1,0:T(8,128)S(1)}, f32[1,256]{1,0:T(1,128)S(1)}) custom-call(s32[26]{0:T(128)S(1)} %concatenate.104.info, f32[1024,768]{1,0:T(8,128)S(1)} %copy-done.9, f32[1024,768]{1,0:T(8,128)S(1)} %copy-done.5, f32[1024,768]{1,0:T(8,128)S(1)} %copy-done.5, f32[1024,256]{1,0:T(8,128)S(1)} %copy-done.29, ...), custom_call_target="tpu_custom_call" | custom-call | flops 1 | bytes 1 | tf_op jit(solution)/shard_map/pallas_call | solution.py:255
  641.8 5.0 shard_map.412
  650.8 5.3 shard_map.413
  668.6 9.3 %collective-permute-done.63 = bf16[256,1408]{1,0:T(8,128)(2,1)S(1)} collective-permute-done((bf16[256,1408]{1,0:T(8,128)(2,1)S(1)}, bf16[256,1408]{1,0:T(8,128)(2,1)S(1)}, u32[]{:S(2)}, u32[]{:S(2)}) %collective-permute-start.63) | collective-permute-done | bytes 720928 | tf_op jit(solution)/shard_map/ppermute | solution.py:546
  681.7 4.1 shard_map.414
  698.6 5.3 shard_map.415
  716.6 3.1 collective-permute-start.75
  726.2 9.5 %collective-permute-done.75 = bf16[256,1024]{1,0:T(8,128)(2,1)S(1)} collective-permute-done((bf16[256,1024]{1,0:T(8,128)(2,1)S(1)}, bf16[256,1024]{1,0:T(8,128)(2,1)S(1)}, u32[]{:S(2)}, u32[]{:S(2)}) %collective-permute-start.75) | collective-permute-done | bytes 524320 | tf_op jit(solution)/shard_map/ppermute | solution.py:549
  745.9 12.2 %collective-permute-done.79 = bf16[128,1408]{1,0:T(8,128)(2,1)S(1)} collective-permute-done((bf16[128,1408]{1,0:T(8,128)(2,1)S(1)}, bf16[128,1408]{1,0:T(8,128)(2,1)S(1)}, u32[]{:S(2)}, u32[]{:S(2)}) %collective-permute-start.79) | collective-permute-done | bytes 360480 | tf_op jit(solution)/shard_map/ppermute | solution.py:543
  770.9 4.3 shard_map.417
  778.5 7.7 collective-permute-done.87
  792.5 4.4 collective-permute-done.92
  812.3 3.8 shard_map.416
  (689 shorter events, 292.2 us)
Async XLA Ops:
  23.1 24.4 %collective-permute-start.4 = (bf16[256,2048]{1,0:T(8,128)(2,1)}, bf16[256,2048]{1,0:T(8,128)(2,1)}, u32[]{:S(2)}, u32[]{:S(2)}) collective-permute-start(bf16[256,2048]{1,0:T(8,128)(2,1)} %fusion.4), channel_id=1, source_target_pairs={{0,2},{2,0},{4,6},{6,4},{8,10},{10,8},{12,14},{14,12},{16,18},{18,... | collective-permute-start | bytes 3145736 | tf_op jit(solution)/shard_map/ppermute | solution.py:543
  23.6 23.8 %collective-permute-start.5 = (bf16[256,2048]{1,0:T(8,128)(2,1)}, bf16[256,2048]{1,0:T(8,128)(2,1)}, u32[]{:S(2)}, u32[]{:S(2)}) collective-permute-start(bf16[256,2048]{1,0:T(8,128)(2,1)} %fusion.4), channel_id=1, source_target_pairs={{0,1},{1,0},{2,3},{3,2},{4,5},{5,4},{6,7},{7,6},{8,9},{9,8},{10,11... | collective-permute-start | bytes 3145736 | tf_op jit(solution)/shard_map/ppermute | solution.py:552
  62.3 19.5 %collective-permute-start.12 = (bf16[256,1280]{1,0:T(8,128)(2,1)S(1)}, bf16[256,1280]{1,0:T(8,128)(2,1)}, u32[]{:S(2)}, u32[]{:S(2)}) collective-permute-start(bf16[256,1280]{1,0:T(8,128)(2,1)S(1)} %pad_maximum_fusion.11.refs_0_), channel_id=1, source_target_pairs={{0,8},{2,10},{4,12},{6,14},{8,16},{10,18},{12,20},{14,22},{16,24},... | collective-permute-start | bytes 1966088 | tf_op jit(solution)/shard_map/ppermute | solution.py:549
  65.4 43.6 %collective-permute-start.17 = (bf16[128,2816]{1,0:T(8,128)(2,1)}, bf16[128,2816]{1,0:T(8,128)(2,1)}, u32[]{:S(2)}, u32[]{:S(2)}) collective-permute-start(bf16[128,2816]{1,0:T(8,128)(2,1)} %get-tuple-element.408), channel_id=1, source_target_pairs={{0,2},{2,0},{4,6},{6,4},{8,10},{10,8},{12,14},{14,12},{16,18},{18,... | collective-permute-start | bytes 2162696 | tf_op jit(solution)/shard_map/ppermute | solution.py:543
  83.5 32.9 %collective-permute-start.16 = (bf16[256,1408]{1,0:T(8,128)(2,1)}, bf16[256,1408]{1,0:T(8,128)(2,1)}, u32[]{:S(2)}, u32[]{:S(2)}) collective-permute-start(bf16[256,1408]{1,0:T(8,128)(2,1)} %pad_maximum_fusion.10), channel_id=1, source_target_pairs={{0,4},{2,6},{4,0},{6,2},{8,12},{10,14},{12,8},{14,10},{16,20},{18,... | collective-permute-start | bytes 2162696 | tf_op jit(solution)/shard_map/ppermute | solution.py:546
  84.1 24.8 %collective-permute-start.14 = (bf16[256,1280]{1,0:T(8,128)(2,1)}, bf16[256,1280]{1,0:T(8,128)(2,1)}, u32[]{:S(2)}, u32[]{:S(2)}) collective-permute-start(bf16[256,1280]{1,0:T(8,128)(2,1)} %collective-permute-done.12.refs_1_), channel_id=1, source_target_pairs={{0,8},{2,10},{4,12},{6,14},{8,16},{10,18},{12,20},{14,22},{16,24},... | collective-permute-start | bytes 1966088 | tf_op jit(solution)/shard_map/ppermute | solution.py:549
  85.2 31.2 %collective-permute-start.15 = (bf16[256,1280]{1,0:T(8,128)(2,1)S(1)}, bf16[256,1280]{1,0:T(8,128)(2,1)}, u32[]{:S(2)}, u32[]{:S(2)}) collective-permute-start(bf16[256,1280]{1,0:T(8,128)(2,1)S(1)} %pad_maximum_fusion.11.refs_0_), channel_id=1, source_target_pairs={{0,4},{2,6},{4,0},{6,2},{8,12},{10,14},{12,8},{14,10},{16,20},{18,... | collective-permute-start | bytes 1966088 | tf_op jit(solution)/shard_map/ppermute | solution.py:546
  88.6 38.2 %collective-permute-start.21 = (bf16[256,2048]{1,0:T(8,128)(2,1)S(1)}, bf16[256,2048]{1,0:T(8,128)(2,1)}, u32[]{:S(2)}, u32[]{:S(2)}) collective-permute-start(bf16[256,2048]{1,0:T(8,128)(2,1)S(1)} %get-tuple-element.415), channel_id=1, source_target_pairs={{0,2},{2,0},{4,6},{6,4},{8,10},{10,8},{12,14},{14,12},{16,18},{18,... | collective-permute-start | bytes 3145736 | tf_op jit(solution)/shard_map/ppermute | solution.py:543
  109.0 21.2 %collective-permute-start.20 = (bf16[256,1280]{1,0:T(8,128)(2,1)}, bf16[256,1280]{1,0:T(8,128)(2,1)S(1)}, u32[]{:S(2)}, u32[]{:S(2)}) collective-permute-start(bf16[256,1280]{1,0:T(8,128)(2,1)} %collective-permute-done.12.refs_1_), channel_id=1, source_target_pairs={{0,4},{2,6},{4,0},{6,2},{8,12},{10,14},{12,8},{14,10},{16,20},{18,... | collective-permute-start | bytes 1966088 | tf_op jit(solution)/shard_map/ppermute | solution.py:546
  116.4 21.3 %collective-permute-start.19 = (bf16[256,1280]{1,0:T(8,128)(2,1)}, bf16[256,1280]{1,0:T(8,128)(2,1)}, u32[]{:S(2)}, u32[]{:S(2)}) collective-permute-start(bf16[256,1280]{1,0:T(8,128)(2,1)} %collective-permute-done.14.refs_2_), channel_id=1, source_target_pairs={{0,8},{2,10},{4,12},{6,14},{8,16},{10,18},{12,20},{14,22},{16,24},... | collective-permute-start | bytes 1966088 | tf_op jit(solution)/shard_map/ppermute | solution.py:549
  117.5 20.2 %all-to-all-start = ((bf16[8,32,640]{2,1,0:T(8,128)(2,1)}), bf16[8,32,640]{2,1,0:T(8,128)(2,1)S(1)}, u32[]{:S(2)}, u32[]{:S(2)}) async-start(bf16[8,32,640]{2,1,0:T(8,128)(2,1)} %bitcast.22), calls=%async_computation | async-start | bytes 655360 | tf_op jit(solution)/shard_map/all_to_all | solution.py:821
  137.7 41.1 %collective-permute-start.24 = (bf16[256,2816]{1,0:T(8,128)(2,1)}, bf16[256,2816]{1,0:T(8,128)(2,1)}, u32[]{:S(2)}, u32[]{:S(2)}) collective-permute-start(bf16[256,2816]{1,0:T(8,128)(2,1)} %pad_maximum_fusion.5.refs_0_), channel_id=1, source_target_pairs={{0,8},{2,10},{4,12},{6,14},{8,16},{10,18},{12,20},{14,22},{16,24},... | collective-permute-start | bytes 4325384 | tf_op jit(solution)/shard_map/ppermute | solution.py:549
  137.7 41.1 %collective-permute-start.25 = (bf16[256,2048]{1,0:T(8,128)(2,1)}, bf16[256,2048]{1,0:T(8,128)(2,1)S(1)}, u32[]{:S(2)}, u32[]{:S(2)}) collective-permute-start(bf16[256,2048]{1,0:T(8,128)(2,1)} %collective-permute-done.21), channel_id=1, source_target_pairs={{0,1},{1,0},{2,3},{3,2},{4,5},{5,4},{6,7},{7,6},{8,9},{9,8},{10,11... | collective-permute-start | bytes 3145736 | tf_op jit(solution)/shard_map/ppermute | solution.py:552
  138.8 40.0 %collective-permute-start.23 = (bf16[256,1280]{1,0:T(8,128)(2,1)}, bf16[256,1280]{1,0:T(8,128)(2,1)}, u32[]{:S(2)}, u32[]{:S(2)}) collective-permute-start(bf16[256,1280]{1,0:T(8,128)(2,1)} %collective-permute-done.19.refs_3_), channel_id=1, source_target_pairs={{0,4},{2,6},{4,0},{6,2},{8,12},{10,14},{12,8},{14,10},{16,20},{18,... | collective-permute-start | bytes 1966088 | tf_op jit(solution)/shard_map/ppermute | solution.py:546
  140.7 37.4 %all-to-all-start.1 = ((bf16[8,32,512]{2,1,0:T(8,128)(2,1)}), bf16[8,32,512]{2,1,0:T(8,128)(2,1)S(1)}, u32[]{:S(2)}, u32[]{:S(2)}) async-start(bf16[8,32,512]{2,1,0:T(8,128)(2,1)} %shard_map.390), calls=%async_computation.1 | async-start | bytes 524288 | tf_op jit(solution)/shard_map/all_to_all | solution.py:821
  146.2 61.3 %collective-permute-start.27 = (bf16[256,2816]{1,0:T(8,128)(2,1)}, bf16[256,2816]{1,0:T(8,128)(2,1)}, u32[]{:S(2)}, u32[]{:S(2)}) collective-permute-start(bf16[256,2816]{1,0:T(8,128)(2,1)} %pad_maximum_fusion.5.refs_0_), channel_id=1, source_target_pairs={{0,4},{2,6},{4,0},{6,2},{8,12},{10,14},{12,8},{14,10},{16,20},{18,... | collective-permute-start | bytes 4325384 | tf_op jit(solution)/shard_map/ppermute | solution.py:546
  179.8 35.8 %collective-permute-start.26 = (bf16[256,2816]{1,0:T(8,128)(2,1)}, bf16[256,2816]{1,0:T(8,128)(2,1)}, u32[]{:S(2)}, u32[]{:S(2)}) collective-permute-start(bf16[256,2816]{1,0:T(8,128)(2,1)} %collective-permute-done.24.refs_1_), channel_id=1, source_target_pairs={{0,8},{2,10},{4,12},{6,14},{8,16},{10,18},{12,20},{14,22},{16,24},... | collective-permute-start | bytes 4325384 | tf_op jit(solution)/shard_map/ppermute | solution.py:549
  217.7 34.2 %collective-permute-start.29 = (bf16[256,2816]{1,0:T(8,128)(2,1)}, bf16[256,2816]{1,0:T(8,128)(2,1)S(1)}, u32[]{:S(2)}, u32[]{:S(2)}) collective-permute-start(bf16[256,2816]{1,0:T(8,128)(2,1)} %collective-permute-done.24.refs_1_), channel_id=1, source_target_pairs={{0,4},{2,6},{4,0},{6,2},{8,12},{10,14},{12,8},{14,10},{16,20},{18,... | collective-permute-start | bytes 4325384 | tf_op jit(solution)/shard_map/ppermute | solution.py:546
  218.6 35.7 %collective-permute-start.28 = (bf16[256,2816]{1,0:T(8,128)(2,1)}, bf16[256,2816]{1,0:T(8,128)(2,1)S(1)}, u32[]{:S(2)}, u32[]{:S(2)}) collective-permute-start(bf16[256,2816]{1,0:T(8,128)(2,1)} %collective-permute-done.26.refs_2_), channel_id=1, source_target_pairs={{0,8},{2,10},{4,12},{6,14},{8,16},{10,18},{12,20},{14,22},{16,24},... | collective-permute-start | bytes 4325384 | tf_op jit(solution)/shard_map/ppermute | solution.py:549
  220.7 33.5 %collective-permute-start.31 = (bf16[256,2048]{1,0:T(8,128)(2,1)S(1)}, bf16[256,2048]{1,0:T(8,128)(2,1)S(1)}, u32[]{:S(2)}, u32[]{:S(2)}) collective-permute-start(bf16[256,2048]{1,0:T(8,128)(2,1)S(1)} %add_convert_fusion.6), channel_id=1, source_target_pairs={{0,2},{2,0},{4,6},{6,4},{8,10},{10,8},{12,14},{14,12},{16,18},{18,... | collective-permute-start | bytes 3145736 | tf_op jit(solution)/shard_map/ppermute | solution.py:543
  254.2 35.8 %collective-permute-start.35 = (bf16[512,1408]{1,0:T(8,128)(2,1)S(1)}, bf16[512,1408]{1,0:T(8,128)(2,1)S(1)}, u32[]{:S(2)}, u32[]{:S(2)}) collective-permute-start(bf16[512,1408]{1,0:T(8,128)(2,1)S(1)} %copy-done.40), channel_id=1, source_target_pairs={{0,8},{2,10},{4,12},{6,14},{8,16},{10,18},{12,20},{14,22},{16,24},... | collective-permute-start | bytes 4325384 | tf_op jit(solution)/shard_map/ppermute | solution.py:549
  254.3 35.7 %collective-permute-start.34 = (bf16[256,2816]{1,0:T(8,128)(2,1)}, bf16[256,2816]{1,0:T(8,128)(2,1)S(1)}, u32[]{:S(2)}, u32[]{:S(2)}) collective-permute-start(bf16[256,2816]{1,0:T(8,128)(2,1)} %collective-permute-done.26.refs_2_), channel_id=1, source_target_pairs={{0,4},{2,6},{4,0},{6,2},{8,12},{10,14},{12,8},{14,10},{16,20},{18,... | collective-permute-start | bytes 4325384 | tf_op jit(solution)/shard_map/ppermute | solution.py:546
  257.9 32.2 %collective-permute-start.36 = (bf16[256,2048]{1,0:T(8,128)(2,1)S(1)}, bf16[256,2048]{1,0:T(8,128)(2,1)S(1)}, u32[]{:S(2)}, u32[]{:S(2)}) collective-permute-start(bf16[256,2048]{1,0:T(8,128)(2,1)S(1)} %multiply_convert_fusion), channel_id=1, source_target_pairs={{0,2},{2,0},{4,6},{6,4},{8,10},{10,8},{12,14},{14,12},{16,18},{18,... | collective-permute-start | bytes 3145736 | tf_op jit(solution)/shard_map/ppermute | solution.py:543
  259.3 30.8 %collective-permute-start.37 = (bf16[256,2048]{1,0:T(8,128)(2,1)S(1)}, bf16[256,2048]{1,0:T(8,128)(2,1)S(1)}, u32[]{:S(2)}, u32[]{:S(2)}) collective-permute-start(bf16[256,2048]{1,0:T(8,128)(2,1)S(1)} %multiply_convert_fusion), channel_id=1, source_target_pairs={{0,1},{1,0},{2,3},{3,2},{4,5},{5,4},{6,7},{7,6},{8,9},{9,8},{10,11... | collective-permute-start | bytes 3145736 | tf_op jit(solution)/shard_map/ppermute | solution.py:552
  259.3 60.1 %collective-permute-start.33 = (bf16[256,2816]{1,0:T(8,128)(2,1)S(1)}, bf16[256,2816]{1,0:T(8,128)(2,1)S(1)}, u32[]{:S(2)}, u32[]{:S(2)}) collective-permute-start(bf16[256,2816]{1,0:T(8,128)(2,1)S(1)} %collective-permute-done.28.refs_3_), channel_id=1, source_target_pairs={{0,4},{2,6},{4,0},{6,2},{8,12},{10,14},{12,8},{14,10},{16,20},{18,... | collective-permute-start | bytes 4325384 | tf_op jit(solution)/shard_map/ppermute | solution.py:546
  290.1 35.1 %collective-permute-start.38 = (bf16[512,1408]{1,0:T(8,128)(2,1)S(1)}, bf16[512,1408]{1,0:T(8,128)(2,1)}, u32[]{:S(2)}, u32[]{:S(2)}) collective-permute-start(bf16[512,1408]{1,0:T(8,128)(2,1)S(1)} %collective-permute-done.35.refs_1_), channel_id=1, source_target_pairs={{0,8},{2,10},{4,12},{6,14},{8,16},{10,18},{12,20},{14,22},{16,24},... | collective-permute-start | bytes 4325384 | tf_op jit(solution)/shard_map/ppermute | solution.py:549
  325.2 37.5 %collective-permute-start.40 = (bf16[512,1408]{1,0:T(8,128)(2,1)}, bf16[512,1408]{1,0:T(8,128)(2,1)}, u32[]{:S(2)}, u32[]{:S(2)}) collective-permute-start(bf16[512,1408]{1,0:T(8,128)(2,1)} %collective-permute-done.38.refs_2_), channel_id=1, source_target_pairs={{0,8},{2,10},{4,12},{6,14},{8,16},{10,18},{12,20},{14,22},{16,24},... | collective-permute-start | bytes 4325384 | tf_op jit(solution)/shard_map/ppermute | solution.py:549
  362.7 34.8 %collective-permute-start.41 = (bf16[512,1408]{1,0:T(8,128)(2,1)}, bf16[512,1408]{1,0:T(8,128)(2,1)}, u32[]{:S(2)}, u32[]{:S(2)}) collective-permute-start(bf16[512,1408]{1,0:T(8,128)(2,1)} %shard_map.396), channel_id=1, source_target_pairs={{0,8},{2,10},{4,12},{6,14},{8,16},{10,18},{12,20},{14,22},{16,24},... | collective-permute-start | bytes 4325384 | tf_op jit(solution)/shard_map/ppermute | solution.py:549
  404.1 35.9 %collective-permute-start.43 = (bf16[512,1408]{1,0:T(8,128)(2,1)}, bf16[512,1408]{1,0:T(8,128)(2,1)}, u32[]{:S(2)}, u32[]{:S(2)}) collective-permute-start(bf16[512,1408]{1,0:T(8,128)(2,1)} %add_convert_fusion.1), channel_id=1, source_target_pairs={{0,8},{2,10},{4,12},{6,14},{8,16},{10,18},{12,20},{14,22},{16,24},... | collective-permute-start | bytes 4325384 | tf_op jit(solution)/shard_map/ppermute | solution.py:549
  404.9 34.6 %collective-permute-start.46 = (bf16[256,2048]{1,0:T(8,128)(2,1)}, bf16[256,2048]{1,0:T(8,128)(2,1)}, u32[]{:S(2)}, u32[]{:S(2)}) collective-permute-start(bf16[256,2048]{1,0:T(8,128)(2,1)} %add_convert_fusion.5), channel_id=1, source_target_pairs={{0,2},{2,0},{4,6},{6,4},{8,10},{10,8},{12,14},{14,12},{16,18},{18,... | collective-permute-start | bytes 3145736 | tf_op jit(solution)/shard_map/ppermute | solution.py:543
  406.2 19.4 %collective-permute-start.44 = (bf16[256,1408]{1,0:T(8,128)(2,1)}, bf16[256,1408]{1,0:T(8,128)(2,1)}, u32[]{:S(2)}, u32[]{:S(2)}) collective-permute-start(bf16[256,1408]{1,0:T(8,128)(2,1)} %get-tuple-element.495), channel_id=1, source_target_pairs={{0,4},{2,6},{4,0},{6,2},{8,12},{10,14},{12,8},{14,10},{16,20},{18,... | collective-permute-start | bytes 2162696 | tf_op jit(solution)/shard_map/ppermute | solution.py:546
  407.4 32.1 %collective-permute-start.45 = (bf16[256,1408]{1,0:T(8,128)(2,1)}, bf16[256,1408]{1,0:T(8,128)(2,1)S(1)}, u32[]{:S(2)}, u32[]{:S(2)}) collective-permute-start(bf16[256,1408]{1,0:T(8,128)(2,1)} %get-tuple-element.496), channel_id=1, source_target_pairs={{0,4},{2,6},{4,0},{6,2},{8,12},{10,14},{12,8},{14,10},{16,20},{18,... | collective-permute-start | bytes 2162696 | tf_op jit(solution)/shard_map/ppermute | solution.py:546
  451.8 39.0 %collective-permute-start.48 = (bf16[512,1408]{1,0:T(8,128)(2,1)}, bf16[512,1408]{1,0:T(8,128)(2,1)}, u32[]{:S(2)}, u32[]{:S(2)}) collective-permute-start(bf16[512,1408]{1,0:T(8,128)(2,1)} %add_convert_fusion), channel_id=1, source_target_pairs={{0,8},{2,10},{4,12},{6,14},{8,16},{10,18},{12,20},{14,22},{16,24},... | collective-permute-start | bytes 4325384 | tf_op jit(solution)/shard_map/ppermute | solution.py:549
  456.0 34.8 %collective-permute-start.51 = (bf16[256,2048]{1,0:T(8,128)(2,1)S(1)}, bf16[256,2048]{1,0:T(8,128)(2,1)}, u32[]{:S(2)}, u32[]{:S(2)}) collective-permute-start(bf16[256,2048]{1,0:T(8,128)(2,1)S(1)} %get-tuple-element.532), channel_id=1, source_target_pairs={{0,2},{2,0},{4,6},{6,4},{8,10},{10,8},{12,14},{14,12},{16,18},{18,... | collective-permute-start | bytes 3145736 | tf_op jit(solution)/shard_map/ppermute | solution.py:543
  456.7 34.1 %collective-permute-start.52 = (bf16[256,2048]{1,0:T(8,128)(2,1)S(1)}, bf16[256,2048]{1,0:T(8,128)(2,1)}, u32[]{:S(2)}, u32[]{:S(2)}) collective-permute-start(bf16[256,2048]{1,0:T(8,128)(2,1)S(1)} %get-tuple-element.532), channel_id=1, source_target_pairs={{0,1},{1,0},{2,3},{3,2},{4,5},{5,4},{6,7},{7,6},{8,9},{9,8},{10,11... | collective-permute-start | bytes 3145736 | tf_op jit(solution)/shard_map/ppermute | solution.py:552
  456.7 19.2 %collective-permute-start.49 = (bf16[256,1408]{1,0:T(8,128)(2,1)S(1)}, bf16[256,1408]{1,0:T(8,128)(2,1)S(1)}, u32[]{:S(2)}, u32[]{:S(2)}) collective-permute-start(bf16[256,1408]{1,0:T(8,128)(2,1)S(1)} %copy-done.121), channel_id=1, source_target_pairs={{0,4},{2,6},{4,0},{6,2},{8,12},{10,14},{12,8},{14,10},{16,20},{18,... | collective-permute-start | bytes 2162696 | tf_op jit(solution)/shard_map/ppermute | solution.py:546
  458.0 32.8 %collective-permute-start.50 = (bf16[256,1408]{1,0:T(8,128)(2,1)S(1)}, bf16[256,1408]{1,0:T(8,128)(2,1)}, u32[]{:S(2)}, u32[]{:S(2)}) collective-permute-start(bf16[256,1408]{1,0:T(8,128)(2,1)S(1)} %get-tuple-element.522), channel_id=1, source_target_pairs={{0,4},{2,6},{4,0},{6,2},{8,12},{10,14},{12,8},{14,10},{16,20},{18,... | collective-permute-start | bytes 2162696 | tf_op jit(solution)/shard_map/ppermute | solution.py:546
  490.9 19.7 %collective-permute-start.53 = (bf16[256,1408]{1,0:T(8,128)(2,1)S(1)}, bf16[256,1408]{1,0:T(8,128)(2,1)S(1)}, u32[]{:S(2)}, u32[]{:S(2)}) collective-permute-start(bf16[256,1408]{1,0:T(8,128)(2,1)S(1)} %get-tuple-element.526), channel_id=1, source_target_pairs={{0,4},{2,6},{4,0},{6,2},{8,12},{10,14},{12,8},{14,10},{16,20},{18,... | collective-permute-start | bytes 2162696 | tf_op jit(solution)/shard_map/ppermute | solution.py:546
  497.6 20.0 %collective-permute-start.55 = (bf16[256,1408]{1,0:T(8,128)(2,1)S(1)}, bf16[256,1408]{1,0:T(8,128)(2,1)S(1)}, u32[]{:S(2)}, u32[]{:S(2)}) collective-permute-start(bf16[256,1408]{1,0:T(8,128)(2,1)S(1)} %add_convert_fusion.12), channel_id=1, source_target_pairs={{0,8},{2,10},{4,12},{6,14},{8,16},{10,18},{12,20},{14,22},{16,24},... | collective-permute-start | bytes 2162696 | tf_op jit(solution)/shard_map/ppermute | solution.py:549
  518.7 25.1 %collective-permute-start.57 = (bf16[256,1408]{1,0:T(8,128)(2,1)}, bf16[256,1408]{1,0:T(8,128)(2,1)}, u32[]{:S(2)}, u32[]{:S(2)}) collective-permute-start(bf16[256,1408]{1,0:T(8,128)(2,1)} %add_convert_fusion.11), channel_id=1, source_target_pairs={{0,8},{2,10},{4,12},{6,14},{8,16},{10,18},{12,20},{14,22},{16,24},... | collective-permute-start | bytes 2162696 | tf_op jit(solution)/shard_map/ppermute | solution.py:549
  518.7 25.1 %collective-permute-start.56 = (bf16[256,1408]{1,0:T(8,128)(2,1)}, bf16[256,1408]{1,0:T(8,128)(2,1)}, u32[]{:S(2)}, u32[]{:S(2)}) collective-permute-start(bf16[256,1408]{1,0:T(8,128)(2,1)} %get-tuple-element.544), channel_id=1, source_target_pairs={{0,4},{2,6},{4,0},{6,2},{8,12},{10,14},{12,8},{14,10},{16,20},{18,... | collective-permute-start | bytes 2162696 | tf_op jit(solution)/shard_map/ppermute | solution.py:546
  519.9 23.8 %all-to-all-start.2 = ((bf16[8,32,512]{2,1,0:T(8,128)(2,1)}), bf16[8,32,512]{2,1,0:T(8,128)(2,1)}, u32[]{:S(2)}, u32[]{:S(2)}) async-start(bf16[8,32,512]{2,1,0:T(8,128)(2,1)} %bitcast.70), calls=%async_computation.2 | async-start | bytes 524288 | tf_op jit(solution)/shard_map/all_to_all | solution.py:821
  543.8 58.8 %collective-permute-start.59 = (bf16[256,1408]{1,0:T(8,128)(2,1)}, bf16[256,1408]{1,0:T(8,128)(2,1)}, u32[]{:S(2)}, u32[]{:S(2)}) collective-permute-start(bf16[256,1408]{1,0:T(8,128)(2,1)} %add_convert_fusion.10), channel_id=1, source_target_pairs={{0,8},{2,10},{4,12},{6,14},{8,16},{10,18},{12,20},{14,22},{16,24},... | collective-permute-start | bytes 2162696 | tf_op jit(solution)/shard_map/ppermute | solution.py:549
  544.5 58.1 %collective-permute-start.60 = (bf16[256,1408]{1,0:T(8,128)(2,1)}, bf16[256,1408]{1,0:T(8,128)(2,1)}, u32[]{:S(2)}, u32[]{:S(2)}) collective-permute-start(bf16[256,1408]{1,0:T(8,128)(2,1)} %copy-done.119), channel_id=1, source_target_pairs={{0,4},{2,6},{4,0},{6,2},{8,12},{10,14},{12,8},{14,10},{16,20},{18,... | collective-permute-start | bytes 2162696 | tf_op jit(solution)/shard_map/ppermute | solution.py:546
  572.4 30.2 %all-to-all-start.3 = ((bf16[8,32,512]{2,1,0:T(8,128)(2,1)}), bf16[8,32,512]{2,1,0:T(8,128)(2,1)S(1)}, u32[]{:S(2)}, u32[]{:S(2)}) async-start(bf16[8,32,512]{2,1,0:T(8,128)(2,1)} %copy-done.99), calls=%async_computation.3 | async-start | bytes 524288 | tf_op jit(solution)/shard_map/all_to_all | solution.py:821
  580.6 58.4 %collective-permute-start.58 = (bf16[256,1408]{1,0:T(8,128)(2,1)}, bf16[256,1408]{1,0:T(8,128)(2,1)}, u32[]{:S(2)}, u32[]{:S(2)}) collective-permute-start(bf16[256,1408]{1,0:T(8,128)(2,1)} %add_convert_fusion.9), channel_id=1, source_target_pairs={{0,8},{2,10},{4,12},{6,14},{8,16},{10,18},{12,20},{14,22},{16,24},... | collective-permute-start | bytes 2162696 | tf_op jit(solution)/shard_map/ppermute | solution.py:549
  602.5 36.4 %collective-permute-start.61 = (bf16[256,1024]{1,0:T(8,128)(2,1)}, bf16[256,1024]{1,0:T(8,128)(2,1)S(1)}, u32[]{:S(2)}, u32[]{:S(2)}) collective-permute-start(bf16[256,1024]{1,0:T(8,128)(2,1)} %copy-done.128), channel_id=1, source_target_pairs={{0,4},{2,6},{4,0},{6,2},{8,12},{10,14},{12,8},{14,10},{16,20},{18,... | collective-permute-start | bytes 1572872 | tf_op jit(solution)/shard_map/ppermute | solution.py:546
  614.7 41.5 %collective-permute-start.66 = (bf16[256,1408]{1,0:T(8,128)(2,1)}, bf16[256,1408]{1,0:T(8,128)(2,1)S(1)}, u32[]{:S(2)}, u32[]{:S(2)}) collective-permute-start(bf16[256,1408]{1,0:T(8,128)(2,1)} %add_convert_fusion.8), channel_id=1, source_target_pairs={{0,8},{2,10},{4,12},{6,14},{8,16},{10,18},{12,20},{14,22},{16,24},... | collective-permute-start | bytes 2162696 | tf_op jit(solution)/shard_map/ppermute | solution.py:549
  614.9 41.3 %collective-permute-start.65 = (bf16[256,1024]{1,0:T(8,128)(2,1)}, bf16[256,1024]{1,0:T(8,128)(2,1)}, u32[]{:S(2)}, u32[]{:S(2)}) collective-permute-start(bf16[256,1024]{1,0:T(8,128)(2,1)} %copy-done.127), channel_id=1, source_target_pairs={{0,4},{2,6},{4,0},{6,2},{8,12},{10,14},{12,8},{14,10},{16,20},{18,... | collective-permute-start | bytes 1572872 | tf_op jit(solution)/shard_map/ppermute | solution.py:546
  616.7 51.9 %collective-permute-start.64 = (bf16[256,1024]{1,0:T(8,128)(2,1)}, bf16[256,1024]{1,0:T(8,128)(2,1)}, u32[]{:S(2)}, u32[]{:S(2)}) collective-permute-start(bf16[256,1024]{1,0:T(8,128)(2,1)} %copy-done.124), channel_id=1, source_target_pairs={{0,4},{2,6},{4,0},{6,2},{8,12},{10,14},{12,8},{14,10},{16,20},{18,... | collective-permute-start | bytes 1572872 | tf_op jit(solution)/shard_map/ppermute | solution.py:546
  660.7 45.3 %collective-permute-start.62 = (bf16[256,1408]{1,0:T(8,128)(2,1)}, bf16[256,1408]{1,0:T(8,128)(2,1)}, u32[]{:S(2)}, u32[]{:S(2)}) collective-permute-start(bf16[256,1408]{1,0:T(8,128)(2,1)} %get-tuple-element.603), channel_id=1, source_target_pairs={{0,4},{2,6},{4,0},{6,2},{8,12},{10,14},{12,8},{14,10},{16,20},{18,... | collective-permute-start | bytes 2162696 | tf_op jit(solution)/shard_map/ppermute | solution.py:546
  662.0 42.3 %collective-permute-start.67 = (bf16[256,1024]{1,0:T(8,128)(2,1)}, bf16[256,1024]{1,0:T(8,128)(2,1)}, u32[]{:S(2)}, u32[]{:S(2)}) collective-permute-start(bf16[256,1024]{1,0:T(8,128)(2,1)} %get-tuple-element.624), channel_id=1, source_target_pairs={{0,4},{2,6},{4,0},{6,2},{8,12},{10,14},{12,8},{14,10},{16,20},{18,... | collective-permute-start | bytes 1572872 | tf_op jit(solution)/shard_map/ppermute | solution.py:546
  667.2 39.2 %collective-permute-start.71 = (bf16[256,2048]{1,0:T(8,128)(2,1)}, bf16[256,2048]{1,0:T(8,128)(2,1)}, u32[]{:S(2)}, u32[]{:S(2)}) collective-permute-start(bf16[256,2048]{1,0:T(8,128)(2,1)} %add_convert_fusion.4), channel_id=1, source_target_pairs={{0,2},{2,0},{4,6},{6,4},{8,10},{10,8},{12,14},{14,12},{16,18},{18,... | collective-permute-start | bytes 3145736 | tf_op jit(solution)/shard_map/ppermute | solution.py:543
  668.5 37.8 %collective-permute-start.70 = (bf16[256,1408]{1,0:T(8,128)(2,1)}, bf16[256,1408]{1,0:T(8,128)(2,1)}, u32[]{:S(2)}, u32[]{:S(2)}) collective-permute-start(bf16[256,1408]{1,0:T(8,128)(2,1)} %add_convert_fusion.7), channel_id=1, source_target_pairs={{0,8},{2,10},{4,12},{6,14},{8,16},{10,18},{12,20},{14,22},{16,24},... | collective-permute-start | bytes 2162696 | tf_op jit(solution)/shard_map/ppermute | solution.py:549
  677.9 28.4 %collective-permute-start.69 = (bf16[256,1024]{1,0:T(8,128)(2,1)}, bf16[256,1024]{1,0:T(8,128)(2,1)}, u32[]{:S(2)}, u32[]{:S(2)}) collective-permute-start(bf16[256,1024]{1,0:T(8,128)(2,1)} %add_convert_fusion.18), channel_id=1, source_target_pairs={{0,8},{2,10},{4,12},{6,14},{8,16},{10,18},{12,20},{14,22},{16,24},... | collective-permute-start | bytes 1572872 | tf_op jit(solution)/shard_map/ppermute | solution.py:549
  704.3 20.5 %collective-permute-start.74 = (bf16[256,1024]{1,0:T(8,128)(2,1)S(1)}, bf16[256,1024]{1,0:T(8,128)(2,1)S(1)}, u32[]{:S(2)}, u32[]{:S(2)}) collective-permute-start(bf16[256,1024]{1,0:T(8,128)(2,1)S(1)} %copy-done.130), channel_id=1, source_target_pairs={{0,4},{2,6},{4,0},{6,2},{8,12},{10,14},{12,8},{14,10},{16,20},{18,... | collective-permute-start | bytes 1572872 | tf_op jit(solution)/shard_map/ppermute | solution.py:546
  706.0 36.7 %collective-permute-start.73 = (bf16[256,1024]{1,0:T(8,128)(2,1)S(1)}, bf16[256,1024]{1,0:T(8,128)(2,1)S(1)}, u32[]{:S(2)}, u32[]{:S(2)}) collective-permute-start(bf16[256,1024]{1,0:T(8,128)(2,1)S(1)} %copy-done.126), channel_id=1, source_target_pairs={{0,4},{2,6},{4,0},{6,2},{8,12},{10,14},{12,8},{14,10},{16,20},{18,... | collective-permute-start | bytes 1572872 | tf_op jit(solution)/shard_map/ppermute | solution.py:546
  724.4 38.6 %collective-permute-start.72 = (bf16[256,2048]{1,0:T(8,128)(2,1)S(1)}, bf16[256,2048]{1,0:T(8,128)(2,1)S(1)}, u32[]{:S(2)}, u32[]{:S(2)}) collective-permute-start(bf16[256,2048]{1,0:T(8,128)(2,1)S(1)} %copy-done.116), channel_id=1, source_target_pairs={{0,1},{1,0},{2,3},{3,2},{4,5},{5,4},{6,7},{7,6},{8,9},{9,8},{10,11... | collective-permute-start | bytes 3145736 | tf_op jit(solution)/shard_map/ppermute | solution.py:552
  724.8 34.8 %collective-permute-start.84 = (bf16[256,2048]{1,0:T(8,128)(2,1)S(1)}, bf16[256,2048]{1,0:T(8,128)(2,1)S(1)}, u32[]{:S(2)}, u32[]{:S(2)}) collective-permute-start(bf16[256,2048]{1,0:T(8,128)(2,1)S(1)} %add_convert_fusion.3), channel_id=1, source_target_pairs={{0,2},{2,0},{4,6},{6,4},{8,10},{10,8},{12,14},{14,12},{16,18},{18,... | collective-permute-start | bytes 3145736 | tf_op jit(solution)/shard_map/ppermute | solution.py:543
  735.8 25.4 %collective-permute-start.80 = (f32[256,2048]{1,0:T(8,128)S(1)}, f32[256,2048]{1,0:T(8,128)S(1)}, u32[]{:S(2)}, u32[]{:S(2)}) collective-permute-start(f32[256,2048]{1,0:T(8,128)S(1)} %fusion.8.mine), channel_id=1, source_target_pairs={{0,1},{1,0},{2,3},{3,2},{4,5},{5,4},{6,7},{7,6},{8,9},{9,8},{10,11... | collective-permute-start | bytes 6291464 | tf_op jit(solution)/shard_map/ppermute | solution.py:552
  738.9 20.6 %collective-permute-start.78 = (bf16[256,1024]{1,0:T(8,128)(2,1)S(1)}, bf16[256,1024]{1,0:T(8,128)(2,1)S(1)}, u32[]{:S(2)}, u32[]{:S(2)}) collective-permute-start(bf16[256,1024]{1,0:T(8,128)(2,1)S(1)} %add_convert_fusion.15), channel_id=1, source_target_pairs={{0,8},{2,10},{4,12},{6,14},{8,16},{10,18},{12,20},{14,22},{16,24},... | collective-permute-start | bytes 1572872 | tf_op jit(solution)/shard_map/ppermute | solution.py:549
  763.0 23.1 %collective-permute-start.87 = (bf16[256,1024]{1,0:T(8,128)(2,1)}, bf16[256,1024]{1,0:T(8,128)(2,1)}, u32[]{:S(2)}, u32[]{:S(2)}) collective-permute-start(bf16[256,1024]{1,0:T(8,128)(2,1)} %add_convert_fusion.14), channel_id=1, source_target_pairs={{0,8},{2,10},{4,12},{6,14},{8,16},{10,18},{12,20},{14,22},{16,24},... | collective-permute-start | bytes 1572872 | tf_op jit(solution)/shard_map/ppermute | solution.py:549
  777.1 30.7 %collective-permute-start.91 = (bf16[128,1408]{1,0:T(8,128)(2,1)}, bf16[128,1408]{1,0:T(8,128)(2,1)}, u32[]{:S(2)}, u32[]{:S(2)}) collective-permute-start(bf16[128,1408]{1,0:T(8,128)(2,1)} %select_convert_fusion), channel_id=1, source_target_pairs={{0,2},{2,0},{4,6},{6,4},{8,10},{10,8},{12,14},{14,12},{16,18},{18,... | collective-permute-start | bytes 1081352 | tf_op jit(solution)/shard_map/ppermute | solution.py:543
  778.5 33.8 %collective-permute-start.85 = (bf16[256,2048]{1,0:T(8,128)(2,1)S(1)}, bf16[256,2048]{1,0:T(8,128)(2,1)S(1)}, u32[]{:S(2)}, u32[]{:S(2)}) collective-permute-start(bf16[256,2048]{1,0:T(8,128)(2,1)S(1)} %add_convert_fusion.2.mine), channel_id=1, source_target_pairs={{0,1},{1,0},{2,3},{3,2},{4,5},{5,4},{6,7},{7,6},{8,9},{9,8},{10,11... | collective-permute-start | bytes 3145736 | tf_op jit(solution)/shard_map/ppermute | solution.py:552
  (221 other events, 1905.8 us)
